TPU v7x, 128 devices: a whole 4x4x4 slice. The times are simulated.
128 devices in a mesh: dp: 64 (over z_lo, y, x, core), tensor: 2 (over z_hi).
Axes of the slice: x: 4, y: 4, z: 4 (z_hi: 2, z_lo: 2; z = z_hi * 2 + z_lo), core: 2. Of those that a mesh axis runs over, the one named last changes fastest.
Arguments:
- tokens: bfloat16 [16384, 768], P(('dp', 'tensor')), may hold values from -24 to 24
- clip_bounds: int32 [2, 16384], P(None, 'dp'), may hold values from 0 to 16384, as said below
- attn_in: bfloat16 [1, 3, 768, 768], P(None, None, 'dp', 'tensor'), may hold values from -0.21875 to 0.21875
- qv_bias: bfloat16 [1, 2, 12, 64], P(None, None, 'tensor', 'dp'), may hold values from -3 to 3
- out_proj: bfloat16 [1, 768, 768], P(None, 'tensor', 'dp'), may hold values from -4 to 4
- fc_in: bfloat16 [1, 768, 3072], P(None, 'dp', 'tensor'), may hold values from -0.21875 to 0.21875
- fc_bias: bfloat16 [1, 12, 256], P(None, 'tensor', 'dp'), may hold values from -3 to 3
- fc_out: bfloat16 [1, 3072, 768], P(None, 'tensor', 'dp'), may hold values from -0.109375 to 0.109375
- ln_gain: bfloat16 [1, 2, 768], P(None, None, ('dp', 'tensor')), may hold values from 0.5 to 1.5
- row_bias: bfloat16 [1, 4, 768], P(None, None, ('dp', 'tensor')), may hold values from -2 to 2
- cotangent: bfloat16 [16384, 768], P(('dp', 'tensor')), may hold values from -24 to 24
Outputs:
- output: bfloat16 [16384, 768], P(('dp', 'tensor'))
- grad_tokens: float32 [16384, 768], P(('dp', 'tensor'))
- grad_attn_in: float32 [1, 3, 768, 768], P(None, None, 'dp', 'tensor')
- grad_qv_bias: float32 [1, 2, 12, 64], P(None, None, 'tensor', 'dp')
- grad_out_proj: float32 [1, 768, 768], P(None, 'tensor', 'dp')
- grad_fc_in: float32 [1, 768, 3072], P(None, 'dp', 'tensor')
- grad_fc_bias: float32 [1, 12, 256], P(None, 'tensor', 'dp')
- grad_fc_out: float32 [1, 3072, 768], P(None, 'tensor', 'dp')
- grad_ln_gain: float32 [1, 2, 768], P(None, None, ('dp', 'tensor'))
- grad_row_bias: float32 [1, 4, 768], P(None, None, ('dp', 'tensor'))
Inputs may be any that keep to these rules, and one draw needn't show every extreme that they name: `clip_bounds`: row 0 holds the position of the first token of each token's clip and row 1 the position one past its last; clips are runs of consecutive tokens of at most 1500 tokens, and one clip has exactly 1500.
All inputs are finite; a program needn't handle non-finite values.
Results may differ from a plain program's by a relative error of at most 0.017.
Values may be sent and summed in bfloat16 or wider, within the bound.
A program may use at most 128 MiB of HBM per device.

v0:
```python
from functools import partial

import jax
import jax.numpy as jnp
from jax import lax
from jax.sharding import PartitionSpec as P

HD = 64
CLIP = 1500


EPS = 1e-05
NEGATIVE = -1e30
SCORE_SCALE = 0.125


def from_behind(value, axis, steps):
    count = lax.axis_size(axis)
    first, last = (max(0, -steps), min(count, count - steps))
    return lax.ppermute(value, axis, [(source, source + steps) for source in range(first, last)])


def matmul(left, right):
    return jnp.dot(left, right, preferred_element_type=jnp.float32)


def matmul_right_t(left, right):
    return lax.dot_general(
        left, right, (((1,), (1,)), ((), ())), preferred_element_type=jnp.float32
    )


def matmul_left_t(left, right):
    return lax.dot_general(
        left, right, (((0,), (0,)), ((), ())), preferred_element_type=jnp.float32
    )


def normalize(hidden, gain, offset):
    average = jnp.mean(hidden, axis=-1, keepdims=True)
    centred = hidden - average
    spread = jnp.mean(centred * centred, axis=-1, keepdims=True)
    scale = lax.rsqrt(spread + EPS)
    unit = centred * scale
    return (unit * gain + offset, unit, scale)


def normalize_back(grad_out, unit, scale, gain):
    grad_unit = grad_out * gain
    first = jnp.mean(grad_unit, axis=-1, keepdims=True)
    second = jnp.mean(grad_unit * unit, axis=-1, keepdims=True)
    return scale * (grad_unit - first - unit * second)


def spread_rows(rows):
    return lax.all_gather(rows, "tensor", axis=0, tiled=True)


def sum_rows(term, share):
    return lax.psum_scatter(
        term(jnp.int32(0), share * lax.axis_size("tensor")).astype(jnp.bfloat16),
        "tensor",
        scatter_dimension=0,
        tiled=True,
    ).astype(jnp.float32)


def fetch_layer(params, layer):
    attn_in, qv_bias, out_proj, fc_in, fc_bias, fc_out = params
    return (
        lax.all_gather(attn_in[layer], "dp", axis=1, tiled=True),
        lax.all_gather(qv_bias[layer], "dp", axis=2, tiled=True),
        lax.all_gather(out_proj[layer], "dp", axis=1, tiled=True),
        lax.all_gather(fc_in[layer], "dp", axis=0, tiled=True),
        lax.all_gather(fc_bias[layer], "dp", axis=1, tiled=True),
        lax.all_gather(fc_out[layer], "dp", axis=1, tiled=True),
    )


def reduce_layer(grads):
    grad_in, grad_qv, grad_out, grad_up, grad_up_bias, grad_down = grads
    return (
        lax.psum_scatter(grad_in, "dp", scatter_dimension=1, tiled=True),
        lax.psum_scatter(grad_qv, "dp", scatter_dimension=2, tiled=True),
        lax.psum_scatter(grad_out, "dp", scatter_dimension=1, tiled=True),
        lax.psum_scatter(grad_up, "dp", scatter_dimension=0, tiled=True),
        lax.psum_scatter(grad_up_bias, "dp", scatter_dimension=1, tiled=True),
        lax.psum_scatter(grad_down, "dp", scatter_dimension=1, tiled=True),
    )


def clip_mask(starts, ends, rank, offset):
    block = starts.shape[0]
    positions = (rank - offset) * block + jnp.arange(block, dtype=jnp.int32)
    return (positions[None, :] >= starts[:, None]) & (positions[None, :] < ends[:, None])


def block_scores(query, keys, allowed):
    scores = SCORE_SCALE * jnp.einsum(
        "qhd,khd->hqk", query, keys, preferred_element_type=jnp.float32
    )
    return jnp.where(allowed[None], scores, NEGATIVE)


def neighbour_blocks(keys, values):
    block = keys.shape[0]
    reach = (CLIP + block - 2) // block
    near = [(0, keys, values)]
    for offset in list(range(1, reach + 1)) + list(range(-reach, 0)):
        moved_keys, moved_values = from_behind((keys, values), "dp", offset)
        near.append((offset, moved_keys, moved_values))
    return near


def attend(query, near, starts, ends, rank):
    top = None
    total = None
    for offset, keys, values in near:
        scores = block_scores(query, keys, clip_mask(starts, ends, rank, offset))
        block_top = jnp.max(scores, axis=-1)
        if top is None:
            top = block_top
            total = jnp.sum(jnp.exp(scores - top[..., None]), axis=-1)
        else:
            new_top = jnp.maximum(top, block_top)
            total = total * jnp.exp(top - new_top) + jnp.sum(
                jnp.exp(scores - new_top[..., None]), axis=-1
            )
            top = new_top
    logsum = top + jnp.log(total)
    mixed = jnp.zeros(query.shape, jnp.float32)
    for offset, keys, values in near:
        scores = block_scores(query, keys, clip_mask(starts, ends, rank, offset))
        weights = jnp.exp(scores - logsum[..., None]).astype(jnp.bfloat16)
        mixed = mixed + jnp.einsum(
            "hqk,khd->qhd", weights, values, preferred_element_type=jnp.float32
        )
    return (mixed, logsum)


def attend_back(query, near, starts, ends, rank, logsum, grad_mixed, mixed):
    delta = jnp.einsum("qhd,qhd->hq", grad_mixed.astype(jnp.float32), mixed)
    grad_query = jnp.zeros(query.shape, jnp.float32)
    grad_keys_total = jnp.zeros(query.shape, jnp.float32)
    grad_values_total = jnp.zeros(query.shape, jnp.float32)
    for offset, keys, values in near:
        scores = block_scores(query, keys, clip_mask(starts, ends, rank, offset))
        probs = jnp.exp(scores - logsum[..., None])
        grad_probs = jnp.einsum(
            "qhd,khd->hqk", grad_mixed, values, preferred_element_type=jnp.float32
        )
        grad_scores = (probs * (grad_probs - delta[..., None])).astype(jnp.bfloat16)
        grad_query = grad_query + jnp.einsum(
            "hqk,khd->qhd", grad_scores, keys, preferred_element_type=jnp.float32
        )
        grad_keys = jnp.einsum(
            "hqk,qhd->khd", grad_scores, query, preferred_element_type=jnp.float32
        )
        grad_values = jnp.einsum(
            "hqk,qhd->khd",
            probs.astype(jnp.bfloat16),
            grad_mixed,
            preferred_element_type=jnp.float32,
        )
        if offset != 0:
            grad_keys, grad_values = (
                from_behind(grad_keys.astype(jnp.bfloat16), "dp", -offset).astype(grad_keys.dtype),
                from_behind(grad_values.astype(jnp.bfloat16), "dp", -offset).astype(
                    grad_values.dtype
                ),
            )
        grad_keys_total = grad_keys_total + grad_keys
        grad_values_total = grad_values_total + grad_values
    return (SCORE_SCALE * grad_query, SCORE_SCALE * grad_keys_total, grad_values_total)


def layer_forward(hidden, weights, gains, biases, starts, ends, rank):
    in_proj, qv_part, out_part, up_part, up_bias, down_part = weights
    block = starts.shape[0]
    share = hidden.shape[0]
    normed, unit_one, scale_one = normalize(hidden, gains[0], biases[0])
    full_one = spread_rows(normed.astype(jnp.bfloat16))
    projected = jnp.einsum("bd,kdc->kbc", full_one, in_proj, preferred_element_type=jnp.float32)
    query = (projected[0] + qv_part[0].reshape(-1)).astype(jnp.bfloat16).reshape(block, -1, HD)
    keys = projected[1].astype(jnp.bfloat16).reshape(block, -1, HD)
    values = (projected[2] + qv_part[1].reshape(-1)).astype(jnp.bfloat16).reshape(block, -1, HD)
    near = neighbour_blocks(keys, values)
    mixed, logsum = attend(query, near, starts, ends, rank)
    mixed_low = mixed.reshape(block, -1).astype(jnp.bfloat16)

    def attn_term(start, count):
        return matmul(mixed_low, out_part)

    hidden_one = hidden + sum_rows(attn_term, share) + biases[1]
    normed_two, unit_two, scale_two = normalize(hidden_one, gains[1], biases[2])
    full_two = spread_rows(normed_two.astype(jnp.bfloat16))
    inner = matmul(full_two, up_part) + up_bias.reshape(-1)
    active = jax.nn.gelu(inner, approximate=False).astype(jnp.bfloat16)

    def mlp_term(start, count):
        return matmul(active, down_part)

    hidden_two = hidden_one + sum_rows(mlp_term, share) + biases[3]
    saved = (
        unit_one,
        scale_one,
        full_one,
        query,
        near,
        mixed,
        mixed_low,
        logsum,
        unit_two,
        scale_two,
        full_two,
        inner,
        active,
    )
    return (hidden_two, saved)


def layer_backward(grad_hidden, weights, gains, saved, starts, ends, rank):
    in_proj, qv_part, out_part, up_part, up_bias, down_part = weights
    (
        unit_one,
        scale_one,
        full_one,
        query,
        near,
        mixed,
        mixed_low,
        logsum,
        unit_two,
        scale_two,
        full_two,
        inner,
        active,
    ) = saved
    block = starts.shape[0]
    share = grad_hidden.shape[0]
    grad_mlp = grad_hidden.astype(jnp.bfloat16)
    full_mlp = spread_rows(grad_mlp)
    grad_down = matmul_left_t(active, full_mlp)
    grad_active = matmul_right_t(full_mlp, down_part)
    unused_value, gelu_back = jax.vjp(partial(jax.nn.gelu, approximate=False), inner)
    grad_inner = gelu_back(grad_active)[0].astype(jnp.bfloat16)
    grad_up = matmul_left_t(full_two, grad_inner)
    grad_up_bias = jnp.sum(grad_inner, axis=0, dtype=jnp.float32).reshape(up_bias.shape)

    def mlp_back(start, count):
        return matmul_right_t(grad_inner, up_part)

    grad_normed_two = sum_rows(mlp_back, share)
    grad_gain_two = jnp.sum(grad_normed_two * unit_two, axis=0)
    grad_offset_two = jnp.sum(grad_normed_two, axis=0)
    grad_bias_two = jnp.sum(grad_mlp, axis=0, dtype=jnp.float32)
    grad_hidden_one = grad_hidden + normalize_back(grad_normed_two, unit_two, scale_two, gains[1])
    grad_attn = grad_hidden_one.astype(jnp.bfloat16)
    full_attn = spread_rows(grad_attn)
    grad_out = matmul_left_t(mixed_low, full_attn)
    grad_mixed = matmul_right_t(full_attn, out_part).astype(jnp.bfloat16).reshape(block, -1, HD)
    grad_bias_out = jnp.sum(grad_attn, axis=0, dtype=jnp.float32)
    grad_query, grad_keys, grad_values = attend_back(
        query, near, starts, ends, rank, logsum, grad_mixed, mixed
    )
    grad_stack = (
        jnp.stack([grad_query, grad_keys, grad_values]).reshape(3, block, -1).astype(jnp.bfloat16)
    )
    grad_in = jnp.einsum("bd,kbc->kdc", full_one, grad_stack, preferred_element_type=jnp.float32)
    grad_qv = jnp.sum(grad_stack[0::2], axis=1, dtype=jnp.float32).reshape(qv_part.shape)

    def attn_back(start, count):
        return jnp.einsum("kbc,kdc->bd", grad_stack, in_proj, preferred_element_type=jnp.float32)

    grad_normed_one = sum_rows(attn_back, share)
    grad_gain_one = jnp.sum(grad_normed_one * unit_one, axis=0)
    grad_offset_one = jnp.sum(grad_normed_one, axis=0)
    grad_input = grad_hidden_one + normalize_back(grad_normed_one, unit_one, scale_one, gains[0])
    weight_grads = (grad_in, grad_qv, grad_out, grad_up, grad_up_bias, grad_down)
    gain_grads = jnp.stack([grad_gain_one, grad_gain_two])
    bias_grads = jnp.stack([grad_offset_one, grad_bias_out, grad_offset_two, grad_bias_two])
    return (grad_input, weight_grads, gain_grads, bias_grads)


def body(
    tokens,
    clip_bounds,
    attn_in,
    qv_bias,
    out_proj,
    fc_in,
    fc_bias,
    fc_out,
    ln_gain,
    row_bias,
    cotangent,
):
    gain_rows, bias_rows = (
        lax.all_gather(ln_gain, ("dp", "tensor"), axis=2, tiled=True),
        lax.all_gather(row_bias, ("dp", "tensor"), axis=2, tiled=True),
    )
    gain_rows = gain_rows.astype(jnp.float32)
    bias_rows = bias_rows.astype(jnp.float32)
    starts = clip_bounds[0]
    ends = clip_bounds[1]
    rank = lax.axis_index("dp")
    params = (attn_in, qv_bias, out_proj, fc_in, fc_bias, fc_out)
    layers = attn_in.shape[0]
    hidden = tokens.astype(jnp.float32)
    kept_weights = []
    layer = 0
    weights = fetch_layer(params, layer)
    hidden, saved = layer_forward(
        hidden, weights, gain_rows[layer], bias_rows[layer], starts, ends, rank
    )
    kept_weights.append(weights)
    kept_saved = [saved]
    output = hidden.astype(jnp.bfloat16)
    grad_hidden = cotangent.astype(jnp.float32)
    weight_parts = [None] * layers
    gain_parts = [None] * layers
    bias_parts = [None] * layers
    for layer in reversed(range(layers)):
        weights = fetch_layer(params, layer)
        grad_hidden, weight_grads, gain_grads, bias_grads = layer_backward(
            grad_hidden, weights, gain_rows[layer], kept_saved[layer], starts, ends, rank
        )
        weight_parts[layer] = reduce_layer(weight_grads)
        gain_parts[layer] = gain_grads
        bias_parts[layer] = bias_grads
    stacked_in = jnp.stack([part[0] for part in weight_parts])
    stacked_qv = jnp.stack([part[1] for part in weight_parts])
    stacked_out = jnp.stack([part[2] for part in weight_parts])
    stacked_up = jnp.stack([part[3] for part in weight_parts])
    stacked_up_bias = jnp.stack([part[4] for part in weight_parts])
    stacked_down = jnp.stack([part[5] for part in weight_parts])
    grad_gains, grad_biases = (
        lax.psum_scatter(jnp.stack(gain_parts), ("dp", "tensor"), scatter_dimension=2, tiled=True),
        lax.psum_scatter(jnp.stack(bias_parts), ("dp", "tensor"), scatter_dimension=2, tiled=True),
    )
    return (
        output,
        grad_hidden,
        stacked_in,
        stacked_qv,
        stacked_out,
        stacked_up,
        stacked_up_bias,
        stacked_down,
        grad_gains,
        grad_biases,
    )


def solution(mesh):
    return jax.shard_map(
        body,
        mesh=mesh,
        in_specs=(
            P(("dp", "tensor"), None),
            P(None, "dp"),
            P(None, None, "dp", "tensor"),
            P(None, None, "tensor", "dp"),
            P(None, "tensor", "dp"),
            P(None, "dp", "tensor"),
            P(None, "tensor", "dp"),
            P(None, "tensor", "dp"),
            P(None, None, ("dp", "tensor")),
            P(None, None, ("dp", "tensor")),
            P(("dp", "tensor"), None),
        ),
        out_specs=(
            P(("dp", "tensor"), None),
            P(("dp", "tensor"), None),
            P(None, None, "dp", "tensor"),
            P(None, None, "tensor", "dp"),
            P(None, "tensor", "dp"),
            P(None, "dp", "tensor"),
            P(None, "tensor", "dp"),
            P(None, "tensor", "dp"),
            P(None, None, ("dp", "tensor")),
            P(None, None, ("dp", "tensor")),
        ),
        check_vma=False,
    )
```

profile of v0, /device:TPU:1, one launch (start us, length us, event | category | flops | bytes accessed | tf_op | source)
XLA Modules:
  0.0 2180.9 jit_solution(10173090393288191090)
XLA Ops:
  11.0 83.8 %all-gather.1 = bf16[1,2,6,64]{2,1,0,3:T(2,128)(2,1)S(1)} all-gather(bf16[1,2,6,1]{2,1,0,3:T(2,128)(2,1)} %bitcast.341), channel_id=3, replica_groups=mesh['dp'=64,'tensor'=2] {'dp'}, dimensions={3}, use_global_device_ids=true | all-gather | bytes 1560 | tf_op jit(solution)/shard_map/all_gather | solution.py:72
  95.6 312.0 %all_gather.41 = bf16[1,4,768]{1,0,2:T(2,128)(2,1)S(1)} all-gather(bf16[1,4,6]{1,0,2:T(2,128)(2,1)S(1)} %copy.492), channel_id=1, replica_groups=mesh['dp'=64,'tensor'=2] {'dp','tensor'}, dimensions={2}, use_global_device_ids=true | all-gather | bytes 6192 | tf_op jit(solution)/shard_map/all_gather | solution.py:300
  408.0 312.5 %all_gather.40 = bf16[1,2,768]{1,0,2:T(2,128)(2,1)S(1)} all-gather(bf16[1,2,6]{1,0,2:T(2,128)(2,1)S(1)} %copy.491), channel_id=1, replica_groups=mesh['dp'=64,'tensor'=2] {'dp','tensor'}, dimensions={2}, use_global_device_ids=true | all-gather | bytes 3096 | tf_op jit(solution)/shard_map/all_gather | solution.py:299
  720.9 82.9 %all-gather.2 = bf16[1,384,768]{1,0,2:T(2,128)(2,1)S(1)} all-gather(bf16[1,384,12]{1,0,2:T(2,128)(2,1)S(1)} %copy.514), channel_id=4, replica_groups=mesh['dp'=64,'tensor'=2] {'dp'}, dimensions={2}, use_global_device_ids=true | all-gather | bytes 599040 | tf_op jit(solution)/shard_map/all_gather | solution.py:73
  807.3 5.2 slice_reduce_fusion.5
  812.5 11.3 slice_reduce_fusion
  824.0 9.1 all_gather.42
  851.7 4.9 collective-permute-start.1
  861.5 7.6 collective-permute-start.2
  872.1 8.2 collective-permute-start.3
  883.5 7.2 collective-permute-start.4
  903.7 9.6 collective-permute-done.6
  915.1 10.5 collective-permute-done.7
  945.2 5.8 collective-permute-start.14
  955.6 7.5 collective-permute-start.15
  967.5 5.6 collective-permute-start.16
  977.8 6.0 collective-permute-start.17
  989.1 7.3 collective-permute-done.18
  998.0 10.1 collective-permute-done.19
  1022.1 84.7 %all-gather.4 = bf16[1,6,256]{1,0,2:T(2,128)(2,1)} all-gather(bf16[1,6,4]{1,0,2:T(2,128)(2,1)S(1)} %copy.517), channel_id=6, replica_groups=mesh['dp'=64,'tensor'=2] {'dp'}, dimensions={2}, use_global_device_ids=true | all-gather | bytes 3120 | tf_op jit(solution)/shard_map/all_gather | solution.py:75
  1111.1 12.2 all_gather.50
  1126.7 9.4 all_gather.46
  1136.1 21.9 %all-gather.14.cloned.1.call-done = bf16[1,1536,768]{1,0,2:T(2,128)(2,1)} async-done(((bf16[1,1536,12]{1,0,2:T(2,128)(2,1)}), bf16[1,1536,768]{1,0,2:T(2,128)(2,1)}) %all-gather.14.cloned.1.call-update) | async-done | bytes 2359312 | tf_op jit(solution)/shard_map/all_gather | solution.py:76
  1157.9 11.7 copy.520
  1169.7 96.9 %all-gather.12.cloned.1.call-done = bf16[1,768,1536]{2,0,1:T(2,128)(2,1)} async-done(((bf16[1,12,1536]{2,0,1:T(2,128)(2,1)}), bf16[1,768,1536]{2,0,1:T(2,128)(2,1)}) %all-gather.12.cloned.1.call-update) | async-done | bytes 2359312 | tf_op jit(solution)/shard_map/all_gather | solution.py:74
  1266.6 7.5 multiply_convert_fusion.13
  1286.5 8.2 reduce-scatter.18.cloned.1.call-done
  1297.6 15.8 reduce-scatter.16.cloned.1.call-done
  1316.4 7.9 all_gather.51
  1407.0 11.9 collective-permute-start.30
  1418.9 5.5 collective-permute-start.31
  1424.5 10.5 collective-permute-start.32
  1441.4 6.2 collective-permute-start.42
  1447.6 5.0 collective-permute-start.43
  1454.5 5.2 collective-permute-start.45
  1479.5 6.3 copy.578
  1485.9 165.1 %fusion.168 = (f32[384,16]{0,1:T(8,128)S(1)}, f32[16,1536]{1,0:T(8,128)S(1)}, f32[1536,16]{0,1:T(8,128)S(1)}) fusion(f32[384,768]{0,1:T(8,128)S(1)} %fusion.198, f32[768,1536]{1,0:T(8,128)} %fusion.199, f32[1536,768]{0,1:T(8,128)} %fusion.200), kind=kCustom, calls=%all-reduce-scatter.3 | all-reduce-scatter fusion | flops 3538945 | bytes 10838528
  1652.3 22.4 %collective-permute-start.63 = (f32[384,12]{0,1:T(8,128)S(1)}, f32[384,12]{0,1:T(8,128)S(1)}, u32[]{:S(2)}, u32[]{:S(2)}) collective-permute-start(f32[384,12]{0,1:T(8,128)S(1)} %slice.78), channel_id=1, source_target_pairs={{0,32},{2,34},{4,36},{6,38},{8,40},{10,42},{12,44},{14,46},{16,48}... | collective-permute-start | bytes 55304
  1681.3 7.1 collective-permute-start.56
  1727.0 4.7 collective-permute-start.72
  1734.7 5.6 collective-permute-start.69
  1742.6 4.6 collective-permute-start.67
  1747.2 9.0 collective-permute-start.66
  1786.6 6.3 collective-permute-start.85
  1793.5 10.0 concatenate.3
  1819.0 8.3 concatenate.4
  1828.5 268.9 %all-reduce.12 = (f32[2,6,64]{1,0,2:T(2,128)S(1)}, f32[6,256]{1,0:T(8,128)S(1)}) all-reduce(f32[2,6,64]{1,0,2:T(2,128)S(1)} %copy.579, f32[6,256]{1,0:T(8,128)S(1)} %reshape.1199), channel_id=13, replica_groups=mesh['dp'=64,'tensor'=2] {'dp'}, use_global_device_ids=true, to_apply=%region_40.41.clone | all-reduce | flops 2304 | bytes 18432
  2100.6 68.5 %all-reduce.11 = (f32[1,2,768]{2,1,0:T(2,128)S(1)}, f32[1,4,768]{2,1,0:T(4,128)S(1)}) all-reduce(f32[1,2,768]{2,1,0:T(2,128)S(1)} %maximum_bitcast_fusion.1, f32[1,4,768]{2,1,0:T(4,128)S(1)} %maximum_bitcast_fusion), channel_id=18, replica_groups=mesh['dp'=64,'tensor'=2] {'dp','tensor'}, use_global_device_ids=true, to_apply=%region_48.49.clone | all-reduce | flops 4608 | bytes 36864
  (675 shorter events, 347.1 us)
Async XLA Ops:
  7.2 827.6 %all-gather.10.cloned.1.call-start = ((), (), s32[]{:S(2)}) async-start(), calls=%async_computation.8 | async-start | bytes 2396160 | tf_op jit(solution)/shard_map/all_gather | solution.py:71
  8.6 1114.7 %reduce-scatter.14.cloned.1.call-start = ((), (), s32[]{:S(2)}) async-start(), calls=%async_computation.4 | async-start | bytes 589824 | tf_op jit(solution)/shard_map/reduce_scatter | solution.py:60
  838.1 98.2 %collective-permute-start.11 = (bf16[256,6,64]{0,2,1:T(8,128)(2,1)}, bf16[256,6,64]{0,2,1:T(8,128)(2,1)}, u32[]{:S(2)}, u32[]{:S(2)}) collective-permute-start(bf16[256,6,64]{0,2,1:T(8,128)(2,1)} %bitcast.12), channel_id=1, source_target_pairs={{2,0},{4,2},{6,4},{8,6},{10,8},{12,10},{14,12},{16,14},{18,16},{20... | collective-permute-start | bytes 589832 | tf_op jit(solution)/shard_map/ppermute | solution.py:20
  840.7 92.8 %collective-permute-start.10 = (bf16[256,6,64]{0,2,1:T(8,128)(2,1)}, bf16[256,6,64]{0,2,1:T(8,128)(2,1)}, u32[]{:S(2)}, u32[]{:S(2)}) collective-permute-start(bf16[256,6,64]{0,2,1:T(8,128)(2,1)} %bitcast.12), channel_id=1, source_target_pairs={{4,0},{6,2},{8,4},{10,6},{12,8},{14,10},{16,12},{18,14},{20,16},{2... | collective-permute-start | bytes 589832 | tf_op jit(solution)/shard_map/ppermute | solution.py:20
  842.0 88.8 %collective-permute-start.9 = (bf16[256,6,64]{0,2,1:T(8,128)(2,1)}, bf16[256,6,64]{0,2,1:T(8,128)(2,1)}, u32[]{:S(2)}, u32[]{:S(2)}) collective-permute-start(bf16[256,6,64]{0,2,1:T(8,128)(2,1)} %bitcast.12), channel_id=1, source_target_pairs={{6,0},{8,2},{10,4},{12,6},{14,8},{16,10},{18,12},{20,14},{22,16},{... | collective-permute-start | bytes 589832 | tf_op jit(solution)/shard_map/ppermute | solution.py:20
  843.3 84.7 %collective-permute-start.8 = (bf16[256,6,64]{0,2,1:T(8,128)(2,1)}, bf16[256,6,64]{0,2,1:T(8,128)(2,1)}, u32[]{:S(2)}, u32[]{:S(2)}) collective-permute-start(bf16[256,6,64]{0,2,1:T(8,128)(2,1)} %bitcast.12), channel_id=1, source_target_pairs={{8,0},{10,2},{12,4},{14,6},{16,8},{18,10},{20,12},{22,14},{24,16},... | collective-permute-start | bytes 589832 | tf_op jit(solution)/shard_map/ppermute | solution.py:20
  925.6 87.2 %collective-permute-start.23 = (bf16[256,6,64]{0,2,1:T(8,128)(2,1)S(1)}, bf16[256,6,64]{0,2,1:T(8,128)(2,1)S(1)}, u32[]{:S(2)}, u32[]{:S(2)}) collective-permute-start(bf16[256,6,64]{0,2,1:T(8,128)(2,1)S(1)} %add_convert_fusion.5), channel_id=1, source_target_pairs={{2,0},{4,2},{6,4},{8,6},{10,8},{12,10},{14,12},{16,14},{18,16},{20... | collective-permute-start | bytes 589832 | tf_op jit(solution)/shard_map/ppermute | solution.py:20
  928.0 84.4 %collective-permute-start.22 = (bf16[256,6,64]{0,2,1:T(8,128)(2,1)S(1)}, bf16[256,6,64]{0,2,1:T(8,128)(2,1)S(1)}, u32[]{:S(2)}, u32[]{:S(2)}) collective-permute-start(bf16[256,6,64]{0,2,1:T(8,128)(2,1)S(1)} %add_convert_fusion.5), channel_id=1, source_target_pairs={{4,0},{6,2},{8,4},{10,6},{12,8},{14,10},{16,12},{18,14},{20,16},{2... | collective-permute-start | bytes 589832 | tf_op jit(solution)/shard_map/ppermute | solution.py:20
  930.8 81.2 %collective-permute-start.21 = (bf16[256,6,64]{0,2,1:T(8,128)(2,1)S(1)}, bf16[256,6,64]{0,2,1:T(8,128)(2,1)S(1)}, u32[]{:S(2)}, u32[]{:S(2)}) collective-permute-start(bf16[256,6,64]{0,2,1:T(8,128)(2,1)S(1)} %add_convert_fusion.5), channel_id=1, source_target_pairs={{6,0},{8,2},{10,4},{12,6},{14,8},{16,10},{18,12},{20,14},{22,16},{... | collective-permute-start | bytes 589832 | tf_op jit(solution)/shard_map/ppermute | solution.py:20
  933.6 78.1 %collective-permute-start.20 = (bf16[256,6,64]{0,2,1:T(8,128)(2,1)S(1)}, bf16[256,6,64]{0,2,1:T(8,128)(2,1)S(1)}, u32[]{:S(2)}, u32[]{:S(2)}) collective-permute-start(bf16[256,6,64]{0,2,1:T(8,128)(2,1)S(1)} %add_convert_fusion.5), channel_id=1, source_target_pairs={{8,0},{10,2},{12,4},{14,6},{16,8},{18,10},{20,12},{22,14},{24,16},... | collective-permute-start | bytes 589832 | tf_op jit(solution)/shard_map/ppermute | solution.py:20
  1018.3 139.7 %all-gather.14.cloned.1.call-start = ((), (), s32[]{:S(2)}) async-start(), calls=%async_computation.10 | async-start | bytes 4792320 | tf_op jit(solution)/shard_map/all_gather | solution.py:76
  1019.8 246.8 %all-gather.12.cloned.1.call-start = ((), (), s32[]{:S(2)}) async-start(), calls=%async_computation.9 | async-start | bytes 4792320 | tf_op jit(solution)/shard_map/all_gather | solution.py:74
  1021.4 273.2 %reduce-scatter.18.cloned.1.call-start = ((), (), s32[]{:S(2)}) async-start(), calls=%async_computation.6 | async-start | bytes 589824 | tf_op jit(solution)/shard_map/reduce_scatter | solution.py:60
  1278.4 35.0 %reduce-scatter.16.cloned.1.call-start = ((), (), s32[]{:S(2)}) async-start(), calls=%async_computation.5 | async-start | bytes 589824 | tf_op jit(solution)/shard_map/reduce_scatter | solution.py:60
  1282.2 817.1 %reduce-scatter.20.cloned.1.call-start = ((), (), s32[]{:S(2)}) async-start(), calls=%async_computation.7 | async-start | bytes 589824 | tf_op jit(solution)/shard_map/reduce_scatter | solution.py:60
  1355.6 29.5 %collective-permute-start.35 = (bf16[256,6,64]{0,2,1:T(8,128)(2,1)}, bf16[256,6,64]{0,2,1:T(8,128)(2,1)}, u32[]{:S(2)}, u32[]{:S(2)}) collective-permute-start(bf16[256,6,64]{0,2,1:T(8,128)(2,1)} %fusion.85), channel_id=1, source_target_pairs={{0,2},{2,4},{4,6},{6,8},{8,10},{10,12},{12,14},{14,16},{16,18},{18... | collective-permute-start | bytes 589832 | tf_op jit(solution)/shard_map/ppermute | solution.py:20
  1360.1 26.4 %collective-permute-start.47 = (bf16[256,6,64]{0,2,1:T(8,128)(2,1)}, bf16[256,6,64]{0,2,1:T(8,128)(2,1)}, u32[]{:S(2)}, u32[]{:S(2)}) collective-permute-start(bf16[256,6,64]{0,2,1:T(8,128)(2,1)} %fusion.97), channel_id=1, source_target_pairs={{0,2},{2,4},{4,6},{6,8},{8,10},{10,12},{12,14},{14,16},{16,18},{18... | collective-permute-start | bytes 589832 | tf_op jit(solution)/shard_map/ppermute | solution.py:20
  1362.0 25.7 %collective-permute-start.24 = (bf16[256,6,64]{0,2,1:T(8,128)(2,1)}, bf16[256,6,64]{0,2,1:T(8,128)(2,1)}, u32[]{:S(2)}, u32[]{:S(2)}) collective-permute-start(bf16[256,6,64]{0,2,1:T(8,128)(2,1)} %fusion.74), channel_id=1, source_target_pairs={{2,0},{4,2},{6,4},{8,6},{10,8},{12,10},{14,12},{16,14},{18,16},{20... | collective-permute-start | bytes 589832 | tf_op jit(solution)/shard_map/ppermute | solution.py:20
  1365.1 24.0 %collective-permute-start.36 = (bf16[256,6,64]{0,2,1:T(8,128)(2,1)}, bf16[256,6,64]{0,2,1:T(8,128)(2,1)}, u32[]{:S(2)}, u32[]{:S(2)}) collective-permute-start(bf16[256,6,64]{0,2,1:T(8,128)(2,1)} %fusion.86), channel_id=1, source_target_pairs={{2,0},{4,2},{6,4},{8,6},{10,8},{12,10},{14,12},{16,14},{18,16},{20... | collective-permute-start | bytes 589832 | tf_op jit(solution)/shard_map/ppermute | solution.py:20
  1367.1 24.8 %collective-permute-start.25 = (bf16[256,6,64]{0,2,1:T(8,128)(2,1)}, bf16[256,6,64]{0,2,1:T(8,128)(2,1)}, u32[]{:S(2)}, u32[]{:S(2)}) collective-permute-start(bf16[256,6,64]{0,2,1:T(8,128)(2,1)} %fusion.75), channel_id=1, source_target_pairs={{4,0},{6,2},{8,4},{10,6},{12,8},{14,10},{16,12},{18,14},{20,16},{2... | collective-permute-start | bytes 589832 | tf_op jit(solution)/shard_map/ppermute | solution.py:20
  1394.3 24.6 %collective-permute-start.28 = (bf16[256,6,64]{0,2,1:T(8,128)(2,1)S(1)}, bf16[256,6,64]{0,2,1:T(8,128)(2,1)S(1)}, u32[]{:S(2)}, u32[]{:S(2)}) collective-permute-start(bf16[256,6,64]{0,2,1:T(8,128)(2,1)S(1)} %fusion.78), channel_id=1, source_target_pairs={{10,0},{12,2},{14,4},{16,6},{18,8},{20,10},{22,12},{24,14},{26,16}... | collective-permute-start | bytes 589832 | tf_op jit(solution)/shard_map/ppermute | solution.py:20
  1396.8 27.6 %collective-permute-start.40 = (bf16[256,6,64]{0,2,1:T(8,128)(2,1)S(1)}, bf16[256,6,64]{0,2,1:T(8,128)(2,1)S(1)}, u32[]{:S(2)}, u32[]{:S(2)}) collective-permute-start(bf16[256,6,64]{0,2,1:T(8,128)(2,1)S(1)} %copy-done.116), channel_id=1, source_target_pairs={{10,0},{12,2},{14,4},{16,6},{18,8},{20,10},{22,12},{24,14},{26,16}... | collective-permute-start | bytes 589832 | tf_op jit(solution)/shard_map/ppermute | solution.py:20
  1399.6 35.3 %collective-permute-start.29 = (bf16[256,6,64]{0,2,1:T(8,128)(2,1)S(1)}, bf16[256,6,64]{0,2,1:T(8,128)(2,1)S(1)}, u32[]{:S(2)}, u32[]{:S(2)}) collective-permute-start(bf16[256,6,64]{0,2,1:T(8,128)(2,1)S(1)} %copy-done.114), channel_id=1, source_target_pairs={{12,0},{14,2},{16,4},{18,6},{20,8},{22,10},{24,12},{26,14},{28,16}... | collective-permute-start | bytes 589832 | tf_op jit(solution)/shard_map/ppermute | solution.py:20
  1402.7 34.7 %collective-permute-start.41 = (bf16[256,6,64]{0,2,1:T(8,128)(2,1)S(1)}, bf16[256,6,64]{0,2,1:T(8,128)(2,1)S(1)}, u32[]{:S(2)}, u32[]{:S(2)}) collective-permute-start(bf16[256,6,64]{0,2,1:T(8,128)(2,1)S(1)} %copy-done.115), channel_id=1, source_target_pairs={{12,0},{14,2},{16,4},{18,6},{20,8},{22,10},{24,12},{26,14},{28,16}... | collective-permute-start | bytes 589832 | tf_op jit(solution)/shard_map/ppermute | solution.py:20
  1407.0 34.3 %collective-permute-start.30 = (bf16[256,6,64]{0,2,1:T(8,128)(2,1)S(1)}, bf16[256,6,64]{0,2,1:T(8,128)(2,1)S(1)}, u32[]{:S(2)}, u32[]{:S(2)}) collective-permute-start(bf16[256,6,64]{0,2,1:T(8,128)(2,1)S(1)} %fusion.80), channel_id=1, source_target_pairs={{0,12},{2,14},{4,16},{6,18},{8,20},{10,22},{12,24},{14,26},{16,28}... | collective-permute-start | bytes 589832 | tf_op jit(solution)/shard_map/ppermute | solution.py:20
  1418.9 28.7 %collective-permute-start.31 = (bf16[256,6,64]{0,2,1:T(8,128)(2,1)S(1)}, bf16[256,6,64]{0,2,1:T(8,128)(2,1)S(1)}, u32[]{:S(2)}, u32[]{:S(2)}) collective-permute-start(bf16[256,6,64]{0,2,1:T(8,128)(2,1)S(1)} %copy-done.113), channel_id=1, source_target_pairs={{0,10},{2,12},{4,14},{6,16},{8,18},{10,20},{12,22},{14,24},{16,26}... | collective-permute-start | bytes 589832 | tf_op jit(solution)/shard_map/ppermute | solution.py:20
  1424.5 28.1 %collective-permute-start.32 = (bf16[256,6,64]{0,2,1:T(8,128)(2,1)S(1)}, bf16[256,6,64]{0,2,1:T(8,128)(2,1)S(1)}, u32[]{:S(2)}, u32[]{:S(2)}) collective-permute-start(bf16[256,6,64]{0,2,1:T(8,128)(2,1)S(1)} %copy-done.112), channel_id=1, source_target_pairs={{0,8},{2,10},{4,12},{6,14},{8,16},{10,18},{12,20},{14,22},{16,24},... | collective-permute-start | bytes 589832 | tf_op jit(solution)/shard_map/ppermute | solution.py:20
  1434.9 19.6 collective-permute-start.33
  1437.5 22.2 %collective-permute-start.34 = (bf16[256,6,64]{0,2,1:T(8,128)(2,1)S(1)}, bf16[256,6,64]{0,2,1:T(8,128)(2,1)S(1)}, u32[]{:S(2)}, u32[]{:S(2)}) collective-permute-start(bf16[256,6,64]{0,2,1:T(8,128)(2,1)S(1)} %copy-done.110), channel_id=1, source_target_pairs={{0,4},{2,6},{4,8},{6,10},{8,12},{10,14},{12,16},{14,18},{16,20},{1... | collective-permute-start | bytes 589832 | tf_op jit(solution)/shard_map/ppermute | solution.py:20
  1441.4 23.7 %collective-permute-start.42 = (bf16[256,6,64]{0,2,1:T(8,128)(2,1)}, bf16[256,6,64]{0,2,1:T(8,128)(2,1)S(1)}, u32[]{:S(2)}, u32[]{:S(2)}) collective-permute-start(bf16[256,6,64]{0,2,1:T(8,128)(2,1)} %fusion.92), channel_id=1, source_target_pairs={{0,12},{2,14},{4,16},{6,18},{8,20},{10,22},{12,24},{14,26},{16,28}... | collective-permute-start | bytes 589832 | tf_op jit(solution)/shard_map/ppermute | solution.py:20
  1473.0 699.3 %all-reduce.16.cloned.1.call-start = ((), (), s32[]{:S(2)}) async-start(), calls=%async_computation.11 | async-start | bytes 9437184
  1651.0 29.0 %collective-permute-start.62 = (f32[384,16]{0,1:T(8,128)S(1)}, f32[384,16]{0,1:T(8,128)S(1)}, u32[]{:S(2)}, u32[]{:S(2)}) collective-permute-start(f32[384,16]{0,1:T(8,128)S(1)} %get-tuple-element.91), channel_id=1, source_target_pairs={{0,30},{2,32},{4,34},{6,36},{8,38},{10,40},{12,42},{14,44},{16,46}... | collective-permute-start | bytes 73736
  1652.3 26.4 %collective-permute-start.63 = (f32[384,12]{0,1:T(8,128)S(1)}, f32[384,12]{0,1:T(8,128)S(1)}, u32[]{:S(2)}, u32[]{:S(2)}) collective-permute-start(f32[384,12]{0,1:T(8,128)S(1)} %slice.78), channel_id=1, source_target_pairs={{0,32},{2,34},{4,36},{6,38},{8,40},{10,42},{12,44},{14,46},{16,48}... | collective-permute-start | bytes 55304
  1691.4 29.5 %collective-permute-start.95 = (f32[1536,12]{0,1:T(8,128)S(1)}, f32[1536,12]{0,1:T(8,128)S(1)}, u32[]{:S(2)}, u32[]{:S(2)}) collective-permute-start(f32[1536,12]{0,1:T(8,128)S(1)} %slice.80), channel_id=1, source_target_pairs={{0,32},{2,34},{4,36},{6,38},{8,40},{10,42},{12,44},{14,46},{16,48}... | collective-permute-start | bytes 221192
  1694.0 29.1 %collective-permute-start.79 = (f32[12,1536]{1,0:T(8,128)S(1)}, f32[12,1536]{1,0:T(8,128)S(1)}, u32[]{:S(2)}, u32[]{:S(2)}) collective-permute-start(f32[12,1536]{1,0:T(8,128)S(1)} %slice.79), channel_id=1, source_target_pairs={{0,32},{2,34},{4,36},{6,38},{8,40},{10,42},{12,44},{14,46},{16,48}... | collective-permute-start | bytes 221192
  1733.4 22.8 %collective-permute-start.70 = (f32[16,1536]{1,0:T(8,128)S(1)}, f32[16,1536]{1,0:T(8,128)S(1)}, u32[]{:S(2)}, u32[]{:S(2)}) collective-permute-start(f32[16,1536]{1,0:T(8,128)S(1)} %get-tuple-element.92), channel_id=1, source_target_pairs={{0,14},{2,16},{4,18},{6,20},{8,22},{10,24},{12,26},{14,28},{16,30}... | collective-permute-start | bytes 294920
  1734.7 23.7 %collective-permute-start.69 = (f32[16,1536]{1,0:T(8,128)S(1)}, f32[16,1536]{1,0:T(8,128)S(1)}, u32[]{:S(2)}, u32[]{:S(2)}) collective-permute-start(f32[16,1536]{1,0:T(8,128)S(1)} %get-tuple-element.92), channel_id=1, source_target_pairs={{0,12},{2,14},{4,16},{6,18},{8,20},{10,22},{12,24},{14,26},{16,28}... | collective-permute-start | bytes 294920
  1740.4 20.8 collective-permute-start.68
  1742.6 19.9 collective-permute-start.67
  1747.2 18.0 collective-permute-start.66
  1762.5 18.1 collective-permute-start.93
  1766.9 17.8 collective-permute-start.91
  1768.4 18.2 collective-permute-start.90
  1778.7 24.8 %collective-permute-start.89 = (f32[1536,16]{0,1:T(8,128)S(1)}, f32[1536,16]{0,1:T(8,128)}, u32[]{:S(2)}, u32[]{:S(2)}) collective-permute-start(f32[1536,16]{0,1:T(8,128)S(1)} %get-tuple-element.93), channel_id=1, source_target_pairs={{0,20},{2,22},{4,24},{6,26},{8,28},{10,30},{12,32},{14,34},{16,36}... | collective-permute-start | bytes 294920
  1780.7 25.7 %collective-permute-start.88 = (f32[1536,16]{0,1:T(8,128)S(1)}, f32[1536,16]{0,1:T(8,128)}, u32[]{:S(2)}, u32[]{:S(2)}) collective-permute-start(f32[1536,16]{0,1:T(8,128)S(1)} %get-tuple-element.93), channel_id=1, source_target_pairs={{0,18},{2,20},{4,22},{6,24},{8,26},{10,28},{12,30},{14,32},{16,34}... | collective-permute-start | bytes 294920
  1782.6 26.9 %collective-permute-start.87 = (f32[1536,16]{0,1:T(8,128)S(1)}, f32[1536,16]{0,1:T(8,128)}, u32[]{:S(2)}, u32[]{:S(2)}) collective-permute-start(f32[1536,16]{0,1:T(8,128)S(1)} %get-tuple-element.93), channel_id=1, source_target_pairs={{0,16},{2,18},{4,20},{6,22},{8,24},{10,26},{12,28},{14,30},{16,32}... | collective-permute-start | bytes 294920
  1784.7 27.9 %collective-permute-start.86 = (f32[1536,16]{0,1:T(8,128)S(1)}, f32[1536,16]{0,1:T(8,128)}, u32[]{:S(2)}, u32[]{:S(2)}) collective-permute-start(f32[1536,16]{0,1:T(8,128)S(1)} %get-tuple-element.93), channel_id=1, source_target_pairs={{0,14},{2,16},{4,18},{6,20},{8,22},{10,24},{12,26},{14,28},{16,30}... | collective-permute-start | bytes 294920
  1786.6 28.2 %collective-permute-start.85 = (f32[1536,16]{0,1:T(8,128)S(1)}, f32[1536,16]{0,1:T(8,128)}, u32[]{:S(2)}, u32[]{:S(2)}) collective-permute-start(f32[1536,16]{0,1:T(8,128)S(1)} %get-tuple-element.93), channel_id=1, source_target_pairs={{0,12},{2,14},{4,16},{6,18},{8,20},{10,22},{12,24},{14,26},{16,28}... | collective-permute-start | bytes 294920
  (205 other events, 7190.5 us)
Sparse Core Ops, SparseCore 0:
  10.3 107.6 all-gather.9
  1018.4 30.1 reduce-scatter.13
  1051.0 106.8 all-gather.13
  1160.2 106.3 all-gather.11
  1278.6 16.0 reduce-scatter.17
  1296.8 16.4 reduce-scatter.15
  1473.1 26.7 reduce-scatter.19
  1502.3 575.0 all-reduce.15
where the time goes:
time: 2190 us; the launch traced here: 2180 us
  blocking collectives  1420 us (65%)
  starting transfers between devices  313 us (14%)
  waiting for transfers between devices  226 us (10%)
  matrix products  96.3 us (4%)
  local copies, waits for them, and re-layouts  88.9 us (4%)
    unnamed x3, blocking collectives  502 us
    all_gather x1, blocking collectives, body(): lax.all_gather(ln_gain, ('dp', 'tensor'), axis=2, tiled=True)  312 us
    all_gather x1, blocking collectives, body(): lax.all_gather(row_bias, ('dp', 'tensor'), axis=2, tiled=True)  312 us
    ppermute x48, starting transfers between devices, from_behind(): lax.ppermute(value, axis, [(source, source + steps) for source in range(f...  165 us
    unnamed x49, starting transfers between devices  148 us
    all_gather x1, waiting for transfers between devices, fetch_layer(): lax.all_gather(fc_in[layer], 'dp', axis=0, tiled=True)  96.9 us
    all_gather x1, blocking collectives, fetch_layer(): lax.all_gather(fc_bias[layer], 'dp', axis=1, tiled=True)  84.7 us
    all_gather x1, blocking collectives, fetch_layer(): lax.all_gather(qv_bias[layer], 'dp', axis=2, tiled=True)  83.8 us
  transfers between devices with their start and end apart: 104, of which 26 were waited for; matrix products, arithmetic and copies ran while one was open for 14% of the time, Pallas kernels for 0%

commit v1 on v0

v1 whole, which is shorter than its diff:
```python
import jax
import jax.numpy as jnp
from jax import lax
import jax.experimental.pallas as pl
import jax.experimental.pallas.tpu as pltpu
from jax.sharding import PartitionSpec as P

EPS = 1e-05
NEGATIVE = -1e30
SCORE_SCALE = 0.125
BF = jnp.bfloat16
F32 = jnp.float32
MESH = pl.DeviceIdType.MESH
VM = pl.BlockSpec(memory_space=pltpu.VMEM)
SM = pl.BlockSpec(memory_space=pltpu.SMEM)
DMA = pltpu.SemaphoreType.DMA
LIMIT = 56 * 2**20
NT = (((1,), (1,)), ((), ()))
TN = (((0,), (0,)), ((), ()))


def coords():
    dp = lax.axis_index("dp")
    return dp // 32, (dp // 8) % 4, (dp // 2) % 4, dp % 2, lax.axis_index("tensor")


def device(z, y, x, k, t):
    return (((z * 4 + y) * 4 + x) * 2 + k, t)


def chip(c, k, t):
    return (c * 2 + k, t)


def greet(peers):
    bar = pltpu.get_barrier_semaphore()
    for peer in peers:
        pl.semaphore_signal(bar, inc=1, device_id=peer, device_id_type=MESH)
    pl.semaphore_wait(bar, len(peers))


def remote(src, dst, sems, index, peer):
    send, recv = sems
    return pltpu.make_async_remote_copy(
        src, dst, send.at[index], recv.at[index], device_id=peer, device_id_type=MESH
    )


def comm_call(kernel, out_shape, scratch, cid, name, args):
    single = not isinstance(out_shape, (list, tuple))
    return pl.pallas_call(
        kernel,
        out_shape=out_shape,
        in_specs=[VM] * len(args),
        out_specs=VM if single else [VM] * len(out_shape),
        scratch_shapes=scratch,
        compiler_params=pltpu.CompilerParams(
            collective_id=cid, has_side_effects=True, vmem_limit_bytes=LIMIT
        ),
        name=name,
    )(*args)


def gather_kernel(pay, tile, clip, cot, w, clip_out, cot_out, pay_s, tile_in, send, recv):
    sems = (send, recv)
    z, y, x, k, t = coords()
    xs = [device(z, y, (x + d) % 4, k, t) for d in (1, 2, 3)]
    ys = [device(z, (y + d) % 4, x, k, t) for d in (1, 2, 3)]
    core = device(z, y, x, 1 - k, t)
    far = device(z, y, x, k, 1 - t)
    both = device(z, y, x, 1 - k, 1 - t)
    low = device(1 - z, y, x, k, t)
    greet(xs + ys + [core, far, both, low])
    c_tile = remote(tile, tile_in, sems, 0, far)
    c_tile.start()
    c_clip = remote(clip, clip_out.at[k], sems, 1, core)
    c_clip.start()
    mine = k * 2 + t
    c_cot = [remote(cot, cot_out.at[mine], sems, 2 + i, p) for i, p in enumerate((core, far, both))]
    clip_out[k] = clip[...]
    cot_out[mine] = cot[...]
    c_tile.wait()
    pay_s[...] = pay[...]
    for q in range(2):
        pay_s[q, :, 0:128] = pay[q, :, 0:128] + tile_in[...]
    swap = remote(pay_s.at[1 - k], w.at[z, y, x, k], sems, 5, core)
    swap.start()
    w[z, y, x, k] = pay_s[k]
    swap.wait()
    c_z = remote(w.at[z, y, x], w.at[z, y, x], sems, 6, low)
    c_z.start()
    c_z.wait()
    h0, h1 = pl.ds(0, 1152), pl.ds(1152, 1152)
    phase = []
    for i in range(3):
        a = w.at[:, y, x, :, :, h0]
        phase.append(remote(a, a, sems, 7 + i, xs[i]))
        b = w.at[:, y, x, :, :, h1]
        phase.append(remote(b, b, sems, 10 + i, ys[i]))
    for c in phase:
        c.start()
    for c in c_cot:
        c.start()
    for c in phase:
        c.wait()
    phase = []
    for i in range(3):
        a = w.at[:, y, :, :, :, h0]
        phase.append(remote(a, a, sems, 13 + i, ys[i]))
        b = w.at[:, :, x, :, :, h1]
        phase.append(remote(b, b, sems, 16 + i, xs[i]))
    for c in phase:
        c.start()
    for c in phase:
        c.wait()
    c_clip.wait()
    for c in c_cot:
        c.wait()


def gather_all(pay, tile, clip, cot):
    return comm_call(
        gather_kernel,
        [
            jax.ShapeDtypeStruct((2, 4, 4, 2, 16, 2304), BF),
            jax.ShapeDtypeStruct((2, 2, 256), jnp.int32),
            jax.ShapeDtypeStruct((4, 128, 768), BF),
        ],
        [pltpu.VMEM((2, 16, 2304), BF), pltpu.VMEM((16, 128), BF), DMA((19,)), DMA((19,))],
        0,
        "gather_weights",
        (pay, tile, clip, cot),
    )


def rows_kernel(a, out, send, recv):
    sems = (send, recv)
    z, y, x, k, t = coords()
    core = device(z, y, x, 1 - k, t)
    far = device(z, y, x, k, 1 - t)
    greet([core, far])
    mine, other = k * 2 + t, k * 2 + 1 - t
    c_far = remote(a, out.at[mine], sems, 0, far)
    c_far.start()
    c_core = remote(a, out.at[mine], sems, 1, core)
    c_core.start()
    out[mine] = a[...]
    c_far.wait_recv()
    c_pass = remote(out.at[other], out.at[other], sems, 2, core)
    c_pass.start()
    c_far.wait_send()
    c_core.wait()
    c_pass.wait()


def gather_rows(a, cid, name):
    full = comm_call(
        rows_kernel,
        jax.ShapeDtypeStruct((4, 128, 768), BF),
        [DMA((3,)), DMA((3,))],
        cid,
        name,
        (a,),
    )
    return full.reshape(512, 768)


def sum_kernel(p, out, got, send, recv):
    sems = (send, recv)
    z, y, x, k, t = coords()
    flips = ((0, 1), (1, 1), (1, 0))
    peers = [((k + dk) % 2, (t + dt) % 2) for dk, dt in flips]
    greet([device(z, y, x, pk, pt) for pk, pt in peers])
    copies = []
    for i, (pk, pt) in enumerate(peers):
        copies.append(
            remote(p.at[:, pk * 2 + pt], got.at[i], sems, i, device(z, y, x, pk, pt))
        )
        copies[-1].start()
    for c in copies:
        c.wait()
    total = p[:, k * 2 + t].astype(F32)
    for i in range(3):
        total = total + got[i].astype(F32)
    out[...] = total


def sum_rows(p, cid, name):
    n = p.shape[0]
    return comm_call(
        sum_kernel,
        jax.ShapeDtypeStruct((n, 128, 768), F32),
        [pltpu.VMEM((3, n, 128, 768), BF), DMA((3,)), DMA((3,))],
        cid,
        name,
        (p,),
    )


def ring(c, k, t):
    return [chip((c + d) % 32, k, t) for d in (1, 2, 3, 29, 30, 31)]


SLOTS = (4, 5, 6, 0, 1, 2)


def halo_kernel(kv, out, send, recv):
    sems = (send, recv)
    dp = lax.axis_index("dp")
    c, k, t = dp // 2, dp % 2, lax.axis_index("tensor")
    peers = ring(c, k, t)
    greet(peers)
    copies = []
    for i in (1, 4, 0, 5, 2, 3):
        copies.append(remote(kv, out.at[6 - SLOTS[i]], sems, i, peers[i]))
        copies[-1].start()
    out[3] = kv[...]
    for cp in copies:
        cp.wait()


def halo(kv):
    return comm_call(
        halo_kernel,
        jax.ShapeDtypeStruct((7, 512, 384), BF),
        [DMA((6,)), DMA((6,))],
        1,
        "halo_kv",
        (kv,),
    )


def halo_back_kernel(d, out, got, send, recv):
    sems = (send, recv)
    dp = lax.axis_index("dp")
    c, k, t = dp // 2, dp % 2, lax.axis_index("tensor")
    peers = ring(c, k, t)
    greet(peers)
    copies = []
    for i in (1, 4, 0, 5, 2, 3):
        copies.append(remote(d.at[SLOTS[i]], got.at[i], sems, i, peers[i]))
        copies[-1].start()
    for cp in copies:
        cp.wait()

    @pl.loop(0, 8)
    def _(r):
        rows = pl.ds(pl.multiple_of(r * 64, 64), 64)
        total = d[3, rows, :].astype(F32)
        for i in range(6):
            total = total + got[i, rows, :].astype(F32)
        out[rows, :] = total.astype(BF)


def halo_back(d):
    return comm_call(
        halo_back_kernel,
        jax.ShapeDtypeStruct((512, 384), BF),
        [pltpu.VMEM((6, 512, 384), BF), DMA((6,)), DMA((6,))],
        2,
        "halo_back",
        (d,),
    )


def reduce_kernel(g, out, tile_out, b0, b1, s0, s1, a0, a1, u0, u1, f0, f1, res, tile, send, recv):
    sems = (send, recv)
    z, y, x, k, t = coords()
    px = [(x + d) % 4 for d in (1, 2, 3)]
    py = [(y + d) % 4 for d in (1, 2, 3)]
    xs = [device(z, y, p, k, t) for p in px]
    ys = [device(z, p, x, k, t) for p in py]
    core = device(z, y, x, 1 - k, t)
    far = device(z, y, x, k, 1 - t)
    low = device(1 - z, y, x, k, t)
    greet(xs + ys + [core, far, low])
    h0, h1 = pl.ds(0, 1152), pl.ds(1152, 1152)
    first, second = [], []
    for i in range(3):
        first.append(remote(g.at[:, py[i], :, :, :, h0], b0.at[i], sems, i, ys[i]))
        second.append(remote(g.at[:, :, px[i], :, :, h1], b1.at[i], sems, 3 + i, xs[i]))
        first[-1].start()
        second[-1].start()
    for c in first:
        c.wait()

    @pl.loop(0, 8)
    def _(n):
        zz, m = n // 4, n % 4
        v = g[zz, y, m, :, :, 0:1152].astype(F32)
        for i in range(3):
            v = v + b0[i, zz, m].astype(F32)
        s0[zz, m] = v.astype(BF)

    first = []
    for i in range(3):
        first.append(remote(s0.at[:, px[i]], a0.at[i], sems, 6 + i, xs[i]))
        first[-1].start()
    for c in second:
        c.wait()

    @pl.loop(0, 8)
    def _(n):
        zz, m = n // 4, n % 4
        v = g[zz, m, x, :, :, 1152:2304].astype(F32)
        for i in range(3):
            v = v + b1[i, zz, m].astype(F32)
        s1[zz, m] = v.astype(BF)

    second = []
    for i in range(3):
        second.append(remote(s1.at[:, py[i]], a1.at[i], sems, 9 + i, ys[i]))
        second[-1].start()
    for c in first:
        c.wait()
    for zz in range(2):
        v = s0[zz, x].astype(F32)
        for i in range(3):
            v = v + a0[i, zz].astype(F32)
        u0[zz] = v.astype(BF)
    z0 = remote(u0.at[1 - z], f0, sems, 12, low)
    z0.start()
    for c in second:
        c.wait()
    for zz in range(2):
        v = s1[zz, y].astype(F32)
        for i in range(3):
            v = v + a1[i, zz].astype(F32)
        u1[zz] = v.astype(BF)
    z1 = remote(u1.at[1 - z], f1, sems, 13, low)
    z1.start()
    z0.wait()
    res[:, :, 0:1152] = u0[z].astype(F32) + f0[...].astype(F32)
    z1.wait()
    res[:, :, 1152:2304] = u1[z].astype(F32) + f1[...].astype(F32)
    swap = remote(res.at[1 - k], out.at[k], sems, 14, core)
    swap.start()
    out[k] = res[k]
    swap.wait()
    tile[...] = out[0, :, 0:128] + out[1, :, 0:128]
    c_tile = remote(tile, tile_out, sems, 15, far)
    c_tile.start()
    c_tile.wait()


def reduce_all(g):
    big = (3, 2, 4, 2, 16, 1152)
    return comm_call(
        reduce_kernel,
        [jax.ShapeDtypeStruct((2, 16, 2304), F32), jax.ShapeDtypeStruct((16, 128), F32)],
        [
            pltpu.VMEM(big, BF),
            pltpu.VMEM(big, BF),
            pltpu.VMEM(big[1:], BF),
            pltpu.VMEM(big[1:], BF),
            pltpu.VMEM((3, 2, 2, 16, 1152), BF),
            pltpu.VMEM((3, 2, 2, 16, 1152), BF),
            pltpu.VMEM((2, 2, 16, 1152), BF),
            pltpu.VMEM((2, 2, 16, 1152), BF),
            pltpu.VMEM((2, 16, 1152), BF),
            pltpu.VMEM((2, 16, 1152), BF),
            pltpu.VMEM((2, 16, 2304), F32),
            pltpu.VMEM((16, 128), F32),
            DMA((16,)),
            DMA((16,)),
        ],
        3,
        "reduce_grads",
        (g,),
    )


def allowed_pairs(lim, clip, qb, j):
    cols = pl.ds(qb * 256, 256)
    pos = lim[4] + j * 256 + lax.broadcasted_iota(jnp.int32, (256, 256), 0)
    return (pos >= clip[0:1, cols]) & (pos < clip[1:2, cols])


def attend_kernel(lim, clip, q, kv, of, lse):
    lane = lax.broadcasted_iota(jnp.int32, (256, 128), 1)
    for qb in range(2):
        rows = slice(qb * 256, qb * 256 + 256)

        def step(j, carry):
            ok = allowed_pairs(lim, clip, qb, j)
            new = []
            for h in range(3):
                m, l, acc = carry[h]
                cols = slice(h * 128, h * 128 + 128)
                keys = kv[j, :, cols]
                s = lax.dot_general(keys, q[rows, cols], NT, preferred_element_type=F32)
                s = jnp.where(ok, s, NEGATIVE)
                top = jnp.maximum(m, jnp.max(s, axis=0, keepdims=True))
                p = jnp.exp(s - top)
                fade = jnp.exp(m - top)
                l = l * fade + jnp.sum(p, axis=0, keepdims=True)
                acc = acc * fade + lax.dot_general(
                    keys, p.astype(BF), TN, preferred_element_type=F32
                )
                new.append((top, l, acc))
            return tuple(new)

        start = tuple(
            (
                jnp.full((1, 256), NEGATIVE, F32),
                jnp.zeros((1, 256), F32),
                jnp.zeros((128, 256), F32),
            )
            for _ in range(3)
        )
        final = lax.fori_loop(lim[2 * qb], lim[2 * qb + 1], step, start)
        for h in range(3):
            m, l, acc = final[h]
            o = (acc / l).T
            of[rows, h * 128 : h * 128 + 128] = jnp.where(lane >= 64, o, 0.0)
            lse[h : h + 1, rows] = m + jnp.log(l)


def attend(lim, clip, q, kv):
    return pl.pallas_call(
        attend_kernel,
        out_shape=[
            jax.ShapeDtypeStruct((512, 384), F32),
            jax.ShapeDtypeStruct((3, 512), F32),
        ],
        in_specs=[SM, VM, VM, VM],
        out_specs=[VM, VM],
        compiler_params=pltpu.CompilerParams(vmem_limit_bytes=LIMIT),
        name="attend",
    )(lim, clip, q, kv)


def attend_back_kernel(lim, clip, q, dox, kv, lse, delta, dq, dkv, total):
    lane = lax.broadcasted_iota(jnp.int32, (256, 128), 1)

    @pl.loop(0, 14)
    def _(j):
        total[j] = jnp.zeros((256, 384), F32)

    for qb in range(2):
        rows = slice(qb * 256, qb * 256 + 256)

        def step(j, carry):
            ok = allowed_pairs(lim, clip, qb, j)
            new = []
            for h in range(3):
                cols = slice(h * 128, h * 128 + 128)
                keys = kv[j, :, cols]
                qh, dh = q[rows, cols], dox[rows, cols]
                s = lax.dot_general(keys, qh, NT, preferred_element_type=F32)
                p = jnp.exp(jnp.where(ok, s, NEGATIVE) - lse[h : h + 1, rows])
                dp = lax.dot_general(keys, dh, NT, preferred_element_type=F32)
                ds = (p * (dp - delta[h : h + 1, rows])).astype(BF)
                new.append(
                    carry[h] + lax.dot_general(keys, ds, TN, preferred_element_type=F32)
                )
                total[j, :, cols] += jnp.dot(
                    ds, qh, preferred_element_type=F32
                ) + jnp.dot(p.astype(BF), dh, preferred_element_type=F32)
            return tuple(new)

        start = tuple(jnp.zeros((128, 256), F32) for _ in range(3))
        final = lax.fori_loop(lim[2 * qb], lim[2 * qb + 1], step, start)
        for h in range(3):
            back = jnp.where(lane < 64, SCORE_SCALE * final[h].T, 0.0)
            dq[rows, h * 128 : h * 128 + 128] = back.astype(BF)

    @pl.loop(0, 14)
    def _(j):
        dkv[j] = total[j].astype(BF)


def attend_back(lim, clip, q, dox, kv, lse, delta):
    return pl.pallas_call(
        attend_back_kernel,
        out_shape=[
            jax.ShapeDtypeStruct((512, 384), BF),
            jax.ShapeDtypeStruct((14, 256, 384), BF),
        ],
        in_specs=[SM] + [VM] * 6,
        out_specs=[VM, VM],
        scratch_shapes=[pltpu.VMEM((14, 256, 384), F32)],
        compiler_params=pltpu.CompilerParams(vmem_limit_bytes=LIMIT),
        name="attend_back",
    )(lim, clip, q, dox, kv, lse, delta)


def matmul(left, right):
    return jnp.dot(left, right, preferred_element_type=F32)


def matmul_nt(left, right):
    return lax.dot_general(left, right, NT, preferred_element_type=F32)


def matmul_tn(left, right):
    return lax.dot_general(left, right, TN, preferred_element_type=F32)


def normalize(hidden, gain, offset):
    average = jnp.mean(hidden, axis=-1, keepdims=True)
    centred = hidden - average
    spread = jnp.mean(centred * centred, axis=-1, keepdims=True)
    scale = lax.rsqrt(spread + EPS)
    unit = centred * scale
    return unit * gain + offset, unit, scale


def normalize_back(grad_out, unit, scale, gain):
    grad_unit = grad_out * gain
    first = jnp.mean(grad_unit, axis=-1, keepdims=True)
    second = jnp.mean(grad_unit * unit, axis=-1, keepdims=True)
    return scale * (grad_unit - first - unit * second)


def body(
    tokens,
    clip_bounds,
    attn_in,
    qv_bias,
    out_proj,
    fc_in,
    fc_bias,
    fc_out,
    ln_gain,
    row_bias,
    cotangent,
):
    dp = lax.axis_index("dp")
    c, k, t = dp // 2, dp % 2, lax.axis_index("tensor")
    feature = lax.broadcasted_iota(jnp.int32, (768, 1024), 0)
    place = lax.broadcasted_iota(jnp.int32, (768, 1024), 1)
    select = (place == (feature // 12) * 16 + feature % 12).astype(BF)

    def widen(rows):
        return matmul(rows, select).astype(BF)

    def narrow(rows):
        return matmul_nt(rows.astype(BF), select).astype(BF)

    parts = attn_in[0].reshape(3, 12, 6, 64)
    proj = out_proj[0].T.reshape(12, 6, 64)
    kv_w = jnp.stack([parts[1], parts[2]], axis=2).reshape(12, 2, 384)
    qo_w = jnp.stack([parts[0], proj], axis=2).reshape(12, 2, 384)
    up_w = fc_in[0].reshape(12, 2, 768)
    down_w = fc_out[0].T.reshape(12, 2, 768)
    pay = jnp.concatenate([kv_w, qo_w, up_w, down_w], axis=-1).transpose(1, 0, 2)
    small = jnp.concatenate(
        [ln_gain.reshape(-1), row_bias.reshape(-1), qv_bias.reshape(-1), fc_bias.reshape(-1)]
    )
    small = jnp.pad(small, (0, 56))
    extra = jnp.pad(small.reshape(1, 1, 128), ((0, 0), (0, 3), (0, 2176)))
    extra = jnp.concatenate([extra, extra], axis=0)
    pay = jnp.concatenate([pay, extra], axis=1)
    tile = jnp.pad(small.reshape(1, 128), ((13, 2), (0, 0)))
    w, clip, cot = gather_all(pay, tile, clip_bounds, cotangent)
    clip = clip.transpose(1, 0, 2).reshape(2, 512)
    w = w.reshape(1024, 2304)
    w_kv, w_qo, w_up, w_down = w[:, 0:384], w[:, 384:768], w[:, 768:1536], w[:, 1536:2304]

    smalls = w.reshape(64, 16, 2304)[:, 12:14, 0:128].astype(F32)
    pair = jnp.where(t == 0, smalls, smalls[:, ::-1])
    gains = pair[:, :, 0:12].reshape(64, 2, 2, 6).transpose(2, 0, 1, 3).reshape(2, 768)
    biases = pair[:, :, 12:36].reshape(64, 2, 4, 6).transpose(2, 0, 1, 3).reshape(4, 768)
    heads = smalls[:, 0, 36:48].reshape(64, 2, 2, 3)
    heads = jnp.where(k == 0, heads[:, :, 0], heads[:, :, 1]).transpose(1, 2, 0)
    blank = jnp.zeros((3, 64), F32)
    qo_bias = jnp.concatenate([heads[0], blank], axis=1).reshape(384)
    kv_bias = jnp.concatenate([blank, heads[1]], axis=1).reshape(384)
    up_bias = smalls[:, 0, 48:72].reshape(64, 2, 3, 4)
    up_bias = jnp.where(k == 0, up_bias[:, 0], up_bias[:, 1]).transpose(1, 0, 2).reshape(768)
    low_lanes = (jnp.arange(384, dtype=jnp.int32) % 128) < 64

    hidden = tokens.astype(F32)
    normed, unit_one, scale_one = normalize(hidden, gains[0], biases[0])
    full_one = widen(gather_rows(normed.astype(BF), 4, "rows_one"))
    kv = (matmul(full_one, w_kv) + kv_bias).astype(BF)
    query = (matmul(full_one, w_qo) + qo_bias).astype(BF)
    query = jnp.where(low_lanes, query * BF(SCORE_SCALE), BF(0))
    near = halo(kv).reshape(14, 256, 384)
    base = (c - 3) * 512
    lim = jnp.stack(
        [
            (clip[0, 0] - base) // 256,
            (clip[1, 255] - base + 255) // 256,
            (clip[0, 256] - base) // 256,
            (clip[1, 511] - base + 255) // 256,
            base,
        ]
    ).astype(jnp.int32)
    mixed, lse = attend(lim, clip, query, near)
    mixed_low = mixed.astype(BF)
    attn = narrow(matmul_nt(mixed_low, w_qo))
    attn = sum_rows(attn.reshape(1, 4, 128, 768), 5, "sum_attn")[0]
    hidden_one = hidden + attn + biases[1]
    normed_two, unit_two, scale_two = normalize(hidden_one, gains[1], biases[2])
    full_two = widen(gather_rows(normed_two.astype(BF), 6, "rows_two"))
    inner = matmul(full_two, w_up) + up_bias
    gelu = lambda v: jax.nn.gelu(v, approximate=False)
    active = gelu(inner).astype(BF)
    mlp = narrow(matmul_nt(active, w_down))
    full_mlp = widen(cot.reshape(512, 768))
    grad_active = matmul(full_mlp, w_down)
    _, gelu_back = jax.vjp(gelu, inner)
    grad_inner = gelu_back(grad_active)[0].astype(BF)
    back_two = narrow(matmul_nt(grad_inner, w_up))
    pair_sum = sum_rows(jnp.stack([mlp, back_two]).reshape(2, 4, 128, 768), 7, "sum_mlp")
    output = (hidden_one + pair_sum[0] + biases[3]).astype(BF)
    grad_normed_two = pair_sum[1]
    grad_hidden_one = cotangent.astype(F32) + normalize_back(
        grad_normed_two, unit_two, scale_two, gains[1]
    )
    grad_attn = grad_hidden_one.astype(BF)
    full_attn = widen(gather_rows(grad_attn, 8, "rows_back"))
    grad_mixed = jnp.where(low_lanes, 0.0, matmul(full_attn, w_qo)).astype(BF)
    delta = (grad_mixed.astype(F32) * mixed).reshape(512, 3, 128).sum(axis=-1).T
    grad_query, grad_near = attend_back(lim, clip, query, grad_mixed, near, lse, delta)
    grad_kv = halo_back(grad_near.reshape(7, 512, 384))
    back_one = narrow(matmul_nt(grad_query, w_qo) + matmul_nt(grad_kv, w_kv))
    grad_normed_one = sum_rows(back_one.reshape(1, 4, 128, 768), 9, "sum_back")[0]
    grad_tokens = grad_hidden_one + normalize_back(
        grad_normed_one, unit_one, scale_one, gains[0]
    )

    sums = jnp.stack(
        [
            jnp.sum(grad_normed_one * unit_one, axis=0),
            jnp.sum(grad_normed_two * unit_two, axis=0),
            jnp.sum(grad_normed_one, axis=0),
            jnp.sum(grad_attn.astype(F32), axis=0),
            jnp.sum(grad_normed_two, axis=0),
            jnp.sum(cotangent.astype(F32), axis=0),
        ]
    )
    sums = sums.reshape(6, 64, 12).transpose(1, 0, 2).reshape(64, 72)
    q_sum = jnp.sum(grad_query.astype(F32), axis=0).reshape(3, 128)[:, :64]
    v_sum = jnp.sum(grad_kv.astype(F32), axis=0).reshape(3, 128)[:, 64:]
    qv_sum = jnp.concatenate([q_sum, v_sum], axis=0).T
    up_sum = jnp.sum(grad_inner.astype(F32), axis=0)
    up_sum = up_sum.reshape(3, 64, 4).transpose(1, 0, 2).reshape(64, 12)
    smalls = jnp.concatenate([sums, qv_sum, up_sum], axis=1)
    smalls = jnp.pad(smalls.reshape(64, 1, 90), ((0, 0), (12, 3), (0, 294))).reshape(1024, 384)
    grads = jnp.concatenate(
        [
            (matmul_tn(full_one, grad_kv) + smalls).astype(BF),
            (matmul_tn(full_one, grad_query) + matmul_tn(full_attn, mixed_low)).astype(BF),
            matmul_tn(full_two, grad_inner).astype(BF),
            matmul_tn(full_mlp, active).astype(BF),
        ],
        axis=1,
    )
    own, far = reduce_all(grads.reshape(2, 4, 4, 2, 16, 2304))
    vec = own[0, 12, 0:128] + own[1, 12, 0:128] + far[12]
    vec = vec[0:72].reshape(6, 2, 6)
    vec = jnp.where(t == 0, vec[:, 0], vec[:, 1])
    grad_gain, grad_row = vec[0:2].reshape(1, 2, 6), vec[2:6].reshape(1, 4, 6)
    grad_qv = own[:, 12, 72:78].reshape(2, 2, 3).transpose(1, 0, 2).reshape(1, 2, 6, 1)
    grad_up_bias = own[:, 12, 78:90].reshape(1, 6, 4)
    main = own[:, 0:12].transpose(1, 0, 2)
    g_kv = main[:, :, 0:384].reshape(12, 6, 2, 64)
    g_qo = main[:, :, 384:768].reshape(12, 6, 2, 64)
    grad_in = jnp.stack(
        [
            g_qo[:, :, 0].reshape(12, 384),
            g_kv[:, :, 0].reshape(12, 384),
            g_kv[:, :, 1].reshape(12, 384),
        ]
    )[None]
    grad_out = g_qo[:, :, 1].reshape(12, 384).T[None]
    grad_up = main[:, :, 768:1536].reshape(1, 12, 1536)
    grad_down = main[:, :, 1536:2304].reshape(12, 1536).T[None]
    return (
        output,
        grad_tokens,
        grad_in,
        grad_qv,
        grad_out,
        grad_up,
        grad_up_bias,
        grad_down,
        grad_gain,
        grad_row,
    )


def solution(mesh):
    return jax.shard_map(
        body,
        mesh=mesh,
        in_specs=(
            P(("dp", "tensor"), None),
            P(None, "dp"),
            P(None, None, "dp", "tensor"),
            P(None, None, "tensor", "dp"),
            P(None, "tensor", "dp"),
            P(None, "dp", "tensor"),
            P(None, "tensor", "dp"),
            P(None, "tensor", "dp"),
            P(None, None, ("dp", "tensor")),
            P(None, None, ("dp", "tensor")),
            P(("dp", "tensor"), None),
        ),
        out_specs=(
            P(("dp", "tensor"), None),
            P(("dp", "tensor"), None),
            P(None, None, "dp", "tensor"),
            P(None, None, "tensor", "dp"),
            P(None, "tensor", "dp"),
            P(None, "dp", "tensor"),
            P(None, "tensor", "dp"),
            P(None, "tensor", "dp"),
            P(None, None, ("dp", "tensor")),
            P(None, None, ("dp", "tensor")),
        ),
        check_vma=False,
    )
```

time: 2190 us -> 450 us (0.21)
  blocking collectives: 1420 us -> 0 us
  Pallas kernels: 0 us -> 328 us
  starting transfers between devices: 313 us -> 0 us
  waiting for transfers between devices: 226 us -> 0 us
  local copies, waits for them, and re-layouts: 88.9 us -> 33.4 us
  matrix products: 96.3 us -> 57.3 us
    all_gather x9 -> x0, blocking collectives: 914 us -> none  [the longest x1 312 us: body(): lax.all_gather(ln_gain, ('dp', 'tensor'), axis=2, tiled=True)]
    unnamed x3 -> x0, blocking collectives: 502 us -> none
    pallas_call x0 -> x12, Pallas kernels: none -> 328 us  [the longest x10 290 us: comm_call(): pl.pallas_call(kernel, out_shape=out_shape, in_specs=[VM] * len(args), ou...]
    ppermute x48 -> x0, starting transfers between devices: 165 us -> none  [from_behind(): lax.ppermute(value, axis, [(source, source + steps) for source in range(f...]
    unnamed x49 -> x0, starting transfers between devices: 148 us -> none
    all_gather x3 -> x0, waiting for transfers between devices: 119 us -> none  [the longest x1 96.9 us: fetch_layer(): lax.all_gather(fc_in[layer], 'dp', axis=0, tiled=True)]
    ppermute x48 -> x0, waiting for transfers between devices: 82 us -> none  [from_behind(): lax.ppermute(value, axis, [(source, source + steps) for source in range(f...]
    dot_general x90 -> x22, matrix products: 96.3 us -> 57.3 us  [the longest x9 27.2 us: matmul(): return jnp.dot(left, right, preferred_element_type=F32)]
  transfers between devices with their start and end apart: 104 -> 0, of which waited for: 26 -> 0; matrix products, arithmetic and copies ran while one was open for 14% -> 0% of each run, Pallas kernels for 0% -> 0%
where the time goes in v1:
time: 450 us; the launch traced here: 448 us
  Pallas kernels  328 us (73%)
  matrix products  57.3 us (13%)
  local copies, waits for them, and re-layouts  33.4 us (7%)
  other arithmetic  24.7 us (5%)
    pallas_call x10, Pallas kernels, comm_call(): pl.pallas_call(kernel, out_shape=out_shape, in_specs=[VM] * len(args), ou...  290 us
    dot_general x9, matrix products, matmul(): return jnp.dot(left, right, preferred_element_type=F32)  27.2 us
    dot_general x8, matrix products, matmul_nt(): return lax.dot_general(left, right, NT, preferred_element_type=F32)  20.3 us
    pallas_call x1, Pallas kernels, attend_back(): pl.pallas_call(attend_back_kernel, out_shape=[jax.ShapeDtypeStruct((512,...  19.9 us
    pallas_call x1, Pallas kernels, attend(): pl.pallas_call(attend_kernel, out_shape=[jax.ShapeDtypeStruct((512, 384),...  18.2 us
    dot_general x5, matrix products, matmul_tn(): return lax.dot_general(left, right, TN, preferred_element_type=F32)  9.84 us

profile of v1, /device:TPU:1, one launch (start us, length us, event | category | flops | bytes accessed | tf_op | source)
XLA Modules:
  0.0 448.1 jit_solution(14784108308218676507)
XLA Ops:
  2.9 1.0 convert_reduce_fusion.3
  4.0 1.1 fusion.44
  11.4 2.3 add_compare_fusion.21
  13.7 55.0 %gather_weights.1 = (bf16[2,4,4,2,16,2304]{5,4,3,2,1,0:T(8,128)(2,1)}, s32[2,2,256]{2,1,0:T(2,128)}, bf16[4,128,768]{2,1,0:T(8,128)(2,1)}) custom-call(bf16[2,16,2304]{2,1,0:T(8,128)(2,1)} %maximum_maximum_fusion.pay, bf16[16,128]{1,0:T(8,128)(2,1)} %pad.20.tile, s32[2,256]{1,0:T(2,128)} %clip.1, bf16[128,768]{1,0:T(8,128)(2,1)} %cot.1), custom_call_target="tpu_custom_call" | custom-call | tf_op jit(solution)/shard_map/gather_weights/pallas_call | solution.py:51
  68.6 1.4 fusion.74
  77.3 2.4 convolution_convert_fusion.6
  79.7 13.3 %rows_one.1 = bf16[4,128,768]{2,1,0:T(8,128)(2,1)} custom-call(bf16[128,768]{1,0:T(8,128)(2,1)} %fusion.38.a), custom_call_target="tpu_custom_call" | custom-call | tf_op jit(solution)/shard_map/rows_one/pallas_call | solution.py:51
  93.1 2.6 convolution_convert_fusion.8
  95.7 1.5 fusion.15.q
  97.2 1.5 fusion.12.kv
  98.7 42.8 %halo_kv.1 = bf16[7,512,384]{2,1,0:T(8,128)(2,1)} custom-call(bf16[512,384]{1,0:T(8,128)(2,1)} %fusion.12.kv), custom_call_target="tpu_custom_call" | custom-call | tf_op jit(solution)/shard_map/halo_kv/pallas_call | solution.py:51
  141.4 18.2 %attend.1 = (f32[512,384]{1,0:T(8,128)}, f32[3,512]{1,0:T(4,128)}) custom-call(s32[5]{0:T(128)} %stack.64.lim, s32[2,512]{1,0:T(2,128)} %bitcast.207, bf16[512,384]{1,0:T(8,128)(2,1)} %fusion.15.q, bf16[14,256,384]{2,1,0:T(8,128)(2,1)} %bitcast.169), custom_call_target="tpu_custom_call" | custom-call | tf_op jit(solution)/shard_map/attend/pallas_call | solution.py:420
  159.6 1.9 convolution_convert_fusion.4.clone.5
  161.5 2.9 convolution_convert_fusion.12
  164.4 15.3 %sum_attn.1 = f32[1,128,768]{2,1,0:T(8,128)} custom-call(bf16[1,4,128,768]{3,2,1,0:T(8,128)(2,1)} %bitcast.189), custom_call_target="tpu_custom_call" | custom-call | tf_op jit(solution)/shard_map/sum_attn/pallas_call | solution.py:51
  179.8 1.1 fusion.67
  181.9 11.6 %rows_two.1 = bf16[4,128,768]{2,1,0:T(8,128)(2,1)} custom-call(bf16[128,768]{1,0:T(8,128)(2,1)} %add_convert_fusion.4.a), custom_call_target="tpu_custom_call" | custom-call | tf_op jit(solution)/shard_map/rows_two/pallas_call | solution.py:51
  193.6 2.6 convolution_convert_fusion.7
  196.2 9.8 %multiply_convert_fusion = (bf16[512,768]{1,0:T(8,128)(2,1)}, f32[512,768]{1,0:T(8,128)S(1)}, f32[512,768]{1,0:T(8,128)S(1)}) fusion(f32[768]{0:T(1024)S(1)} %add.216, bf16[512,1024]{1,0:T(8,128)(2,1)S(1)} %convolution_convert_fusion.7, bf16[1024,2304]{1,0:T(8,128)(2,1)S(1)} %bitcast.186), kind=kOutput, calls=%fused_computation.12 | convolution fusion | flops 831258624 | bytes 6557696 | tf_op jit(solution)/shard_map/dot_general | solution.py:489
  205.9 1.4 convert_reduce_fusion
  208.2 3.4 convolution_convert_fusion.1
  211.6 2.7 convolution_convert_fusion.2.clone.5
  214.3 2.2 convolution_convert_fusion.10
  216.5 2.2 convolution_convert_fusion
  218.7 2.4 convolution_convert_fusion.3.clone.5
  221.1 2.4 convolution_convert_fusion.11
  223.6 1.3 pad_maximum_fusion.1.p
  224.9 23.4 %sum_mlp.1 = f32[2,128,768]{2,1,0:T(8,128)} custom-call(bf16[2,4,128,768]{3,2,1,0:T(8,128)(2,1)} %pad_maximum_fusion.1.p), custom_call_target="tpu_custom_call" | custom-call | tf_op jit(solution)/shard_map/sum_mlp/pallas_call | solution.py:51
  248.3 1.1 slice_reduce_fusion
  249.4 1.2 fusion.46
  252.4 11.7 %rows_back.1 = bf16[4,128,768]{2,1,0:T(8,128)(2,1)} custom-call(bf16[128,768]{1,0:T(8,128)(2,1)} %get-tuple-element.69.a), custom_call_target="tpu_custom_call" | custom-call | tf_op jit(solution)/shard_map/rows_back/pallas_call | solution.py:51
  264.0 2.6 convolution_convert_fusion.5
  266.7 2.9 convert_multiply_fusion
  269.6 2.3 copy.85
  271.9 1.8 reduce_sum.168
  273.7 19.9 %attend_back.1 = (bf16[512,384]{1,0:T(8,128)(2,1)}, bf16[14,256,384]{2,1,0:T(8,128)(2,1)}) custom-call(s32[5]{0:T(128)} %stack.64.lim, s32[2,512]{1,0:T(2,128)} %bitcast.208, bf16[512,384]{1,0:T(8,128)(2,1)} %fusion.15.q, bf16[512,384]{1,0:T(8,128)(2,1)} %get-tuple-element.98.dox, bf16[14,256,384]{2,1,0:T(8,128)(2,1)} %bitcast.170, ...), custom_call_target="tpu_custom_call" | custom-call | tf_op jit(solution)/shard_map/attend_back/pallas_call | solution.py:474
  293.6 49.2 %halo_back.1 = bf16[512,384]{1,0:T(8,128)(2,1)} custom-call(bf16[7,512,384]{2,1,0:T(8,128)(2,1)} %bitcast.174), custom_call_target="tpu_custom_call" | custom-call | tf_op jit(solution)/shard_map/halo_back/pallas_call | solution.py:51
  342.8 1.1 convert_reduce_fusion.1
  344.7 1.6 add_convert_fusion.1
  346.2 1.9 fusion.25
  348.2 3.8 convolution_convert_fusion.9
  352.0 15.2 %sum_back.1 = f32[1,128,768]{2,1,0:T(8,128)} custom-call(bf16[1,4,128,768]{3,2,1,0:T(8,128)(2,1)} %bitcast.188), custom_call_target="tpu_custom_call" | custom-call | tf_op jit(solution)/shard_map/sum_back/pallas_call | solution.py:51
  368.2 1.2 fusion.43
  369.5 1.9 fusion.42
  372.6 2.1 add_convert_fusion.2
  374.7 3.7 pad_maximum_fusion
  378.3 6.8 %copy.96 = bf16[1024,2304]{1,0:T(8,128)(2,1)} copy(bf16[1024,2304]{0,1:T(8,128)(2,1)} %pad_maximum_fusion) | data formatting | bytes 9437184 | tf_op jit(solution)/shard_map/concatenate | solution.py:643
  385.1 52.9 %reduce_grads.1 = (f32[2,16,2304]{2,1,0:T(8,128)}, f32[16,128]{1,0:T(8,128)}) custom-call(bf16[2,4,4,2,16,2304]{5,4,3,2,1,0:T(8,128)(2,1)} %bitcast.171), custom_call_target="tpu_custom_call" | custom-call | tf_op jit(solution)/shard_map/reduce_grads/pallas_call | solution.py:51
  (173 shorter events, 29.5 us)
Async XLA Ops:
  11.4 65.1 %copy-start.2 = (bf16[128,768]{1,0:T(8,128)(2,1)S(1)}, bf16[128,768]{1,0:T(8,128)(2,1)}, u32[]{:S(2)}) copy-start(bf16[128,768]{1,0:T(8,128)(2,1)} %param.11) | copy-start | bytes 589828
  68.6 8.7 %copy-start.9 = (bf16[4,128,768]{2,1,0:T(8,128)(2,1)S(1)}, bf16[4,128,768]{2,1,0:T(8,128)(2,1)}, u32[]{:S(2)}) copy-start(bf16[4,128,768]{2,1,0:T(8,128)(2,1)} %get-tuple-element.22) | copy-start | bytes 2359300
  79.7 16.0 %slice-start = ((s8[4718592]{0:T(1024)(128)(4,1)}), s8[4194304]{0:T(1024)(128)(4,1)S(1)}, s32[]{:S(2)}) async-start(s8[4718592]{0:T(1024)(128)(4,1)} %bitcast.181), calls=%async_computation | async-start | bytes 8388608
  93.1 2.7 slice-start.1
  95.7 248.3 %copy-start.3 = (bf16[512,1024]{1,0:T(8,128)(2,1)}, bf16[512,1024]{1,0:T(8,128)(2,1)S(1)}, u32[]{:S(2)}) copy-start(bf16[512,1024]{1,0:T(8,128)(2,1)S(1)} %convolution_convert_fusion.8) | copy-start | bytes 3145732
  196.1 9.8 %copy-start.14 = (bf16[512,1024]{1,0:T(8,128)(2,1)}, bf16[512,1024]{1,0:T(8,128)(2,1)S(1)}, u32[]{:S(2)}) copy-start(bf16[512,1024]{1,0:T(8,128)(2,1)S(1)} %convolution_convert_fusion.7) | copy-start | bytes 3145732
  196.2 9.8 %copy-start.12 = (bf16[512,1024]{1,0:T(8,128)(2,1)S(1)}, bf16[512,1024]{1,0:T(8,128)(2,1)}, u32[]{:S(2)}) copy-start(bf16[512,1024]{1,0:T(8,128)(2,1)} %convolution_convert_fusion.6) | copy-start | bytes 3145732
  207.3 0.9 copy-start.11
  214.3 2.3 copy-start.10
  214.3 2.3 copy-start.13
  224.9 25.8 %copy-start.8 = (bf16[128,768]{1,0:T(8,128)(2,1)S(1)}, bf16[128,768]{1,0:T(8,128)(2,1)}, u32[]{:S(2)}) copy-start(bf16[128,768]{1,0:T(8,128)(2,1)} %cot.1) | copy-start | bytes 589828
  248.3 2.4 copy-start
  264.0 2.6 copy-start.1
  293.6 50.4 %copy-start.5 = (bf16[512,384]{1,0:T(8,128)(2,1)S(1)}, bf16[512,384]{1,0:T(8,128)(2,1)}, u32[]{:S(2)}) copy-start(bf16[512,384]{1,0:T(8,128)(2,1)} %get-tuple-element.24) | copy-start | bytes 1179652
  346.2 1.9 copy-start.4
  372.5 2.1 copy-start.6
  372.6 2.1 copy-start.7

commit v2 on v1

v2 whole, which is shorter than its diff:
```python
import jax
import jax.numpy as jnp
from jax import lax
import jax.experimental.pallas as pl
import jax.experimental.pallas.tpu as pltpu
from jax.sharding import PartitionSpec as P

EPS = 1e-05
NEGATIVE = -1e30
SCORE_SCALE = 0.125
BF = jnp.bfloat16
F32 = jnp.float32
MESH = pl.DeviceIdType.MESH
VM = pl.BlockSpec(memory_space=pltpu.VMEM)
SM = pl.BlockSpec(memory_space=pltpu.SMEM)
DMA = pltpu.SemaphoreType.DMA
LIMIT = 56 * 2**20
NT = (((1,), (1,)), ((), ()))
TN = (((0,), (0,)), ((), ()))


def coords():
    dp = lax.axis_index("dp")
    return dp // 32, (dp // 8) % 4, (dp // 2) % 4, dp % 2, lax.axis_index("tensor")


def device(z, y, x, k, t):
    return (((z * 4 + y) * 4 + x) * 2 + k, t)


def chip(c, k, t):
    return (c * 2 + k, t)


def greet(peers):
    bar = pltpu.get_barrier_semaphore()
    for peer in peers:
        pl.semaphore_signal(bar, inc=1, device_id=peer, device_id_type=MESH)
    pl.semaphore_wait(bar, len(peers))


def remote(src, dst, sems, index, peer):
    send, recv = sems
    return pltpu.make_async_remote_copy(
        src, dst, send.at[index], recv.at[index], device_id=peer, device_id_type=MESH
    )


def comm_call(kernel, out_shape, scratch, cid, name, args):
    single = not isinstance(out_shape, (list, tuple))
    return pl.pallas_call(
        kernel,
        out_shape=out_shape,
        in_specs=[VM] * len(args),
        out_specs=VM if single else [VM] * len(out_shape),
        scratch_shapes=scratch,
        compiler_params=pltpu.CompilerParams(
            collective_id=cid, has_side_effects=True, vmem_limit_bytes=LIMIT
        ),
        name=name,
    )(*args)


def spots():
    z, y, x, k, t = coords()
    xs = [device(z, y, (x + d) % 4, k, t) for d in (1, 2, 3)]
    ys = [device(z, (y + d) % 4, x, k, t) for d in (1, 2, 3)]
    core = device(z, y, x, 1 - k, t)
    far = device(z, y, x, k, 1 - t)
    low = device(1 - z, y, x, k, t)
    ring = [chip(((z * 4 + y) * 4 + x + d) % 32, k, t) for d in RING]
    return (z, y, x, k, t), xs, ys, core, far, low, ring


RING = (2, -2, 3, -3, 1, -1)


class Copies:
    def __init__(self, send, recv):
        self.sems, self.count = (send, recv), 0

    def __call__(self, src, dst, peer):
        made = remote(src, dst, self.sems, self.count, peer)
        self.count += 1
        made.start()
        return made


def gather_kernel(
    pay, tile, clip, cot, tok, w, f0, f1, clip_out, cot_out, tk, pay_s, tile_in, ws, send, recv
):
    (z, y, x, k, t), xs, ys, core, far, low, ring = spots()
    copy = Copies(send, recv)
    mine, other = k * 2 + t, k * 2 + 1 - t
    greet(xs + ys + [core, far, low] + ring)
    c_tile = copy(tile, tile_in, far)
    cot_far = copy(cot, cot_out.at[mine], far)
    own_far = copy(tok, tk.at[3, mine], far)
    order = (4, 5, 2, 3, 0, 1)
    pushes = {i: copy(tok, tk.at[3 - RING[i], mine], ring[i]) for i in order}
    done = [
        copy(cot, cot_out.at[mine], core),
        copy(tok, tk.at[3, mine], core),
        copy(clip, clip_out.at[k], core),
    ]
    clip_out[k] = clip[...]
    cot_out[mine] = cot[...]
    tk[3, mine] = tok[...]
    c_tile.wait()
    pay_s[...] = pay[...]
    for q in range(2):
        pay_s[q, :, 0:128] = pay[q, :, 0:128] + tile_in[...]
    swap = copy(pay_s.at[1 - k], ws.at[z, k], core)
    ws[z, k] = pay_s[k]
    swap.wait()
    copy(ws.at[z], ws.at[z], low).wait()
    w[:, y, x] = ws[:, :, :, 0:768]
    f0[:, x] = ws[:, :, :, 768:1536]
    f1[:, y] = ws[:, :, :, 1536:2304]
    h0, h1 = pl.ds(0, 384), pl.ds(384, 384)
    phase = []
    for i in range(3):
        phase.append(copy(ws.at[:, :, :, h0], w.at[:, y, x, :, :, h0], xs[i]))
        phase.append(copy(ws.at[:, :, :, h1], w.at[:, y, x, :, :, h1], ys[i]))
    rest = []
    for i in range(3):
        rest.append(copy(ws.at[:, :, :, pl.ds(768, 768)], f0.at[:, x], xs[i]))
        rest.append(copy(ws.at[:, :, :, pl.ds(1536, 768)], f1.at[:, y], ys[i]))
    for c in phase:
        c.wait()
    for i in range(3):
        a = w.at[:, y, :, :, :, h0]
        rest.append(copy(a, a, ys[i]))
        b = w.at[:, :, x, :, :, h1]
        rest.append(copy(b, b, xs[i]))
    to_far = {}
    for i in order:
        pushes[i].wait_recv()
        a = tk.at[3 - RING[i], mine]
        to_far[i] = copy(a, a, far)
        done.append(copy(a, a, core))
    cot_far.wait_recv()
    done.append(copy(cot_out.at[other], cot_out.at[other], core))
    own_far.wait_recv()
    done.append(copy(tk.at[3, other], tk.at[3, other], core))
    for i in order:
        to_far[i].wait_recv()
        a = tk.at[3 - RING[i], other]
        done.append(copy(a, a, core))
    for i in order:
        pushes[i].wait_send()
        to_far[i].wait_send()
    cot_far.wait_send()
    own_far.wait_send()
    for c in rest + done:
        c.wait()


def gather_all(pay, tile, clip, cot, tok):
    return comm_call(
        gather_kernel,
        [
            jax.ShapeDtypeStruct((2, 4, 4, 2, 16, 768), BF),
            jax.ShapeDtypeStruct((2, 4, 2, 16, 768), BF),
            jax.ShapeDtypeStruct((2, 4, 2, 16, 768), BF),
            jax.ShapeDtypeStruct((2, 2, 256), jnp.int32),
            jax.ShapeDtypeStruct((4, 128, 768), BF),
            jax.ShapeDtypeStruct((7, 4, 128, 768), BF),
        ],
        [
            pltpu.VMEM((2, 16, 2304), BF),
            pltpu.VMEM((16, 128), BF),
            pltpu.VMEM((2, 2, 16, 2304), BF),
            DMA((56,)),
            DMA((56,)),
        ],
        0,
        "gather_first",
        (pay, tile, clip, cot, tok),
    )


def piece_copies(copy, f0, f1, p0, p1, p, x, y, xs, ys):
    made = []
    for i in range(3):
        made.append(copy(f0.at[p], p0.at[y], ys[i]))
        made.append(copy(f1.at[p], p1.at[:, x], xs[i]))
    p0[y] = f0[p]
    p1[:, x] = f1[p]
    return made


PIECE = [jax.ShapeDtypeStruct((4, 4, 2, 16, 768), BF)] * 2


def exchange_rows(copy, a, out, k, t, core, far):
    mine, other = k * 2 + t, k * 2 + 1 - t
    c_far = copy(a, out.at[mine], far)
    c_core = copy(a, out.at[mine], core)
    out[mine] = a[...]

    def finish():
        c_far.wait_recv()
        c_pass = copy(out.at[other], out.at[other], core)
        c_far.wait_send()
        c_core.wait()
        c_pass.wait()

    return finish


def exchange_sums(copy, p, out, got_core, mid, got_far, k, t, core, far):
    n = p.shape[0]
    to_core = [copy(p.at[i, pl.ds((1 - k) * 2, 2)], got_core.at[i], core) for i in range(n)]

    def finish():
        to_far = []
        for i in range(n):
            to_core[i].wait()
            mid[i] = (p[i, k * 2 + 1 - t].astype(F32) + got_core[i, 1 - t].astype(F32)).astype(BF)
            to_far.append(copy(mid.at[i], got_far.at[i], far))
        for i in range(n):
            part = p[i, k * 2 + t].astype(F32) + got_core[i, t].astype(F32)
            to_far[i].wait()
            out[i] = part + got_far[i].astype(F32)

    return finish


def sum_scratch(n):
    return [
        pltpu.VMEM((n, 2, 128, 768), BF),
        pltpu.VMEM((n, 128, 768), BF),
        pltpu.VMEM((n, 128, 768), BF),
    ]


def sum_attn_kernel(p, f0, f1, out, p0, p1, got_core, mid, got_far, send, recv):
    (z, y, x, k, t), xs, ys, core, far, low, ring = spots()
    copy = Copies(send, recv)
    greet(xs + ys + [core, far])
    finish = exchange_sums(copy, p, out, got_core, mid, got_far, k, t, core, far)
    made = piece_copies(copy, f0, f1, p0, p1, 0, x, y, xs, ys)
    finish()
    for c in made:
        c.wait()


def sum_attn(p, f0, f1):
    return comm_call(
        sum_attn_kernel,
        [jax.ShapeDtypeStruct((1, 128, 768), F32)] + PIECE,
        sum_scratch(1) + [DMA((8,)), DMA((8,))],
        1,
        "sum_attn",
        (p, f0, f1),
    )


def rows_two_kernel(a, f0, f1, out, p0, p1, send, recv):
    (z, y, x, k, t), xs, ys, core, far, low, ring = spots()
    copy = Copies(send, recv)
    greet(xs + ys + [core, far])
    finish = exchange_rows(copy, a, out, k, t, core, far)
    made = piece_copies(copy, f0, f1, p0, p1, 1, x, y, xs, ys)
    finish()
    for c in made:
        c.wait()


def rows_two(a, f0, f1):
    return comm_call(
        rows_two_kernel,
        [jax.ShapeDtypeStruct((4, 128, 768), BF)] + PIECE,
        [DMA((9,)), DMA((9,))],
        2,
        "rows_two",
        (a, f0, f1),
    )


def spread_first(copy, g0, g1, b0, b1, x, y, xs, ys):
    over_y, over_x = [], []
    for i in range(3):
        over_y.append(copy(g0.at[:, (y + i + 1) % 4], b0.at[i], ys[i]))
        over_x.append(copy(g1.at[:, :, (x + i + 1) % 4], b1.at[i], xs[i]))
    return over_y, over_x


def add_first(g0, g1, b0, b1, s0, s1, x, y, over_y, over_x):
    for c in over_y:
        c.wait()

    @pl.loop(0, 8)
    def _(n):
        zz, m = n // 4, n % 4
        v = g0[zz, y, m].astype(F32)
        for i in range(3):
            v = v + b0[i, zz, m].astype(F32)
        s0[zz, m] = v.astype(BF)

    for c in over_x:
        c.wait()

    @pl.loop(0, 8)
    def _(n):
        zz, m = n // 4, n % 4
        v = g1[zz, m, x].astype(F32)
        for i in range(3):
            v = v + b1[i, zz, m].astype(F32)
        s1[zz, m] = v.astype(BF)


def spread_second(copy, s0, s1, a0, a1, x, y, xs, ys):
    over_x, over_y = [], []
    for i in range(3):
        over_x.append(copy(s0.at[:, (x + i + 1) % 4], a0.at[i], xs[i]))
        over_y.append(copy(s1.at[:, (y + i + 1) % 4], a1.at[i], ys[i]))
    return over_x, over_y


def add_second(s0, s1, a0, a1, u0, u1, x, y, over_x, over_y):
    for c in over_x + over_y:
        c.wait()
    for zz in range(2):
        v = s0[zz, x].astype(F32)
        v1 = s1[zz, y].astype(F32)
        for i in range(3):
            v = v + a0[i, zz].astype(F32)
            v1 = v1 + a1[i, zz].astype(F32)
        u0[zz] = v.astype(BF)
        u1[zz] = v1.astype(BF)


def sum_mlp_kernel(p, g0, g1, out, s0, s1, got_core, mid, got_far, b0, b1, send, recv):
    (z, y, x, k, t), xs, ys, core, far, low, ring = spots()
    copy = Copies(send, recv)
    greet(xs + ys + [core, far])
    finish = exchange_sums(copy, p, out, got_core, mid, got_far, k, t, core, far)
    over = spread_first(copy, g0, g1, b0, b1, x, y, xs, ys)
    finish()
    add_first(g0, g1, b0, b1, s0, s1, x, y, *over)


def sum_mlp(p, g0, g1):
    return comm_call(
        sum_mlp_kernel,
        [jax.ShapeDtypeStruct((2, 128, 768), F32)]
        + [jax.ShapeDtypeStruct((2, 4, 2, 16, 768), BF)] * 2,
        sum_scratch(2)
        + [pltpu.VMEM((3, 2, 4, 2, 16, 768), BF)] * 2
        + [DMA((10,)), DMA((10,))],
        3,
        "sum_mlp",
        (p, g0, g1),
    )


def rows_back_kernel(a, s0, s1, out, u0, u1, a0, a1, send, recv):
    (z, y, x, k, t), xs, ys, core, far, low, ring = spots()
    copy = Copies(send, recv)
    greet(xs + ys + [core, far])
    finish = exchange_rows(copy, a, out, k, t, core, far)
    over = spread_second(copy, s0, s1, a0, a1, x, y, xs, ys)
    finish()
    add_second(s0, s1, a0, a1, u0, u1, x, y, *over)


def rows_back(a, s0, s1):
    return comm_call(
        rows_back_kernel,
        [jax.ShapeDtypeStruct((4, 128, 768), BF)]
        + [jax.ShapeDtypeStruct((2, 2, 16, 768), BF)] * 2,
        [pltpu.VMEM((3, 2, 2, 16, 768), BF)] * 2 + [DMA((9,)), DMA((9,))],
        4,
        "rows_back",
        (a, s0, s1),
    )


def return_kernel(
    d, g, u0, u1, out, own, tile_out,
    got_core, e_send, got_far, r_send, got_ring,
    b0, b1, s0, s1, a0, a1, v0, v1, z_in0, z_in1, z_in2, z_in3, res, tile, send, recv,
):
    (z, y, x, k, t), xs, ys, core, far, low, ring = spots()
    copy = Copies(send, recv)
    greet(xs + ys + [core, far, low] + ring)
    order = [3 + r for r in RING] + [3]
    to_core = {j: copy(d.at[j, pl.ds((1 - k) * 2, 2)], got_core.at[j], core) for j in order}
    g0, g1 = g.at[:, :, :, :, :, pl.ds(0, 384)], g.at[:, :, :, :, :, pl.ds(384, 384)]
    over = spread_first(copy, g0, g1, b0, b1, x, y, xs, ys)
    fc_z = [copy(u0.at[1 - z], z_in0, low), copy(u1.at[1 - z], z_in1, low)]
    to_far = {}
    for j in order:
        to_core[j].wait()
        e_send[j] = (d[j, k * 2 + 1 - t].astype(F32) + got_core[j, 1 - t].astype(F32)).astype(BF)
        to_far[j] = copy(e_send.at[j], got_far.at[j], far)
    add_first(g0, g1, b0, b1, s0, s1, x, y, *over)
    over = spread_second(copy, s0, s1, a0, a1, x, y, xs, ys)
    home = []

    def send_home(i):
        j = order[i]
        to_far[j].wait()
        v = d[j, k * 2 + t].astype(F32) + got_core[j, t].astype(F32) + got_far[j].astype(F32)
        r_send[i] = v.astype(BF)
        home.append(copy(r_send.at[i], got_ring.at[i], ring[i]))

    for i in range(3):
        send_home(i)
    add_second(s0, s1, a0, a1, v0, v1, x, y, *over)
    attn_z = [copy(v0.at[1 - z], z_in2, low), copy(v1.at[1 - z], z_in3, low)]
    for i in range(3, 6):
        send_home(i)
    for c in fc_z + attn_z:
        c.wait()
    res[:, :, 0:384] = v0[z].astype(F32) + z_in2[...].astype(F32)
    res[:, :, 384:768] = v1[z].astype(F32) + z_in3[...].astype(F32)
    res[:, :, 768:1536] = u0[z].astype(F32) + z_in0[...].astype(F32)
    res[:, :, 1536:2304] = u1[z].astype(F32) + z_in1[...].astype(F32)
    swap = copy(res.at[1 - k], own.at[k], core)
    own[k] = res[k]
    to_far[3].wait()
    total = d[3, k * 2 + t].astype(F32) + got_core[3, t].astype(F32) + got_far[3].astype(F32)
    swap.wait()
    tile[...] = own[0, :, 0:128] + own[1, :, 0:128]
    c_tile = copy(tile, tile_out, far)
    for i in range(6):
        home[i].wait()
        total = total + got_ring[i].astype(F32)
    out[...] = total
    c_tile.wait()


def return_all(d, g, u0, u1):
    return comm_call(
        return_kernel,
        [
            jax.ShapeDtypeStruct((128, 768), F32),
            jax.ShapeDtypeStruct((2, 16, 2304), F32),
            jax.ShapeDtypeStruct((16, 128), F32),
        ],
        [
            pltpu.VMEM((7, 2, 128, 768), BF),
            pltpu.VMEM((7, 128, 768), BF),
            pltpu.VMEM((7, 128, 768), BF),
            pltpu.VMEM((6, 128, 768), BF),
            pltpu.VMEM((6, 128, 768), BF),
        ]
        + [pltpu.VMEM((3, 2, 4, 2, 16, 384), BF)] * 2
        + [pltpu.VMEM((2, 4, 2, 16, 384), BF)] * 2
        + [pltpu.VMEM((3, 2, 2, 16, 384), BF)] * 2
        + [pltpu.VMEM((2, 2, 16, 384), BF)] * 2
        + [pltpu.VMEM((2, 16, 768), BF)] * 2
        + [pltpu.VMEM((2, 16, 384), BF)] * 2
        + [pltpu.VMEM((2, 16, 2304), F32), pltpu.VMEM((16, 128), F32), DMA((38,)), DMA((38,))],
        5,
        "return_all",
        (d, g, u0, u1),
    )


def allowed_pairs(lim, clip, qb, j):
    cols = pl.ds(qb * 256, 256)
    pos = lim[4] + j * 256 + lax.broadcasted_iota(jnp.int32, (256, 256), 0)
    return (pos >= clip[0:1, cols]) & (pos < clip[1:2, cols])


def attend_kernel(lim, clip, q, kv, of, lse):
    lane = lax.broadcasted_iota(jnp.int32, (256, 128), 1)
    for qb in range(2):
        rows = slice(qb * 256, qb * 256 + 256)

        def step(j, carry):
            ok = allowed_pairs(lim, clip, qb, j)
            new = []
            for h in range(3):
                m, l, acc = carry[h]
                cols = slice(h * 128, h * 128 + 128)
                keys = kv[j, :, cols]
                s = lax.dot_general(keys, q[rows, cols], NT, preferred_element_type=F32)
                s = jnp.where(ok, s, NEGATIVE)
                top = jnp.maximum(m, jnp.max(s, axis=0, keepdims=True))
                p = jnp.exp(s - top)
                fade = jnp.exp(m - top)
                l = l * fade + jnp.sum(p, axis=0, keepdims=True)
                acc = acc * fade + lax.dot_general(
                    keys, p.astype(BF), TN, preferred_element_type=F32
                )
                new.append((top, l, acc))
            return tuple(new)

        start = tuple(
            (
                jnp.full((1, 256), NEGATIVE, F32),
                jnp.zeros((1, 256), F32),
                jnp.zeros((128, 256), F32),
            )
            for _ in range(3)
        )
        final = lax.fori_loop(lim[2 * qb], lim[2 * qb + 1], step, start)
        for h in range(3):
            m, l, acc = final[h]
            o = (acc / l).T
            of[rows, h * 128 : h * 128 + 128] = jnp.where(lane >= 64, o, 0.0)
            lse[h : h + 1, rows] = m + jnp.log(l)


def attend(lim, clip, q, kv):
    return pl.pallas_call(
        attend_kernel,
        out_shape=[
            jax.ShapeDtypeStruct((512, 384), F32),
            jax.ShapeDtypeStruct((3, 512), F32),
        ],
        in_specs=[SM, VM, VM, VM],
        out_specs=[VM, VM],
        compiler_params=pltpu.CompilerParams(vmem_limit_bytes=LIMIT),
        name="attend",
    )(lim, clip, q, kv)


def attend_back_kernel(lim, clip, q, dox, kv, lse, delta, dz, total):
    lane = lax.broadcasted_iota(jnp.int32, (256, 128), 1)

    @pl.loop(0, 14)
    def _(j):
        total[j] = jnp.zeros((256, 384), F32)

    for qb in range(2):
        rows = slice(qb * 256, qb * 256 + 256)

        def step(j, carry):
            ok = allowed_pairs(lim, clip, qb, j)
            new = []
            for h in range(3):
                cols = slice(h * 128, h * 128 + 128)
                keys = kv[j, :, cols]
                qh, dh = q[rows, cols], dox[rows, cols]
                s = lax.dot_general(keys, qh, NT, preferred_element_type=F32)
                p = jnp.exp(jnp.where(ok, s, NEGATIVE) - lse[h : h + 1, rows])
                dp = lax.dot_general(keys, dh, NT, preferred_element_type=F32)
                ds = (p * (dp - delta[h : h + 1, rows])).astype(BF)
                new.append(
                    carry[h] + lax.dot_general(keys, ds, TN, preferred_element_type=F32)
                )
                total[j, :, cols] += jnp.dot(
                    ds, qh, preferred_element_type=F32
                ) + jnp.dot(p.astype(BF), dh, preferred_element_type=F32)
            return tuple(new)

        start = tuple(jnp.zeros((128, 256), F32) for _ in range(3))
        final = lax.fori_loop(lim[2 * qb], lim[2 * qb + 1], step, start)
        for h in range(3):
            back = jnp.where(lane < 64, SCORE_SCALE * final[h].T, 0.0)
            dz[6 + qb, :, 384 + h * 128 : 512 + h * 128] = back.astype(BF)

    @pl.loop(0, 14)
    def _(j):
        dz[j, :, 0:384] = total[j].astype(BF)

    for j in range(14):
        if j not in (6, 7):
            dz[j, :, 384:768] = jnp.zeros((256, 384), BF)


def attend_back(lim, clip, q, dox, kv, lse, delta):
    return pl.pallas_call(
        attend_back_kernel,
        out_shape=jax.ShapeDtypeStruct((14, 256, 768), BF),
        in_specs=[SM] + [VM] * 6,
        out_specs=VM,
        scratch_shapes=[pltpu.VMEM((14, 256, 384), F32)],
        compiler_params=pltpu.CompilerParams(vmem_limit_bytes=LIMIT),
        name="attend_back",
    )(lim, clip, q, dox, kv, lse, delta)


def matmul(left, right):
    return jnp.dot(left, right, preferred_element_type=F32)


def matmul_nt(left, right):
    return lax.dot_general(left, right, NT, preferred_element_type=F32)


def matmul_tn(left, right):
    return lax.dot_general(left, right, TN, preferred_element_type=F32)


def normalize(hidden, gain, offset):
    average = jnp.mean(hidden, axis=-1, keepdims=True)
    centred = hidden - average
    spread = jnp.mean(centred * centred, axis=-1, keepdims=True)
    scale = lax.rsqrt(spread + EPS)
    unit = centred * scale
    return unit * gain + offset, unit, scale


def normalize_back(grad_out, unit, scale, gain):
    grad_unit = grad_out * gain
    first = jnp.mean(grad_unit, axis=-1, keepdims=True)
    second = jnp.mean(grad_unit * unit, axis=-1, keepdims=True)
    return scale * (grad_unit - first - unit * second)


def body(
    tokens,
    clip_bounds,
    attn_in,
    qv_bias,
    out_proj,
    fc_in,
    fc_bias,
    fc_out,
    ln_gain,
    row_bias,
    cotangent,
):
    dp = lax.axis_index("dp")
    c, k, t = dp // 2, dp % 2, lax.axis_index("tensor")
    feature = lax.broadcasted_iota(jnp.int32, (384, 512), 0)
    place = lax.broadcasted_iota(jnp.int32, (384, 512), 1)
    select = (place == (feature // 12) * 16 + feature % 12).astype(BF)

    def narrow(padded):
        return matmul(select, padded.reshape(512, -1)).astype(BF)

    def widen(rows):
        halves = [matmul_tn(select, rows[i : i + 384]).astype(BF) for i in (0, 384)]
        return jnp.stack(halves).reshape(2, 4, 4, 2, 16, -1)

    parts = attn_in[0].reshape(3, 12, 6, 64)
    proj = out_proj[0].T.reshape(12, 6, 64)
    kv_w = jnp.stack([parts[1], parts[2]], axis=2).reshape(12, 2, 384)
    qo_w = jnp.stack([parts[0], proj], axis=2).reshape(12, 2, 384)
    up_w = fc_in[0].reshape(12, 2, 768)
    down_w = fc_out[0].T.reshape(12, 2, 768)
    pay = jnp.concatenate([kv_w, qo_w, up_w, down_w], axis=-1).transpose(1, 0, 2)
    small = jnp.concatenate(
        [ln_gain.reshape(-1), row_bias.reshape(-1), qv_bias.reshape(-1), fc_bias.reshape(-1)]
    )
    small = jnp.pad(small, (0, 56))
    extra = jnp.pad(small.reshape(1, 1, 128), ((0, 0), (0, 3), (0, 2176)))
    extra = jnp.concatenate([extra, extra], axis=0)
    pay = jnp.concatenate([pay, extra], axis=1)
    tile = jnp.pad(small.reshape(1, 128), ((13, 2), (0, 0)))
    w, f0, f1, clip, cot, near_tokens = gather_all(pay, tile, clip_bounds, cotangent, tokens)
    clip = clip.transpose(1, 0, 2).reshape(2, 512)
    w_attn = jnp.concatenate([narrow(w[0]), narrow(w[1])])
    w_kv, w_qo = w_attn[:, 0:384], w_attn[:, 384:768]

    smalls = w.reshape(64, 16, 768)[:, 12:14, 0:128].astype(F32)
    pair = jnp.where(t == 0, smalls, smalls[:, ::-1])
    gains = pair[:, :, 0:12].reshape(64, 2, 2, 6).transpose(2, 0, 1, 3).reshape(2, 768)
    biases = pair[:, :, 12:36].reshape(64, 2, 4, 6).transpose(2, 0, 1, 3).reshape(4, 768)
    heads = smalls[:, 0, 36:48].reshape(64, 2, 2, 3)
    heads = jnp.where(k == 0, heads[:, :, 0], heads[:, :, 1]).transpose(1, 2, 0)
    blank = jnp.zeros((3, 64), F32)
    qo_bias = jnp.concatenate([heads[0], blank], axis=1).reshape(384)
    kv_bias = jnp.concatenate([blank, heads[1]], axis=1).reshape(384)
    up_bias = smalls[:, 0, 48:72].reshape(64, 2, 3, 4)
    up_bias = jnp.where(k == 0, up_bias[:, 0], up_bias[:, 1]).transpose(1, 0, 2).reshape(768)
    low_lanes = (jnp.arange(384, dtype=jnp.int32) % 128) < 64

    hidden = tokens.astype(F32)
    near_one, near_unit, _ = normalize(
        near_tokens.reshape(3584, 768).astype(F32), gains[0], biases[0]
    )
    near_one, near_unit = near_one.astype(BF), near_unit.astype(BF)
    near = (matmul(near_one, w_kv) + kv_bias).astype(BF).reshape(14, 256, 384)
    query = (matmul(near_one[1536:2048], w_qo) + qo_bias).astype(BF)
    query = jnp.where(low_lanes, query * BF(SCORE_SCALE), BF(0))
    base = (c - 3) * 512
    lim = jnp.stack(
        [
            (clip[0, 0] - base) // 256,
            (clip[1, 255] - base + 255) // 256,
            (clip[0, 256] - base) // 256,
            (clip[1, 511] - base + 255) // 256,
            base,
        ]
    ).astype(jnp.int32)
    mixed, lse = attend(lim, clip, query, near)
    mixed_low = mixed.astype(BF)
    attn = matmul_nt(mixed_low, w_qo).astype(BF)
    attn, up_a, down_a = sum_attn(attn.reshape(1, 4, 128, 768), f0, f1)
    hidden_one = hidden + attn[0] + biases[1]
    normed_two, unit_two, scale_two = normalize(hidden_one, gains[1], biases[2])
    full_two, up_b, down_b = rows_two(normed_two.astype(BF), f0, f1)
    full_two = full_two.reshape(512, 768)
    w_up = jnp.concatenate([narrow(up_a), narrow(up_b)])
    w_down = jnp.concatenate([narrow(down_a), narrow(down_b)])
    inner = matmul(full_two, w_up) + up_bias
    gelu = lambda v: jax.nn.gelu(v, approximate=False)
    active = gelu(inner).astype(BF)
    mlp = matmul_nt(active, w_down).astype(BF)
    full_mlp = cot.reshape(512, 768)
    grad_active = matmul(full_mlp, w_down)
    _, gelu_back = jax.vjp(gelu, inner)
    grad_inner = gelu_back(grad_active)[0].astype(BF)
    back_two = matmul_nt(grad_inner, w_up).astype(BF)
    grad_up = widen(matmul_tn(full_two, grad_inner).astype(BF))
    grad_down = widen(matmul_tn(full_mlp, active).astype(BF))
    pair_sum, s0, s1 = sum_mlp(
        jnp.stack([mlp, back_two]).reshape(2, 4, 128, 768), grad_up, grad_down
    )
    output = (hidden_one + pair_sum[0] + biases[3]).astype(BF)
    grad_normed_two = pair_sum[1]
    grad_hidden_one = cotangent.astype(F32) + normalize_back(
        grad_normed_two, unit_two, scale_two, gains[1]
    )
    grad_attn = grad_hidden_one.astype(BF)
    full_attn, u0, u1 = rows_back(grad_attn, s0, s1)
    full_attn = full_attn.reshape(512, 768)
    grad_mixed = jnp.where(low_lanes, 0.0, matmul(full_attn, w_qo)).astype(BF)
    delta = (grad_mixed.astype(F32) * mixed).reshape(512, 3, 128).sum(axis=-1).T
    grad_near = attend_back(lim, clip, query, grad_mixed, near, lse, delta).reshape(3584, 768)
    near_back = matmul_nt(grad_near, w_attn).astype(BF).reshape(7, 4, 128, 768)
    near_sum = jnp.sum(grad_near.astype(F32), axis=0)
    unit_grad = matmul_tn(near_unit, grad_near)
    grad_w = unit_grad * gains[0][:, None] + biases[0][:, None] * near_sum[None, :]
    grad_w_out = matmul_tn(full_attn, mixed_low)
    w_full = w_attn.astype(F32)

    sums = jnp.stack(
        [
            jnp.sum(unit_grad * w_full, axis=1),
            jnp.sum(grad_normed_two * unit_two, axis=0),
            jnp.sum(w_full * near_sum[None, :], axis=1),
            jnp.sum(grad_attn.astype(F32), axis=0),
            jnp.sum(grad_normed_two, axis=0),
            jnp.sum(cotangent.astype(F32), axis=0),
        ]
    )
    sums = sums.reshape(6, 64, 12).transpose(1, 0, 2).reshape(64, 72)
    q_sum = near_sum[384:768].reshape(3, 128)[:, :64]
    v_sum = near_sum[0:384].reshape(3, 128)[:, 64:]
    qv_sum = jnp.concatenate([q_sum, v_sum], axis=0).T
    up_sum = jnp.sum(grad_inner.astype(F32), axis=0)
    up_sum = up_sum.reshape(3, 64, 4).transpose(1, 0, 2).reshape(64, 12)
    smalls = jnp.concatenate([sums, qv_sum, up_sum], axis=1)
    smalls = jnp.pad(smalls.reshape(64, 1, 90), ((0, 0), (12, 3), (0, 678)))
    grad_w = jnp.concatenate([grad_w[:, 0:384], grad_w[:, 384:768] + grad_w_out], axis=1)
    grad_w = widen(grad_w.astype(BF)) + smalls.astype(BF).reshape(2, 4, 4, 2, 16, 768)
    back_one, own, far = return_all(near_back, grad_w, u0, u1)
    _, unit_one, scale_one = normalize(hidden, gains[0], biases[0])
    grad_tokens = grad_hidden_one + normalize_back(back_one, unit_one, scale_one, gains[0])
    vec = own[0, 12, 0:128] + own[1, 12, 0:128] + far[12]
    vec = vec[0:72].reshape(6, 2, 6)
    vec = jnp.where(t == 0, vec[:, 0], vec[:, 1])
    grad_gain, grad_row = vec[0:2].reshape(1, 2, 6), vec[2:6].reshape(1, 4, 6)
    grad_qv = own[:, 12, 72:78].reshape(2, 2, 3).transpose(1, 0, 2).reshape(1, 2, 6, 1)
    grad_up_bias = own[:, 12, 78:90].reshape(1, 6, 4)
    main = own[:, 0:12].transpose(1, 0, 2)
    g_kv = main[:, :, 0:384].reshape(12, 6, 2, 64)
    g_qo = main[:, :, 384:768].reshape(12, 6, 2, 64)
    grad_in = jnp.stack(
        [
            g_qo[:, :, 0].reshape(12, 384),
            g_kv[:, :, 0].reshape(12, 384),
            g_kv[:, :, 1].reshape(12, 384),
        ]
    )[None]
    grad_out = g_qo[:, :, 1].reshape(12, 384).T[None]
    grad_fc_in = main[:, :, 768:1536].reshape(1, 12, 1536)
    grad_fc_out = main[:, :, 1536:2304].reshape(12, 1536).T[None]
    return (
        output,
        grad_tokens,
        grad_in,
        grad_qv,
        grad_out,
        grad_fc_in,
        grad_up_bias,
        grad_fc_out,
        grad_gain,
        grad_row,
    )


def solution(mesh):
    return jax.shard_map(
        body,
        mesh=mesh,
        in_specs=(
            P(("dp", "tensor"), None),
            P(None, "dp"),
            P(None, None, "dp", "tensor"),
            P(None, None, "tensor", "dp"),
            P(None, "tensor", "dp"),
            P(None, "dp", "tensor"),
            P(None, "tensor", "dp"),
            P(None, "tensor", "dp"),
            P(None, None, ("dp", "tensor")),
            P(None, None, ("dp", "tensor")),
            P(("dp", "tensor"), None),
        ),
        out_specs=(
            P(("dp", "tensor"), None),
            P(("dp", "tensor"), None),
            P(None, None, "dp", "tensor"),
            P(None, None, "tensor", "dp"),
            P(None, "tensor", "dp"),
            P(None, "dp", "tensor"),
            P(None, "tensor", "dp"),
            P(None, "tensor", "dp"),
            P(None, None, ("dp", "tensor")),
            P(None, None, ("dp", "tensor")),
        ),
        check_vma=False,
    )
```

time: 450 us -> 385 us (0.86); the launches traced: 448 us -> 378 us
  Pallas kernels: 328 us -> 247 us
  other arithmetic: 24.7 us -> 35.6 us
    pallas_call x10 -> x6, Pallas kernels: 290 us -> 208 us  [comm_call(): pl.pallas_call(kernel, out_shape=out_shape, in_specs=[VM] * len(args), ou...]
    dot_general x8 -> x4, matrix products: 20.3 us -> 10.7 us  [matmul_nt(): return lax.dot_general(left, right, NT, preferred_element_type=F32)]
    dot_general x5 -> x10, matrix products: 9.84 us -> 18.1 us  [matmul_tn(): return lax.dot_general(left, right, TN, preferred_element_type=F32)]
    concatenate x1 -> x0, local copies, waits for them, and re-layouts: 6.79 us -> none  [body(): jnp.concatenate([(matmul_tn(full_one, grad_kv) + smalls).astype(BF), (mat...]
    convert_element_type x3 -> x4, other arithmetic: 1.69 us -> 6.34 us  [the longest x2 5.51 us: body(): near_one, near_unit = (near_one.astype(BF), near_unit.astype(BF))]
    dot_general x9 -> x11, matrix products: 27.2 us -> 29.3 us  [matmul(): return jnp.dot(left, right, preferred_element_type=F32)]
where the time goes in v2:
time: 385 us; the launch traced here: 378 us
  Pallas kernels  247 us (64%)
  matrix products  58.1 us (15%)
  other arithmetic  35.6 us (9%)
  local copies, waits for them, and re-layouts  32.2 us (8%)
  between operations  4.77 us (1%)
    pallas_call x6, Pallas kernels, comm_call(): pl.pallas_call(kernel, out_shape=out_shape, in_specs=[VM] * len(args), ou...  208 us
    dot_general x11, matrix products, matmul(): return jnp.dot(left, right, preferred_element_type=F32)  29.3 us
    pallas_call x1, Pallas kernels, attend_back(): pl.pallas_call(attend_back_kernel, out_shape=jax.ShapeDtypeStruct((14, 25...  21.1 us
    pallas_call x1, Pallas kernels, attend(): pl.pallas_call(attend_kernel, out_shape=[jax.ShapeDtypeStruct((512, 384),...  18.2 us
    dot_general x10, matrix products, matmul_tn(): return lax.dot_general(left, right, TN, preferred_element_type=F32)  18.1 us
    dot_general x4, matrix products, matmul_nt(): return lax.dot_general(left, right, NT, preferred_element_type=F32)  10.7 us

profile of v2, /device:TPU:1, one launch (start us, length us, event | category | flops | bytes accessed | tf_op | source)
XLA Modules:
  0.0 378.1 jit_solution(11345528384772424130)
XLA Ops:
  3.4 1.0 convert_reduce_fusion.2
  13.0 70.7 %gather_first.1 = (bf16[2,4,4,2,16,768]{5,4,3,2,1,0:T(8,128)(2,1)}, bf16[2,4,2,16,768]{4,3,2,1,0:T(8,128)(2,1)}, bf16[2,4,2,16,768]{4,3,2,1,0:T(8,128)(2,1)}, s3...) custom-call(bf16[2,16,2304]{2,1,0:T(8,128)(2,1)} %maximum_maximum_fusion.pay, ...), custom_call_target="tpu_custom_call" | custom-call | tf_op jit(solution)/shard_map/gather_first/pallas_call | solution.py:51
  83.7 1.3 fusion.79
  88.3 3.5 convert_reduce_fusion.1
  92.5 1.8 multiply_reduce_fusion
  102.7 1.8 convolution_convert_fusion.16
  104.7 1.0 convolution_convert_fusion.17
  105.8 2.0 fusion.3
  107.8 3.5 multiply_convert_fusion
  111.3 1.3 fusion.17.q
  112.6 4.5 %fusion.4 = bf16[3584,384]{1,0:T(8,128)(2,1)} fusion(bf16[3584,768]{1,0:T(8,128)(2,1)S(1)} %fusion.3, f32[384]{0:T(512)S(1)} %copy-done.34, bf16[384,768]{1,0:T(8,128)(2,1)S(1)} %convolution_convert_fusion.17, bf16[384,768]{1,0:T(8,128)(2,1)S(1)} %convolution_convert_fusion.16), kind=kOutput, calls=%fused_computation.11 | convolution fusion | flops 2117861376 | bytes 9438720 | tf_op jit(solution)/shard_map/dot_general | solution.py:581
  117.1 18.2 %attend.1 = (f32[512,384]{1,0:T(8,128)}, f32[3,512]{1,0:T(4,128)}) custom-call(s32[5]{0:T(128)} %stack.91.lim, s32[2,512]{1,0:T(2,128)} %bitcast.203, bf16[512,384]{1,0:T(8,128)(2,1)} %fusion.17.q, bf16[14,256,384]{2,1,0:T(8,128)(2,1)} %bitcast.171), custom_call_target="tpu_custom_call" | custom-call | tf_op jit(solution)/shard_map/attend/pallas_call | solution.py:511
  135.3 2.7 convolution_convert_fusion.11
  138.1 22.8 %sum_attn.1 = (f32[1,128,768]{2,1,0:T(8,128)}, bf16[4,4,2,16,768]{4,3,2,1,0:T(8,128)(2,1)}, bf16[4,4,2,16,768]{4,3,2,1,0:T(8,128)(2,1)}) custom-call(bf16[1,4,128,768]{3,2,1,0:T(8,128)(2,1)} %bitcast.177, bf16[2,4,2,16,768]{4,3,2,1,0:T(8,128)(2,1)} %get-tuple-element.37.f0, bf16[2,4,2,16,768]{4,3,2,1,0:T(8,128)(2,1)} %get-tuple-element.38.f1), custom_call_target="tpu_custom_call" | custom-call | tf_op jit(solution)/shard_map/sum_attn/pallas_call | solution.py:51
  160.9 1.2 fusion.71
  162.1 2.2 convolution_convert_fusion.15
  165.4 1.0 convolution_convert_fusion.13
  166.4 14.1 %rows_two.1 = (bf16[4,128,768]{2,1,0:T(8,128)(2,1)}, bf16[4,4,2,16,768]{4,3,2,1,0:T(8,128)(2,1)}, bf16[4,4,2,16,768]{4,3,2,1,0:T(8,128)(2,1)}) custom-call(bf16[128,768]{1,0:T(8,128)(2,1)} %add_convert_fusion.1.a, bf16[2,4,2,16,768]{4,3,2,1,0:T(8,128)(2,1)} %get-tuple-element.37.f0, bf16[2,4,2,16,768]{4,3,2,1,0:T(8,128)(2,1)} %get-tuple-element.38.f1), custom_call_target="tpu_custom_call" | custom-call | tf_op jit(solution)/shard_map/rows_two/pallas_call | solution.py:51
  180.5 2.2 convolution_convert_fusion.14
  182.7 1.0 convolution_convert_fusion.12
  183.9 10.6 %multiply_convert_fusion.1 = (bf16[512,768]{1,0:T(8,128)(2,1)S(1)}, f32[512,768]{1,0:T(8,128)S(1)}, f32[512,768]{1,0:T(8,128)S(1)}) fusion(f32[768]{0:T(1024)S(1)} %copy-done.25, bf16[512,768]{1,0:T(8,128)(2,1)S(1)} %bitcast.217, bf16[384,768]{1,0:T(8,128)(2,1)S(1)} %convolution_convert_fusion.14, bf16[384,768]{1,0:T(8,128)(2,1)S(1)} %convolution_convert_fusion.15), kind=kOutput, calls=%fused_computation.24 | convolution fusion | flops 632291328 | bytes 5901312 | tf_op jit(solution)/shard_map/dot_general | solution.py:581
  194.5 1.2 fusion.80
  196.5 1.9 convolution_convert_fusion.1
  199.2 1.3 pad_maximum_fusion.p
  200.8 2.2 convolution_convert_fusion.2
  203.0 0.9 convolution_convert_fusion.9
  204.9 1.3 pad_maximum_fusion.1.g0
  206.6 0.9 convolution_convert_fusion.7
  207.6 1.0 convolution_convert_fusion.8
  208.5 1.3 pad_maximum_fusion.2.g1
  209.9 25.1 %sum_mlp.1 = (f32[2,128,768]{2,1,0:T(8,128)}, bf16[2,4,2,16,768]{4,3,2,1,0:T(8,128)(2,1)}, bf16[2,4,2,16,768]{4,3,2,1,0:T(8,128)(2,1)}) custom-call(bf16[2,4,128,768]{3,2,1,0:T(8,128)(2,1)} %pad_maximum_fusion.p, bf16[2,4,4,2,16,768]{5,4,3,2,1,0:T(8,128)(2,1)} %pad_maximum_fusion.1.g0, bf16[2,4,4,2,16,768]{5,4,3,2,1,0:T(8,128)(2,1)} %pad_maximum_fusion.2.g1), custom_call_target="tpu_custom_call" | custom-call | tf_op jit(solution)/shard_map/sum_mlp/pallas_call | solution.py:51
  235.1 1.1 slice_reduce_fusion
  236.4 2.0 fusion.40
  238.4 1.1 fusion.69
  240.1 12.7 %rows_back.1 = (bf16[4,128,768]{2,1,0:T(8,128)(2,1)}, bf16[2,2,16,768]{3,2,1,0:T(8,128)(2,1)}, bf16[2,2,16,768]{3,2,1,0:T(8,128)(2,1)}) custom-call(bf16[128,768]{1,0:T(8,128)(2,1)} %get-tuple-element.98.a, bf16[2,4,2,16,768]{4,3,2,1,0:T(8,128)(2,1)} %get-tuple-element.47.s0, bf16[2,4,2,16,768]{4,3,2,1,0:T(8,128)(2,1)} %get-tuple-element.48.s1), custom_call_target="tpu_custom_call" | custom-call | tf_op jit(solution)/shard_map/rows_back/pallas_call | solution.py:51
  252.8 2.6 convert_multiply_fusion.2
  256.3 21.1 %attend_back.1 = bf16[14,256,768]{2,1,0:T(8,128)(2,1)} custom-call(s32[5]{0:T(128)} %stack.91.lim, s32[2,512]{1,0:T(2,128)} %bitcast.204, bf16[512,384]{1,0:T(8,128)(2,1)} %fusion.17.q, bf16[512,384]{1,0:T(8,128)(2,1)} %get-tuple-element.133.dox, bf16[14,256,384]{2,1,0:T(8,128)(2,1)} %bitcast.172, f32[3,512]{1,0:T(4,128)} %get-tuple-element.50.lse, ...), custom_call_target="tpu_custom_call" | custom-call | tf_op jit(solution)/shard_map/attend_back/pallas_call | solution.py:569
  277.4 3.5 convert_reduce_fusion
  281.6 7.7 %fusion.6 = (bf16[768]{0:T(1024)(128)(2,1)S(1)}, bf16[768]{0:T(1024)(128)(2,1)S(1)}, f32[768,768]{1,0:T(8,128)S(1)}) fusion(f32[768]{0:T(1024)S(1)} %convert_reduce_fusion, bf16[384,768]{1,0:T(8,128)(2,1)S(1)} %convolution_convert_fusion.16, bf16[384,768]{1,0:T(8,128)(2,1)S(1)} %copy-done.7, f32[768]{0:T(1024)S(1)} %copy-done.20, f32[768]{0:T(1024)S(1)} %copy-done.15, ...), kind=kOutput, calls=%fused_computation.16 | convolution fusion | flops 4234344960 | bytes 14561280 | tf_op jit(solution)/shard_map/dot_general | solution.py:589
  289.3 6.3 %convolution_convert_fusion = bf16[3584,768]{1,0:T(8,128)(2,1)} fusion(bf16[3584,768]{1,0:T(8,128)(2,1)S(1)} %bitcast.170, bf16[384,768]{1,0:T(8,128)(2,1)S(1)} %convolution_convert_fusion.16, bf16[384,768]{1,0:T(8,128)(2,1)S(1)} %copy-done.7), kind=kOutput, calls=%fused_computation.9 | convolution fusion | flops 4232970240 | bytes 12189696 | tf_op jit(solution)/shard_map/dot_general | solution.py:585
  297.1 1.3 slice.406
  298.5 0.9 convolution_convert_fusion.5
  299.5 0.9 convolution_convert_fusion.6
  300.6 1.3 maximum_add_fusion.g
  301.9 62.7 %return_all.1 = (f32[128,768]{1,0:T(8,128)}, f32[2,16,2304]{2,1,0:T(8,128)}, f32[16,128]{1,0:T(8,128)}) custom-call(bf16[7,4,128,768]{3,2,1,0:T(8,128)(2,1)} %bitcast.175, bf16[2,4,4,2,16,768]{5,4,3,2,1,0:T(8,128)(2,1)} %maximum_add_fusion.g, bf16[2,2,16,768]{3,2,1,0:T(8,128)(2,1)} %get-tuple-element.51.u0, bf16[2,2,16,768]{3,2,1,0:T(8,128)(2,1)} %get-tuple-element.52.u1), custom_call_target="tpu_custom_call" | custom-call | tf_op jit(solution)/shard_map/return_all/pallas_call | solution.py:51
  366.9 1.0 slice_bitcast_fusion
  368.6 1.2 multiply_reduce_fusion.3
  369.8 1.9 fusion.37
  (244 shorter events, 38.2 us)
Async XLA Ops:
  88.3 4.2 %copy-start = (bf16[7,4,128,768]{3,2,1,0:T(8,128)(2,1)S(1)}, bf16[7,4,128,768]{3,2,1,0:T(8,128)(2,1)}, u32[]{:S(2)}) copy-start(bf16[7,4,128,768]{3,2,1,0:T(8,128)(2,1)} %get-tuple-element.34) | copy-start | bytes 16515076
  92.5 3.0 copy-start.8
  92.5 13.1 %slice-start = ((s8[5505024]{0:T(1024)(128)(4,1)}), s8[1310720]{0:T(1024)(128)(4,1)S(1)}, s32[]{:S(2)}) async-start(s8[5505024]{0:T(1024)(128)(4,1)} %bitcast.167), calls=%async_computation | async-start | bytes 2621440
  94.3 1.2 copy-start.12
  102.6 3.1 slice-start.1
  102.7 1.9 copy-start.26
  102.7 1.9 copy-start.28
  102.7 1.9 copy-start.30
  102.7 1.9 copy-start.32
  102.7 1.9 copy-start.41
  102.7 1.9 copy-start.43
  104.6 1.1 copy-start.14
  104.6 1.1 copy-start.17
  104.6 1.1 copy-start.18
  104.6 1.1 copy-start.19
  105.7 29.6 %copy-start.6 = (bf16[384,768]{1,0:T(8,128)(2,1)}, bf16[384,768]{1,0:T(8,128)(2,1)S(1)}, u32[]{:S(2)}) copy-start(bf16[384,768]{1,0:T(8,128)(2,1)S(1)} %convolution_convert_fusion.17) | copy-start | bytes 1769476
  105.7 2.0 copy-start.13
  107.8 3.5 copy-start.35
  107.8 3.5 copy-start.36
  111.3 1.3 copy-start.34
  135.3 25.6 %copy-start.3 = (bf16[128,768]{1,0:T(8,128)(2,1)S(1)}, bf16[128,768]{1,0:T(8,128)(2,1)}, u32[]{:S(2)}) copy-start(bf16[128,768]{1,0:T(8,128)(2,1)} %tok.1) | copy-start | bytes 589828
  135.3 25.6 %copy-start.23 = (f32[768]{0:T(1024)S(1)}, f32[768]{0:T(1024)}, u32[]{:S(2)}) copy-start(f32[768]{0:T(1024)} %add.239) | copy-start | bytes 9220
  135.3 25.6 %copy-start.24 = (f32[128]{0:T(128)S(1)}, f32[128]{0:T(128)}, u32[]{:S(2)}) copy-start(f32[128]{0:T(128)} %broadcast_multiply_fusion.3) | copy-start | bytes 1540
  162.1 2.4 copy-start.16
  162.1 2.4 copy-start.22
  162.1 3.3 copy-start.39
  180.5 2.2 copy-start.40
  182.7 1.1 copy-start.38
  183.9 10.6 %copy-start.37 = (bf16[4,128,768]{2,1,0:T(8,128)(2,1)S(1)}, bf16[4,128,768]{2,1,0:T(8,128)(2,1)}, u32[]{:S(2)}) copy-start(bf16[4,128,768]{2,1,0:T(8,128)(2,1)} %get-tuple-element.45) | copy-start | bytes 2359300
  195.7 2.7 copy-start.46
  204.9 1.7 copy-start.45
  209.9 26.5 %copy-start.21 = (f32[768]{0:T(1024)S(1)}, f32[768]{0:T(1024)}, u32[]{:S(2)}) copy-start(f32[768]{0:T(1024)} %add.250) | copy-start | bytes 9220
  235.0 3.3 copy-start.5
  235.1 3.3 copy-start.11
  238.4 14.4 %copy-start.2 = (f32[512,384]{1,0:T(8,128)S(1)}, f32[512,384]{1,0:T(8,128)}, u32[]{:S(2)}) copy-start(f32[512,384]{1,0:T(8,128)} %get-tuple-element.36) | copy-start | bytes 2359300
  256.3 24.7 %copy-start.7 = (bf16[384,768]{1,0:T(8,128)(2,1)S(1)}, bf16[384,768]{1,0:T(8,128)(2,1)}, u32[]{:S(2)}) copy-start(bf16[384,768]{1,0:T(8,128)(2,1)} %copy-done.6) | copy-start | bytes 1769476
  256.3 24.7 %copy-start.20 = (f32[768]{0:T(1024)S(1)}, f32[768]{0:T(1024)}, u32[]{:S(2)}) copy-start(f32[768]{0:T(1024)} %add.226) | copy-start | bytes 9220
  277.4 4.2 %copy-start.1 = (bf16[14,256,768]{2,1,0:T(8,128)(2,1)S(1)}, bf16[14,256,768]{2,1,0:T(8,128)(2,1)}, u32[]{:S(2)}) copy-start(bf16[14,256,768]{2,1,0:T(8,128)(2,1)} %attend_back.1) | copy-start | bytes 16515076
  277.4 4.2 %copy-start.15 = (f32[768]{0:T(1024)S(1)}, f32[768]{0:T(1024)}, u32[]{:S(2)}) copy-start(f32[768]{0:T(1024)} %mul.216) | copy-start | bytes 9220
  289.3 6.4 %copy-start.10 = (f32[768,768]{1,0:T(8,128)}, f32[768,768]{1,0:T(8,128)S(1)}, u32[]{:S(2)}) copy-start(f32[768,768]{1,0:T(8,128)S(1)} %get-tuple-element.104) | copy-start | bytes 7077892
  289.3 6.4 %copy-start.4 = (bf16[4,128,768]{2,1,0:T(8,128)(2,1)S(1)}, bf16[4,128,768]{2,1,0:T(8,128)(2,1)}, u32[]{:S(2)}) copy-start(bf16[4,128,768]{2,1,0:T(8,128)(2,1)} %get-tuple-element.49) | copy-start | bytes 2359300
  295.7 2.8 copy-start.27
  295.7 2.8 copy-start.29
  295.7 2.8 copy-start.31
  295.7 2.8 copy-start.33
  295.7 2.8 copy-start.42
  295.7 2.8 copy-start.44
  301.9 67.9 %copy-start.9 = (f32[128,768]{1,0:T(8,128)S(1)}, f32[128,768]{1,0:T(8,128)}, u32[]{:S(2)}) copy-start(f32[128,768]{1,0:T(8,128)} %get-tuple-element.99) | copy-start | bytes 1179652
  (1 other events, 1.0 us)

commit v3 on v2

--- a/solution.py
+++ b/solution.py
@@ -1,5 +1,6 @@
 import jax
 import jax.numpy as jnp
+import numpy as np
 from jax import lax
 import jax.experimental.pallas as pl
 import jax.experimental.pallas.tpu as pltpu
@@ -87,24 +88,18 @@
 
 
 def gather_kernel(
-    pay, tile, clip, cot, tok, w, f0, f1, clip_out, cot_out, tk, pay_s, tile_in, ws, send, recv
+    pay, tile, clip, tok, w, f0, f1, clip_out, tk, pay_s, tile_in, ws, send, recv
 ):
     (z, y, x, k, t), xs, ys, core, far, low, ring = spots()
     copy = Copies(send, recv)
     mine, other = k * 2 + t, k * 2 + 1 - t
     greet(xs + ys + [core, far, low] + ring)
     c_tile = copy(tile, tile_in, far)
-    cot_far = copy(cot, cot_out.at[mine], far)
     own_far = copy(tok, tk.at[3, mine], far)
     order = (4, 5, 2, 3, 0, 1)
     pushes = {i: copy(tok, tk.at[3 - RING[i], mine], ring[i]) for i in order}
-    done = [
-        copy(cot, cot_out.at[mine], core),
-        copy(tok, tk.at[3, mine], core),
-        copy(clip, clip_out.at[k], core),
-    ]
+    done = [copy(tok, tk.at[3, mine], core), copy(clip, clip_out.at[k], core)]
     clip_out[k] = clip[...]
-    cot_out[mine] = cot[...]
     tk[3, mine] = tok[...]
     c_tile.wait()
     pay_s[...] = pay[...]
@@ -113,7 +108,18 @@
     swap = copy(pay_s.at[1 - k], ws.at[z, k], core)
     ws[z, k] = pay_s[k]
     swap.wait()
-    copy(ws.at[z], ws.at[z], low).wait()
+    c_low = copy(ws.at[z], ws.at[z], low)
+    to_far = {}
+
+    def pass_on(i):
+        pushes[i].wait_recv()
+        a = tk.at[3 - RING[i], mine]
+        to_far[i] = copy(a, a, far)
+        done.append(copy(a, a, core))
+
+    pass_on(4)
+    pass_on(5)
+    c_low.wait()
     w[:, y, x] = ws[:, :, :, 0:768]
     f0[:, x] = ws[:, :, :, 768:1536]
     f1[:, y] = ws[:, :, :, 1536:2304]
@@ -122,25 +128,21 @@
     for i in range(3):
         phase.append(copy(ws.at[:, :, :, h0], w.at[:, y, x, :, :, h0], xs[i]))
         phase.append(copy(ws.at[:, :, :, h1], w.at[:, y, x, :, :, h1], ys[i]))
-    rest = []
-    for i in range(3):
-        rest.append(copy(ws.at[:, :, :, pl.ds(768, 768)], f0.at[:, x], xs[i]))
-        rest.append(copy(ws.at[:, :, :, pl.ds(1536, 768)], f1.at[:, y], ys[i]))
+    pass_on(2)
+    pass_on(3)
     for c in phase:
         c.wait()
+    rest = []
     for i in range(3):
         a = w.at[:, y, :, :, :, h0]
         rest.append(copy(a, a, ys[i]))
         b = w.at[:, :, x, :, :, h1]
         rest.append(copy(b, b, xs[i]))
-    to_far = {}
-    for i in order:
-        pushes[i].wait_recv()
-        a = tk.at[3 - RING[i], mine]
-        to_far[i] = copy(a, a, far)
-        done.append(copy(a, a, core))
-    cot_far.wait_recv()
-    done.append(copy(cot_out.at[other], cot_out.at[other], core))
+    pass_on(0)
+    pass_on(1)
+    for i in range(3):
+        rest.append(copy(ws.at[:, :, :, pl.ds(768, 768)], f0.at[:, x], xs[i]))
+        rest.append(copy(ws.at[:, :, :, pl.ds(1536, 768)], f1.at[:, y], ys[i]))
     own_far.wait_recv()
     done.append(copy(tk.at[3, other], tk.at[3, other], core))
     for i in order:
@@ -150,13 +152,12 @@
     for i in order:
         pushes[i].wait_send()
         to_far[i].wait_send()
-    cot_far.wait_send()
     own_far.wait_send()
     for c in rest + done:
         c.wait()
 
 
-def gather_all(pay, tile, clip, cot, tok):
+def gather_all(pay, tile, clip, tok):
     return comm_call(
         gather_kernel,
         [
@@ -164,19 +165,18 @@
             jax.ShapeDtypeStruct((2, 4, 2, 16, 768), BF),
             jax.ShapeDtypeStruct((2, 4, 2, 16, 768), BF),
             jax.ShapeDtypeStruct((2, 2, 256), jnp.int32),
-            jax.ShapeDtypeStruct((4, 128, 768), BF),
             jax.ShapeDtypeStruct((7, 4, 128, 768), BF),
         ],
         [
             pltpu.VMEM((2, 16, 2304), BF),
             pltpu.VMEM((16, 128), BF),
             pltpu.VMEM((2, 2, 16, 2304), BF),
-            DMA((56,)),
-            DMA((56,)),
+            DMA((53,)),
+            DMA((53,)),
         ],
         0,
         "gather_first",
-        (pay, tile, clip, cot, tok),
+        (pay, tile, clip, tok),
     )
 
 
@@ -257,25 +257,27 @@
     )
 
 
-def rows_two_kernel(a, f0, f1, out, p0, p1, send, recv):
+def rows_two_kernel(a, cot, f0, f1, out, cot_out, p0, p1, send, recv):
     (z, y, x, k, t), xs, ys, core, far, low, ring = spots()
     copy = Copies(send, recv)
     greet(xs + ys + [core, far])
     finish = exchange_rows(copy, a, out, k, t, core, far)
     made = piece_copies(copy, f0, f1, p0, p1, 1, x, y, xs, ys)
+    finish_cot = exchange_rows(copy, cot, cot_out, k, t, core, far)
     finish()
+    finish_cot()
     for c in made:
         c.wait()
 
 
-def rows_two(a, f0, f1):
+def rows_two(a, cot, f0, f1):
     return comm_call(
         rows_two_kernel,
-        [jax.ShapeDtypeStruct((4, 128, 768), BF)] + PIECE,
-        [DMA((9,)), DMA((9,))],
+        [jax.ShapeDtypeStruct((4, 128, 768), BF)] * 2 + PIECE,
+        [DMA((12,)), DMA((12,))],
         2,
         "rows_two",
-        (a, f0, f1),
+        (a, cot, f0, f1),
     )
 
 
@@ -461,13 +463,94 @@
     )
 
 
+def layout_tables():
+    d = np.arange(768)
+    n64 = np.arange(64)[:, None]
+    own = (d // 12 == n64).astype(np.float32)
+    lane = d % 128
+    high = d < 384
+    column = np.where(high, lane - 64, lane)
+    heads = ((column == n64) & (column >= 0) & (column < 64)).astype(np.float32)
+    hidden = ((d % 256) // 4 == n64).astype(np.float32)
+    spread = np.stack([own, heads, hidden])
+    spot = 64 * ((d % 12) // 6) + d % 6
+    head = (d % 384) // 128
+    rows = [spot + 6 * p for p in range(6)]
+    rows.append(np.where(high, 6, 0) + head)
+    rows.append(12 + (d // 256) * 4 + d % 4)
+    step = np.zeros((8, 768), np.int32)
+    step[6], step[7] = 3, 12
+    back = [12 * p + d % 12 for p in range(6)]
+    back.append(72 + np.where(high, 3, 0) + head)
+    back.append(78 + (d // 256) * 4 + d % 4)
+    select = np.arange(512)[None, :] == (np.arange(384) // 12 * 16 + np.arange(384) % 12)[:, None]
+    row12 = np.arange(512)[:, None] == np.arange(32)[None, :] * 16 + 12
+    return (
+        spread,
+        np.stack(rows).astype(np.int32),
+        step,
+        np.stack(back).astype(np.int32),
+        select.astype(np.float32),
+        row12.astype(np.float32),
+    )
+
+
+SPREAD, FETCH, FETCH_STEP, PUT, SELECT, ROW12 = layout_tables()
+
+
+def matmul(left, right):
+    return jnp.dot(left, right, preferred_element_type=F32)
+
+
+def matmul_nt(left, right):
+    return lax.dot_general(left, right, NT, preferred_element_type=F32)
+
+
+def matmul_tn(left, right):
+    return lax.dot_general(left, right, TN, preferred_element_type=F32)
+
+
 def allowed_pairs(lim, clip, qb, j):
     cols = pl.ds(qb * 256, 256)
     pos = lim[4] + j * 256 + lax.broadcasted_iota(jnp.int32, (256, 256), 0)
     return (pos >= clip[0:1, cols]) & (pos < clip[1:2, cols])
 
 
-def attend_kernel(lim, clip, q, kv, of, lse):
+def front_kernel(
+    lim, clip, w, row12, row13, spread, fetch, select, tk,
+    vecs, w_attn, unit, kv, q, of, lse, attn,
+):
+    line = lax.broadcasted_iota(jnp.int32, (128, 768), 0)
+    wide = matmul_tn(row12[...], spread[0])
+    for p in range(6):
+        hit = line == fetch[p : p + 1, :]
+        vecs[p : p + 1, :] = jnp.sum(jnp.where(hit, wide, 0.0), axis=0, keepdims=True)
+    for p in (6, 7):
+        wide = matmul_tn(row13[...], spread[p - 5])
+        hit = line == fetch[p : p + 1, :]
+        vecs[p : p + 1, :] = jnp.sum(jnp.where(hit, wide, 0.0), axis=0, keepdims=True)
+    for z in range(2):
+        w_attn[z * 384 : z * 384 + 384, :] = matmul(select[...], w[z]).astype(BF)
+
+    def norm_rows(j):
+        v = tk[j].astype(F32)
+        centred = v - jnp.mean(v, axis=-1, keepdims=True)
+        spread_out = jnp.mean(centred * centred, axis=-1, keepdims=True)
+        u = centred * lax.rsqrt(spread_out + EPS)
+        return u, (u * vecs[0:1, :] + vecs[2:3, :]).astype(BF)
+
+    @pl.loop(lim[0], lim[3])
+    def _(j):
+        u, a = norm_rows(j)
+        unit[j] = u.astype(BF)
+        kv[j] = (matmul(a, w_attn[:, 0:384]) + vecs[6:7, 0:384]).astype(BF)
+
+    low = (lax.broadcasted_iota(jnp.int32, (256, 384), 1) & 127) < 64
+    for qb in range(2):
+        _, a = norm_rows(6 + qb)
+        v = (matmul(a, w_attn[:, 384:768]) + vecs[6:7, 384:768]).astype(BF).astype(F32)
+        q[qb * 256 : qb * 256 + 256, :] = jnp.where(low, v * SCORE_SCALE, 0.0).astype(BF)
+
     lane = lax.broadcasted_iota(jnp.int32, (256, 128), 1)
     for qb in range(2):
         rows = slice(qb * 256, qb * 256 + 256)
@@ -479,15 +562,12 @@
                 m, l, acc = carry[h]
                 cols = slice(h * 128, h * 128 + 128)
                 keys = kv[j, :, cols]
-                s = lax.dot_general(keys, q[rows, cols], NT, preferred_element_type=F32)
-                s = jnp.where(ok, s, NEGATIVE)
+                s = jnp.where(ok, matmul_nt(keys, q[rows, cols]), NEGATIVE)
                 top = jnp.maximum(m, jnp.max(s, axis=0, keepdims=True))
                 p = jnp.exp(s - top)
                 fade = jnp.exp(m - top)
                 l = l * fade + jnp.sum(p, axis=0, keepdims=True)
-                acc = acc * fade + lax.dot_general(
-                    keys, p.astype(BF), TN, preferred_element_type=F32
-                )
+                acc = acc * fade + matmul_tn(keys, p.astype(BF))
                 new.append((top, l, acc))
             return tuple(new)
 
@@ -505,28 +585,103 @@
             o = (acc / l).T
             of[rows, h * 128 : h * 128 + 128] = jnp.where(lane >= 64, o, 0.0)
             lse[h : h + 1, rows] = m + jnp.log(l)
-
-
-def attend(lim, clip, q, kv):
+        attn[rows, :] = matmul_nt(of[rows, :].astype(BF), w_attn[:, 384:768]).astype(BF)
+
+
+def front(lim, clip, w, row12, row13, spread, fetch, select, tk):
     return pl.pallas_call(
-        attend_kernel,
+        front_kernel,
         out_shape=[
+            jax.ShapeDtypeStruct((8, 768), F32),
+            jax.ShapeDtypeStruct((768, 768), BF),
+            jax.ShapeDtypeStruct((14, 256, 768), BF),
+            jax.ShapeDtypeStruct((14, 256, 384), BF),
+            jax.ShapeDtypeStruct((512, 384), BF),
             jax.ShapeDtypeStruct((512, 384), F32),
             jax.ShapeDtypeStruct((3, 512), F32),
+            jax.ShapeDtypeStruct((512, 768), BF),
         ],
-        in_specs=[SM, VM, VM, VM],
-        out_specs=[VM, VM],
+        in_specs=[SM] + [VM] * 8,
+        out_specs=[VM] * 8,
         compiler_params=pltpu.CompilerParams(vmem_limit_bytes=LIMIT),
-        name="attend",
-    )(lim, clip, q, kv)
-
-
-def attend_back_kernel(lim, clip, q, dox, kv, lse, delta, dz, total):
+        name="front",
+    )(lim, clip, w, row12, row13, spread, fetch, select, tk)
+
+
+def middle_kernel(
+    b, cot, up_a, up_b, down_a, down_b, vecs, select,
+    pair, g0, g1, up_sum, w_up, w_down, active, inner_back,
+):
+    for i, (up, down) in enumerate(((up_a, down_a), (up_b, down_b))):
+        rows = slice(i * 384, i * 384 + 384)
+        w_up[rows, :] = matmul(select[...], up[...]).astype(BF)
+        w_down[rows, :] = matmul(select[...], down[...]).astype(BF)
+    up_sum[...] = jnp.zeros((1, 768), F32)
+
+    @pl.loop(0, 4)
+    def _(r):
+        rows = pl.ds(pl.multiple_of(r * 128, 128), 128)
+        u = matmul(b[rows, :], w_up[...]) + vecs[7:8, :]
+        phi = 0.5 + 0.5 * lax.erf(u * 0.7071067811865476)
+        gl = (u * phi).astype(BF)
+        active[rows, :] = gl
+        pair[0, rows, :] = matmul_nt(gl, w_down[...]).astype(BF)
+        slope = phi + u * jnp.exp(-0.5 * u * u) * 0.3989422804014327
+        du = (matmul(cot[rows, :], w_down[...]) * slope).astype(BF)
+        inner_back[rows, :] = du
+        up_sum[...] += jnp.sum(du.astype(F32), axis=0, keepdims=True)
+        pair[1, rows, :] = matmul_nt(du, w_up[...]).astype(BF)
+
+    for i in range(2):
+        cols = slice(i * 384, i * 384 + 384)
+        g = matmul_tn(b[:, cols], inner_back[...]).astype(BF)
+        g0[i] = matmul_tn(select[...], g).astype(BF)
+        g = matmul_tn(cot[:, cols], active[...]).astype(BF)
+        g1[i] = matmul_tn(select[...], g).astype(BF)
+
+
+def middle(b, cot, up_a, up_b, down_a, down_b, vecs, select):
+    return pl.pallas_call(
+        middle_kernel,
+        out_shape=[
+            jax.ShapeDtypeStruct((2, 512, 768), BF),
+            jax.ShapeDtypeStruct((2, 512, 768), BF),
+            jax.ShapeDtypeStruct((2, 512, 768), BF),
+            jax.ShapeDtypeStruct((1, 768), F32),
+        ],
+        in_specs=[VM] * 8,
+        out_specs=[VM] * 4,
+        scratch_shapes=[
+            pltpu.VMEM((768, 768), BF),
+            pltpu.VMEM((768, 768), BF),
+            pltpu.VMEM((512, 768), BF),
+            pltpu.VMEM((512, 768), BF),
+        ],
+        compiler_params=pltpu.CompilerParams(vmem_limit_bytes=LIMIT),
+        name="middle",
+    )(b, cot, up_a, up_b, down_a, down_b, vecs, select)
+
+
+def back_kernel(
+    lim, clip, q, dr, of, kv, lse, unit, w_attn, vecs, sums, up_sum, spread, put, select, row12,
+    d_out, grad, total, dox, delta, dq, ug,
+):
     lane = lax.broadcasted_iota(jnp.int32, (256, 128), 1)
+    high = (lax.broadcasted_iota(jnp.int32, (256, 384), 1) & 127) >= 64
 
     @pl.loop(0, 14)
     def _(j):
         total[j] = jnp.zeros((256, 384), F32)
+        d_out[j] = jnp.zeros((256, 768), BF)
+
+    for qb in range(2):
+        rows = slice(qb * 256, qb * 256 + 256)
+        g = jnp.where(high, matmul(dr[rows, :], w_attn[:, 384:768]), 0.0).astype(BF)
+        dox[rows, :] = g
+        prod = g.astype(F32) * of[rows, :]
+        for h in range(3):
+            part = prod[:, h * 128 : h * 128 + 128].T
+            delta[h : h + 1, rows] = jnp.sum(part, axis=0, keepdims=True)
 
     for qb in range(2):
         rows = slice(qb * 256, qb * 256 + 256)
@@ -538,55 +693,84 @@
                 cols = slice(h * 128, h * 128 + 128)
                 keys = kv[j, :, cols]
                 qh, dh = q[rows, cols], dox[rows, cols]
-                s = lax.dot_general(keys, qh, NT, preferred_element_type=F32)
-                p = jnp.exp(jnp.where(ok, s, NEGATIVE) - lse[h : h + 1, rows])
-                dp = lax.dot_general(keys, dh, NT, preferred_element_type=F32)
-                ds = (p * (dp - delta[h : h + 1, rows])).astype(BF)
-                new.append(
-                    carry[h] + lax.dot_general(keys, ds, TN, preferred_element_type=F32)
-                )
-                total[j, :, cols] += jnp.dot(
-                    ds, qh, preferred_element_type=F32
-                ) + jnp.dot(p.astype(BF), dh, preferred_element_type=F32)
+                s = jnp.where(ok, matmul_nt(keys, qh), NEGATIVE)
+                p = jnp.exp(s - lse[h : h + 1, rows])
+                ds = (p * (matmul_nt(keys, dh) - delta[h : h + 1, rows])).astype(BF)
+                new.append(carry[h] + matmul_tn(keys, ds))
+                total[j, :, cols] += matmul(ds, qh) + matmul(p.astype(BF), dh)
             return tuple(new)
 
         start = tuple(jnp.zeros((128, 256), F32) for _ in range(3))
         final = lax.fori_loop(lim[2 * qb], lim[2 * qb + 1], step, start)
         for h in range(3):
-            back = jnp.where(lane < 64, SCORE_SCALE * final[h].T, 0.0)
-            dz[6 + qb, :, 384 + h * 128 : 512 + h * 128] = back.astype(BF)
-
-    @pl.loop(0, 14)
-    def _(j):
-        dz[j, :, 0:384] = total[j].astype(BF)
-
-    for j in range(14):
-        if j not in (6, 7):
-            dz[j, :, 384:768] = jnp.zeros((256, 384), BF)
-
-
-def attend_back(lim, clip, q, dox, kv, lse, delta):
+            part = jnp.where(lane < 64, SCORE_SCALE * final[h].T, 0.0)
+            dq[rows, h * 128 : h * 128 + 128] = part.astype(BF)
+
+    ug[...] = jnp.zeros((768, 768), F32)
+
+    def chunk(j, kv_sum):
+        z = total[j].astype(BF)
+        d_out[j] = matmul_nt(z, w_attn[:, 0:384]).astype(BF)
+        ug[:, 0:384] += matmul_tn(unit[j], z)
+        return kv_sum + jnp.sum(z.astype(F32), axis=0, keepdims=True)
+
+    kv_sum = lax.fori_loop(lim[0], lim[3], chunk, jnp.zeros((1, 384), F32))
+    for qb in range(2):
+        rows = slice(qb * 256, qb * 256 + 256)
+        own = matmul_nt(total[6 + qb].astype(BF), w_attn[:, 0:384])
+        d_out[6 + qb] = (own + matmul_nt(dq[rows, :], w_attn[:, 384:768])).astype(BF)
+        ug[:, 384:768] += matmul_tn(unit[6 + qb], dq[rows, :])
+    q_sum = jnp.sum(dq[...].astype(F32), axis=0, keepdims=True)
+    z_sum = jnp.concatenate([kv_sum, q_sum], axis=1)
+
+    line = lax.broadcasted_iota(jnp.int32, (128, 768), 0)
+
+    def place(p, row):
+        return jnp.where(line == put[p : p + 1, :], row, 0.0)
+
+    columns = vecs[...].T
+    gain_col, offset_col = columns[:, 0:1], columns[:, 2:3]
+    w_full = w_attn[...].astype(F32)
+    gain_sum = jnp.sum(ug[...] * w_full, axis=1, keepdims=True)
+    offset_sum = jnp.sum(w_full * z_sum, axis=1, keepdims=True)
+    flip = lax.broadcasted_iota(jnp.int32, (768, 128), 1)
+    both = jnp.where(flip == 0, gain_sum, jnp.where(flip == 1, offset_sum, 0.0)).T
+    own = place(0, both[0:1, :]) + place(2, both[1:2, :])
+    for i, p in enumerate((1, 3, 4, 5)):
+        own = own + place(p, sums[i : i + 1, :])
+    small = matmul_nt(spread[0], own.astype(BF))
+    small += matmul_nt(spread[1], place(6, z_sum).astype(BF))
+    small += matmul_nt(spread[2], place(7, up_sum[...]).astype(BF))
+    small = small.astype(BF)
+
+    ug[...] = ug[...] * gain_col + offset_col * z_sum
+    ug[:, 384:768] += matmul_tn(dr[...], of[...].astype(BF))
+    for i in range(2):
+        g = matmul_tn(select[...], ug[i * 384 : i * 384 + 384, :].astype(BF))
+        grad[i] = g.astype(BF)
+        extra = matmul(row12[...], small[i * 32 : i * 32 + 32, :])
+        grad[i, :, 0:128] = (g[:, 0:128] + extra).astype(BF)
+
+
+def back(lim, *args):
     return pl.pallas_call(
-        attend_back_kernel,
-        out_shape=jax.ShapeDtypeStruct((14, 256, 768), BF),
-        in_specs=[SM] + [VM] * 6,
-        out_specs=VM,
-        scratch_shapes=[pltpu.VMEM((14, 256, 384), F32)],
+        back_kernel,
+        out_shape=[
+            jax.ShapeDtypeStruct((14, 256, 768), BF),
+            jax.ShapeDtypeStruct((2, 512, 768), BF),
+        ],
+        in_specs=[SM] + [VM] * len(args),
+        out_specs=[VM, VM],
+        scratch_shapes=[
+            pltpu.VMEM((14, 256, 384), F32),
+            pltpu.VMEM((512, 384), BF),
+            pltpu.VMEM((3, 512), F32),
+            pltpu.VMEM((512, 384), BF),
+            pltpu.VMEM((768, 768), F32),
+        ],
         compiler_params=pltpu.CompilerParams(vmem_limit_bytes=LIMIT),
-        name="attend_back",
-    )(lim, clip, q, dox, kv, lse, delta)
-
-
-def matmul(left, right):
-    return jnp.dot(left, right, preferred_element_type=F32)
-
-
-def matmul_nt(left, right):
-    return lax.dot_general(left, right, NT, preferred_element_type=F32)
-
-
-def matmul_tn(left, right):
-    return lax.dot_general(left, right, TN, preferred_element_type=F32)
+        name="back",
+    )(lim, *args)
 
 
 def normalize(hidden, gain, offset):
@@ -620,16 +804,9 @@
 ):
     dp = lax.axis_index("dp")
     c, k, t = dp // 2, dp % 2, lax.axis_index("tensor")
-    feature = lax.broadcasted_iota(jnp.int32, (384, 512), 0)
-    place = lax.broadcasted_iota(jnp.int32, (384, 512), 1)
-    select = (place == (feature // 12) * 16 + feature % 12).astype(BF)
-
-    def narrow(padded):
-        return matmul(select, padded.reshape(512, -1)).astype(BF)
-
-    def widen(rows):
-        halves = [matmul_tn(select, rows[i : i + 384]).astype(BF) for i in (0, 384)]
-        return jnp.stack(halves).reshape(2, 4, 4, 2, 16, -1)
+    spread, select, row12 = jnp.asarray(SPREAD, BF), jnp.asarray(SELECT, BF), jnp.asarray(ROW12, BF)
+    put = jnp.asarray(PUT)
+    fetch = jnp.asarray(FETCH) + k * jnp.asarray(FETCH_STEP)
 
     parts = attn_in[0].reshape(3, 12, 6, 64)
     proj = out_proj[0].T.reshape(12, 6, 64)
@@ -638,40 +815,22 @@
     up_w = fc_in[0].reshape(12, 2, 768)
     down_w = fc_out[0].T.reshape(12, 2, 768)
     pay = jnp.concatenate([kv_w, qo_w, up_w, down_w], axis=-1).transpose(1, 0, 2)
-    small = jnp.concatenate(
-        [ln_gain.reshape(-1), row_bias.reshape(-1), qv_bias.reshape(-1), fc_bias.reshape(-1)]
-    )
-    small = jnp.pad(small, (0, 56))
-    extra = jnp.pad(small.reshape(1, 1, 128), ((0, 0), (0, 3), (0, 2176)))
-    extra = jnp.concatenate([extra, extra], axis=0)
-    pay = jnp.concatenate([pay, extra], axis=1)
-    tile = jnp.pad(small.reshape(1, 128), ((13, 2), (0, 0)))
-    w, f0, f1, clip, cot, near_tokens = gather_all(pay, tile, clip_bounds, cotangent, tokens)
+    norms = jnp.concatenate([ln_gain.reshape(1, 12), row_bias.reshape(1, 24)], axis=1)
+    blank = jnp.zeros((1, 64), BF)
+    norms = jnp.pad(norms, ((0, 0), (0, 28)))
+    norms = jnp.where(
+        t == 0,
+        jnp.concatenate([norms, blank], axis=1),
+        jnp.concatenate([blank, norms], axis=1),
+    )
+    others = jnp.concatenate([qv_bias.reshape(1, 12), fc_bias.reshape(1, 24)], axis=1)
+    others = jnp.pad(others, ((0, 0), (0, 92)))
+    extra = jnp.pad(jnp.concatenate([norms, others]), ((0, 2), (0, 2176)))[None]
+    pay = jnp.concatenate([pay, jnp.concatenate([extra, extra])], axis=1)
+    tile = jnp.pad(norms, ((12, 3), (0, 0)))
+    w, f0, f1, clip, near_tokens = gather_all(pay, tile, clip_bounds, tokens)
     clip = clip.transpose(1, 0, 2).reshape(2, 512)
-    w_attn = jnp.concatenate([narrow(w[0]), narrow(w[1])])
-    w_kv, w_qo = w_attn[:, 0:384], w_attn[:, 384:768]
-
-    smalls = w.reshape(64, 16, 768)[:, 12:14, 0:128].astype(F32)
-    pair = jnp.where(t == 0, smalls, smalls[:, ::-1])
-    gains = pair[:, :, 0:12].reshape(64, 2, 2, 6).transpose(2, 0, 1, 3).reshape(2, 768)
-    biases = pair[:, :, 12:36].reshape(64, 2, 4, 6).transpose(2, 0, 1, 3).reshape(4, 768)
-    heads = smalls[:, 0, 36:48].reshape(64, 2, 2, 3)
-    heads = jnp.where(k == 0, heads[:, :, 0], heads[:, :, 1]).transpose(1, 2, 0)
-    blank = jnp.zeros((3, 64), F32)
-    qo_bias = jnp.concatenate([heads[0], blank], axis=1).reshape(384)
-    kv_bias = jnp.concatenate([blank, heads[1]], axis=1).reshape(384)
-    up_bias = smalls[:, 0, 48:72].reshape(64, 2, 3, 4)
-    up_bias = jnp.where(k == 0, up_bias[:, 0], up_bias[:, 1]).transpose(1, 0, 2).reshape(768)
-    low_lanes = (jnp.arange(384, dtype=jnp.int32) % 128) < 64
-
-    hidden = tokens.astype(F32)
-    near_one, near_unit, _ = normalize(
-        near_tokens.reshape(3584, 768).astype(F32), gains[0], biases[0]
-    )
-    near_one, near_unit = near_one.astype(BF), near_unit.astype(BF)
-    near = (matmul(near_one, w_kv) + kv_bias).astype(BF).reshape(14, 256, 384)
-    query = (matmul(near_one[1536:2048], w_qo) + qo_bias).astype(BF)
-    query = jnp.where(low_lanes, query * BF(SCORE_SCALE), BF(0))
+    rows = w.reshape(64, 16, 768)[:, 12:14, 0:128]
     base = (c - 3) * 512
     lim = jnp.stack(
         [
@@ -682,29 +841,36 @@
             base,
         ]
     ).astype(jnp.int32)
-    mixed, lse = attend(lim, clip, query, near)
-    mixed_low = mixed.astype(BF)
-    attn = matmul_nt(mixed_low, w_qo).astype(BF)
+    vecs, w_attn, unit, near, query, mixed, lse, attn = front(
+        lim,
+        clip,
+        w.reshape(2, 512, 768),
+        rows[:, 0],
+        rows[:, 1],
+        spread,
+        fetch,
+        select,
+        near_tokens.reshape(14, 256, 768),
+    )
+    gains, biases = vecs[0:2], vecs[2:6]
+    hidden = tokens.astype(F32)
     attn, up_a, down_a = sum_attn(attn.reshape(1, 4, 128, 768), f0, f1)
     hidden_one = hidden + attn[0] + biases[1]
     normed_two, unit_two, scale_two = normalize(hidden_one, gains[1], biases[2])
-    full_two, up_b, down_b = rows_two(normed_two.astype(BF), f0, f1)
-    full_two = full_two.reshape(512, 768)
-    w_up = jnp.concatenate([narrow(up_a), narrow(up_b)])
-    w_down = jnp.concatenate([narrow(down_a), narrow(down_b)])
-    inner = matmul(full_two, w_up) + up_bias
-    gelu = lambda v: jax.nn.gelu(v, approximate=False)
-    active = gelu(inner).astype(BF)
-    mlp = matmul_nt(active, w_down).astype(BF)
-    full_mlp = cot.reshape(512, 768)
-    grad_active = matmul(full_mlp, w_down)
-    _, gelu_back = jax.vjp(gelu, inner)
-    grad_inner = gelu_back(grad_active)[0].astype(BF)
-    back_two = matmul_nt(grad_inner, w_up).astype(BF)
-    grad_up = widen(matmul_tn(full_two, grad_inner).astype(BF))
-    grad_down = widen(matmul_tn(full_mlp, active).astype(BF))
+    full_two, cot, up_b, down_b = rows_two(normed_two.astype(BF), cotangent, f0, f1)
+    pair, grad_up, grad_down, up_sum = middle(
+        full_two.reshape(512, 768),
+        cot.reshape(512, 768),
+        up_a.reshape(512, 768),
+        up_b.reshape(512, 768),
+        down_a.reshape(512, 768),
+        down_b.reshape(512, 768),
+        vecs,
+        select,
+    )
+    shape = (2, 4, 4, 2, 16, 768)
     pair_sum, s0, s1 = sum_mlp(
-        jnp.stack([mlp, back_two]).reshape(2, 4, 128, 768), grad_up, grad_down
+        pair.reshape(2, 4, 128, 768), grad_up.reshape(shape), grad_down.reshape(shape)
     )
     output = (hidden_one + pair_sum[0] + biases[3]).astype(BF)
     grad_normed_two = pair_sum[1]
@@ -713,38 +879,35 @@
     )
     grad_attn = grad_hidden_one.astype(BF)
     full_attn, u0, u1 = rows_back(grad_attn, s0, s1)
-    full_attn = full_attn.reshape(512, 768)
-    grad_mixed = jnp.where(low_lanes, 0.0, matmul(full_attn, w_qo)).astype(BF)
-    delta = (grad_mixed.astype(F32) * mixed).reshape(512, 3, 128).sum(axis=-1).T
-    grad_near = attend_back(lim, clip, query, grad_mixed, near, lse, delta).reshape(3584, 768)
-    near_back = matmul_nt(grad_near, w_attn).astype(BF).reshape(7, 4, 128, 768)
-    near_sum = jnp.sum(grad_near.astype(F32), axis=0)
-    unit_grad = matmul_tn(near_unit, grad_near)
-    grad_w = unit_grad * gains[0][:, None] + biases[0][:, None] * near_sum[None, :]
-    grad_w_out = matmul_tn(full_attn, mixed_low)
-    w_full = w_attn.astype(F32)
-
     sums = jnp.stack(
         [
-            jnp.sum(unit_grad * w_full, axis=1),
             jnp.sum(grad_normed_two * unit_two, axis=0),
-            jnp.sum(w_full * near_sum[None, :], axis=1),
             jnp.sum(grad_attn.astype(F32), axis=0),
             jnp.sum(grad_normed_two, axis=0),
             jnp.sum(cotangent.astype(F32), axis=0),
         ]
     )
-    sums = sums.reshape(6, 64, 12).transpose(1, 0, 2).reshape(64, 72)
-    q_sum = near_sum[384:768].reshape(3, 128)[:, :64]
-    v_sum = near_sum[0:384].reshape(3, 128)[:, 64:]
-    qv_sum = jnp.concatenate([q_sum, v_sum], axis=0).T
-    up_sum = jnp.sum(grad_inner.astype(F32), axis=0)
-    up_sum = up_sum.reshape(3, 64, 4).transpose(1, 0, 2).reshape(64, 12)
-    smalls = jnp.concatenate([sums, qv_sum, up_sum], axis=1)
-    smalls = jnp.pad(smalls.reshape(64, 1, 90), ((0, 0), (12, 3), (0, 678)))
-    grad_w = jnp.concatenate([grad_w[:, 0:384], grad_w[:, 384:768] + grad_w_out], axis=1)
-    grad_w = widen(grad_w.astype(BF)) + smalls.astype(BF).reshape(2, 4, 4, 2, 16, 768)
-    back_one, own, far = return_all(near_back, grad_w, u0, u1)
+    near_back, grad_w = back(
+        lim,
+        clip,
+        query,
+        full_attn.reshape(512, 768),
+        mixed,
+        near,
+        lse,
+        unit,
+        w_attn,
+        vecs,
+        sums,
+        up_sum,
+        spread,
+        put,
+        select,
+        row12,
+    )
+    back_one, own, far = return_all(
+        near_back.reshape(7, 4, 128, 768), grad_w.reshape(shape), u0, u1
+    )
     _, unit_one, scale_one = normalize(hidden, gains[0], biases[0])
     grad_tokens = grad_hidden_one + normalize_back(back_one, unit_one, scale_one, gains[0])
     vec = own[0, 12, 0:128] + own[1, 12, 0:128] + far[12]

time: 385 us -> 312 us (0.81); the launches traced: 378 us -> 314 us
  matrix products: 58.1 us -> 0 us
  Pallas kernels: 247 us -> 275 us
  other arithmetic: 35.6 us -> 13.5 us
  local copies, waits for them, and re-layouts: 32.2 us -> 21.8 us
    dot_general x25 -> x0, matrix products: 58.1 us -> none  [the longest x11 29.3 us: matmul(): return jnp.dot(left, right, preferred_element_type=F32)]
    pallas_call x2 -> x3, Pallas kernels: 39.3 us -> 74.3 us  [the longest x1 31.1 us: back(): pl.pallas_call(back_kernel, out_shape=[jax.ShapeDtypeStruct((14, 256, 768...]
    pallas_call x6, Pallas kernels: 208 us -> 201 us  [comm_call(): pl.pallas_call(kernel, out_shape=out_shape, in_specs=[VM] * len(args), ou...]
    convert_element_type x4 -> x1, other arithmetic: 6.34 us -> 0.83 us  [body(): normed_two.astype(BF)]
    add x6 -> x0, local copies, waits for them, and re-layouts: 4.33 us -> none  [the longest x2 1.49 us: normalize(): return (unit * gain + offset, unit, scale)]
    reduce_sum x2 -> x0, other arithmetic: 4.21 us -> none  [the longest x1 3.54 us: body(): near_sum = jnp.sum(grad_near.astype(F32), axis=0)]
where the time goes in v3:
time: 312 us; the launch traced here: 314 us
  Pallas kernels  275 us (88%)
  local copies, waits for them, and re-layouts  21.8 us (7%)
  other arithmetic  13.5 us (4%)
  between operations  3.67 us (1%)
    pallas_call x6, Pallas kernels, comm_call(): pl.pallas_call(kernel, out_shape=out_shape, in_specs=[VM] * len(args), ou...  201 us
    pallas_call x1, Pallas kernels, back(): pl.pallas_call(back_kernel, out_shape=[jax.ShapeDtypeStruct((14, 256, 768...  31.1 us
    pallas_call x1, Pallas kernels, front(): pl.pallas_call(front_kernel, out_shape=[jax.ShapeDtypeStruct((8, 768), F3...  29.7 us
    pallas_call x1, Pallas kernels, middle(): pl.pallas_call(middle_kernel, out_shape=[jax.ShapeDtypeStruct((2, 512, 76...  13.5 us

profile of v3, /device:TPU:1, one launch (start us, length us, event | category | flops | bytes accessed | tf_op | source)
XLA Modules:
  0.0 313.9 jit_solution(3602580075258987361)
XLA Ops:
  0.7 0.7 reshape.174
  1.4 0.7 reshape.172
  2.1 0.8 reshape.173
  3.0 1.0 convert_reduce_fusion
  4.0 0.8 copy.40
  5.0 0.6 pad.21.tile
  5.6 1.4 multiply_add_fusion.fetch
  7.0 0.8 stack_reshape.4
  7.8 0.8 reshape_squeeze.13
  8.6 0.8 reshape.171
  9.5 0.8 fusion.28
  11.0 0.7 maximum_maximum_fusion.pay
  11.7 63.8 %gather_first.1 = (bf16[2,4,4,2,16,768]{5,4,3,2,1,0:T(8,128)(2,1)}, bf16[2,4,2,16,768]{4,3,2,1,0:T(8,128)(2,1)}, bf16[2,4,2,16,768]{4,3,2,1,0:T(8,128)(2,1)}, s3...) custom-call(bf16[2,16,2304]{2,1,0:T(8,128)(2,1)} %maximum_maximum_fusion.pay, bf16[16,128]{1,0:T(8,128)(2,1)} %pad.21.tile, ...), custom_call_target="tpu_custom_call" | custom-call | tf_op jit(solution)/shard_map/gather_first/pallas_call | solution.py:52
  75.4 1.3 fusion.29
  79.4 0.6 stack.49.lim
  80.0 1.0 fusion.25
  81.1 0.6 copy.59
  81.7 0.6 copy.60
  82.3 29.7 %front.1 = (f32[8,768]{1,0:T(8,128)}, bf16[768,768]{1,0:T(8,128)(2,1)}, bf16[14,256,768]{2,1,0:T(8,128)(2,1)}, bf16[14,256,384]{2,1,0:T(8,128)(2,1)}, bf16[512,3...) custom-call(s32[5]{0:T(128)} %stack.49.lim, s32[2,512]{1,0:T(2,128)} %bitcast.113, ...), custom_call_target="tpu_custom_call" | custom-call | tf_op jit(solution)/shard_map/front/pallas_call | solution.py:592
  112.0 1.0 slice_reduce_fusion.5
  112.9 14.9 %sum_attn.1 = (f32[1,128,768]{2,1,0:T(8,128)}, bf16[4,4,2,16,768]{4,3,2,1,0:T(8,128)(2,1)}, bf16[4,4,2,16,768]{4,3,2,1,0:T(8,128)(2,1)}) custom-call(bf16[1,4,128,768]{3,2,1,0:T(8,128)(2,1)} %bitcast.105, bf16[2,4,2,16,768]{4,3,2,1,0:T(8,128)(2,1)} %get-tuple-element.49.f0, bf16[2,4,2,16,768]{4,3,2,1,0:T(8,128)(2,1)} %get-tuple-element.50.f1), custom_call_target="tpu_custom_call" | custom-call | tf_op jit(solution)/shard_map/sum_attn/pallas_call | solution.py:52
  127.9 1.2 fusion.23
  129.3 0.8 add_convert_fusion.a
  130.1 17.2 %rows_two.1 = (bf16[4,128,768]{2,1,0:T(8,128)(2,1)}, bf16[4,128,768]{2,1,0:T(8,128)(2,1)}, bf16[4,4,2,16,768]{4,3,2,1,0:T(8,128)(2,1)}, bf16[4,4,2,16,768]{4,3,2,1,0:T(8,128)(2,1)}) custom-call(bf16[128,768]{1,0:T(8,128)(2,1)} %add_convert_fusion.a, bf16[128,768]{1,0:T(8,128)(2,1)} %cot.1, bf16[2,4,2,16,768]{4,3,2,1,0:T(8,128)(2,1)} %get-tuple-element.49.f0, ...), custom_call_target="tpu_custom_call" | custom-call | tf_op jit(solution)/shard_map/rows_two/pallas_call | solution.py:52
  147.3 13.5 %middle.1 = (bf16[2,512,768]{2,1,0:T(8,128)(2,1)}, bf16[2,512,768]{2,1,0:T(8,128)(2,1)}, bf16[2,512,768]{2,1,0:T(8,128)(2,1)}, f32[1,768]{1,0:T(1,128)}) custom-call(bf16[512,768]{1,0:T(8,128)(2,1)} %bitcast.101, bf16[512,768]{1,0:T(8,128)(2,1)} %bitcast.102, bf16[512,768]{1,0:T(8,128)(2,1)} %bitcast.98, bf16[512,768]{1,0:T(8,128)(2,1)} %bitcast.103, ...), custom_call_target="tpu_custom_call" | custom-call | tf_op jit(solution)/shard_map/middle/pallas_call | solution.py:644
  160.9 24.8 %sum_mlp.1 = (f32[2,128,768]{2,1,0:T(8,128)}, bf16[2,4,2,16,768]{4,3,2,1,0:T(8,128)(2,1)}, bf16[2,4,2,16,768]{4,3,2,1,0:T(8,128)(2,1)}) custom-call(bf16[2,4,128,768]{3,2,1,0:T(8,128)(2,1)} %bitcast.95, bf16[2,4,4,2,16,768]{5,4,3,2,1,0:T(8,128)(2,1)} %bitcast.96, bf16[2,4,4,2,16,768]{5,4,3,2,1,0:T(8,128)(2,1)} %bitcast.97), custom_call_target="tpu_custom_call" | custom-call | tf_op jit(solution)/shard_map/sum_mlp/pallas_call | solution.py:52
  185.7 1.1 slice_reduce_fusion
  186.8 1.2 fusion.10
  188.1 0.9 convert_reduce_fusion.2
  189.0 0.6 pad_maximum_fusion.2.sums
  189.6 12.3 %rows_back.1 = (bf16[4,128,768]{2,1,0:T(8,128)(2,1)}, bf16[2,2,16,768]{3,2,1,0:T(8,128)(2,1)}, bf16[2,2,16,768]{3,2,1,0:T(8,128)(2,1)}) custom-call(bf16[128,768]{1,0:T(8,128)(2,1)} %get-tuple-element.115.a, bf16[2,4,2,16,768]{4,3,2,1,0:T(8,128)(2,1)} %get-tuple-element.64.s0, bf16[2,4,2,16,768]{4,3,2,1,0:T(8,128)(2,1)} %get-tuple-element.65.s1), custom_call_target="tpu_custom_call" | custom-call | tf_op jit(solution)/shard_map/rows_back/pallas_call | solution.py:52
  202.0 31.1 %back.1 = (bf16[14,256,768]{2,1,0:T(8,128)(2,1)}, bf16[2,512,768]{2,1,0:T(8,128)(2,1)}) custom-call(s32[5]{0:T(128)} %stack.49.lim, s32[2,512]{1,0:T(2,128)} %bitcast.114, bf16[512,384]{1,0:T(8,128)(2,1)} %get-tuple-element.63.q, bf16[512,768]{1,0:T(8,128)(2,1)} %bitcast.100, f32[512,384]{1,0:T(8,128)} %get-tuple-element.67.of, ...), custom_call_target="tpu_custom_call" | custom-call | tf_op jit(solution)/shard_map/back/pallas_call | solution.py:756
  233.1 67.6 %return_all.1 = (f32[128,768]{1,0:T(8,128)}, f32[2,16,2304]{2,1,0:T(8,128)}, f32[16,128]{1,0:T(8,128)}) custom-call(bf16[7,4,128,768]{3,2,1,0:T(8,128)(2,1)} %bitcast.90, bf16[2,4,4,2,16,768]{5,4,3,2,1,0:T(8,128)(2,1)} %bitcast.94, bf16[2,2,16,768]{3,2,1,0:T(8,128)(2,1)} %get-tuple-element.75.u0, bf16[2,2,16,768]{3,2,1,0:T(8,128)(2,1)} %get-tuple-element.76.u1), custom_call_target="tpu_custom_call" | custom-call | tf_op jit(solution)/shard_map/return_all/pallas_call | solution.py:52
  300.7 0.7 bitcast_add_fusion.1
  301.4 0.8 slice_reduce_fusion.10
  302.2 0.8 slice_reduce_fusion.11
  303.0 1.0 slice_bitcast_fusion
  304.1 0.6 reshape.195
  304.7 1.2 multiply_reduce_fusion.2
  305.9 1.9 fusion.7
  307.9 0.7 copy.51
  308.7 0.6 slice.172
  309.3 0.6 slice.173
  310.0 0.7 copy.52
  310.8 0.2 slice_reduce_fusion.1
  311.1 0.6 copy.49
  312.5 0.7 copy.47
  313.2 0.7 reshape.201
  (56 shorter events, 2.6 us)
Async XLA Ops:
  111.9 15.9 %copy-start = (bf16[128,768]{1,0:T(8,128)(2,1)S(1)}, bf16[128,768]{1,0:T(8,128)(2,1)}, u32[]{:S(2)}) copy-start(bf16[128,768]{1,0:T(8,128)(2,1)} %tok.1) | copy-start | bytes 589828
  160.8 27.2 %copy-start.2 = (bf16[128,768]{1,0:T(8,128)(2,1)S(1)}, bf16[128,768]{1,0:T(8,128)(2,1)}, u32[]{:S(2)}) copy-start(bf16[128,768]{1,0:T(8,128)(2,1)} %cot.1) | copy-start | bytes 589828
  185.7 2.4 copy-start.1

commit v4 on v3

--- a/solution.py
+++ b/solution.py
@@ -180,19 +180,6 @@
     )
 
 
-def piece_copies(copy, f0, f1, p0, p1, p, x, y, xs, ys):
-    made = []
-    for i in range(3):
-        made.append(copy(f0.at[p], p0.at[y], ys[i]))
-        made.append(copy(f1.at[p], p1.at[:, x], xs[i]))
-    p0[y] = f0[p]
-    p1[:, x] = f1[p]
-    return made
-
-
-PIECE = [jax.ShapeDtypeStruct((4, 4, 2, 16, 768), BF)] * 2
-
-
 def exchange_rows(copy, a, out, k, t, core, far):
     mine, other = k * 2 + t, k * 2 + 1 - t
     c_far = copy(a, out.at[mine], far)
@@ -207,78 +194,6 @@
         c_pass.wait()
 
     return finish
-
-
-def exchange_sums(copy, p, out, got_core, mid, got_far, k, t, core, far):
-    n = p.shape[0]
-    to_core = [copy(p.at[i, pl.ds((1 - k) * 2, 2)], got_core.at[i], core) for i in range(n)]
-
-    def finish():
-        to_far = []
-        for i in range(n):
-            to_core[i].wait()
-            mid[i] = (p[i, k * 2 + 1 - t].astype(F32) + got_core[i, 1 - t].astype(F32)).astype(BF)
-            to_far.append(copy(mid.at[i], got_far.at[i], far))
-        for i in range(n):
-            part = p[i, k * 2 + t].astype(F32) + got_core[i, t].astype(F32)
-            to_far[i].wait()
-            out[i] = part + got_far[i].astype(F32)
-
-    return finish
-
-
-def sum_scratch(n):
-    return [
-        pltpu.VMEM((n, 2, 128, 768), BF),
-        pltpu.VMEM((n, 128, 768), BF),
-        pltpu.VMEM((n, 128, 768), BF),
-    ]
-
-
-def sum_attn_kernel(p, f0, f1, out, p0, p1, got_core, mid, got_far, send, recv):
-    (z, y, x, k, t), xs, ys, core, far, low, ring = spots()
-    copy = Copies(send, recv)
-    greet(xs + ys + [core, far])
-    finish = exchange_sums(copy, p, out, got_core, mid, got_far, k, t, core, far)
-    made = piece_copies(copy, f0, f1, p0, p1, 0, x, y, xs, ys)
-    finish()
-    for c in made:
-        c.wait()
-
-
-def sum_attn(p, f0, f1):
-    return comm_call(
-        sum_attn_kernel,
-        [jax.ShapeDtypeStruct((1, 128, 768), F32)] + PIECE,
-        sum_scratch(1) + [DMA((8,)), DMA((8,))],
-        1,
-        "sum_attn",
-        (p, f0, f1),
-    )
-
-
-def rows_two_kernel(a, cot, f0, f1, out, cot_out, p0, p1, send, recv):
-    (z, y, x, k, t), xs, ys, core, far, low, ring = spots()
-    copy = Copies(send, recv)
-    greet(xs + ys + [core, far])
-    finish = exchange_rows(copy, a, out, k, t, core, far)
-    made = piece_copies(copy, f0, f1, p0, p1, 1, x, y, xs, ys)
-    finish_cot = exchange_rows(copy, cot, cot_out, k, t, core, far)
-    finish()
-    finish_cot()
-    for c in made:
-        c.wait()
-
-
-def rows_two(a, cot, f0, f1):
-    return comm_call(
-        rows_two_kernel,
-        [jax.ShapeDtypeStruct((4, 128, 768), BF)] * 2 + PIECE,
-        [DMA((12,)), DMA((12,))],
-        2,
-        "rows_two",
-        (a, cot, f0, f1),
-    )
 
 
 def spread_first(copy, g0, g1, b0, b1, x, y, xs, ys):
@@ -334,49 +249,149 @@
         u1[zz] = v1.astype(BF)
 
 
-def sum_mlp_kernel(p, g0, g1, out, s0, s1, got_core, mid, got_far, b0, b1, send, recv):
+def mid_kernel(
+    p, f0, f1, cot, tok, vecs, select,
+    output, e1, dr_full, sums, up_sum, u0, u1,
+    got, mid, got_far, p0, p1, w_up, w_down, b_full, cot_full, dg, active, du_full,
+    pr, got_two, mid_two, far_two, dr, g0, g1, b0, b1, s0, s1, a0, a1, send, recv,
+):
     (z, y, x, k, t), xs, ys, core, far, low, ring = spots()
     copy = Copies(send, recv)
     greet(xs + ys + [core, far])
-    finish = exchange_sums(copy, p, out, got_core, mid, got_far, k, t, core, far)
+    mine, across, beside, both = k * 2 + t, k * 2 + 1 - t, 2 - 2 * k + t, 3 - 2 * k - t
+    to_core = copy(p.at[pl.ds((1 - k) * 2, 2)], got, core)
+    made = []
+    for i in range(2):
+        for j in range(3):
+            made.append(copy(f0.at[i], p0.at[i, y], ys[j]))
+            made.append(copy(f1.at[i], p1.at[i, :, x], xs[j]))
+        p0[i, y] = f0[i]
+        p1[i, :, x] = f1[i]
+    to_core.wait()
+    mid[...] = (p[across].astype(F32) + got[1 - t].astype(F32)).astype(BF)
+    to_far = copy(mid, got_far, far)
+    finish_cot = exchange_rows(copy, cot, cot_full, k, t, core, far)
+    part = p[mine].astype(F32) + got[t].astype(F32) + tok[...].astype(F32) + vecs[3:4, :]
+    to_far.wait()
+    hidden = part + got_far[...].astype(F32)
+    centred = hidden - jnp.mean(hidden, axis=-1, keepdims=True)
+    scale = lax.rsqrt(jnp.mean(centred * centred, axis=-1, keepdims=True) + EPS)
+    unit = centred * scale
+    b_full[mine] = (unit * vecs[1:2, :] + vecs[4:5, :]).astype(BF)
+    rows_far = copy(b_full.at[mine], b_full.at[mine], far)
+    rows_core = copy(b_full.at[mine], b_full.at[mine], core)
+    e1[...] = hidden
+    finish_cot()
+    for c in made:
+        c.wait()
+    for i in range(2):
+        rows = slice(i * 384, i * 384 + 384)
+        w_up[rows, :] = matmul(select[...], p0[i].reshape(512, 768)).astype(BF)
+        w_down[rows, :] = matmul(select[...], p1[i].reshape(512, 768)).astype(BF)
+
+    @pl.loop(0, 4)
+    def _(i):
+        dg[i] = matmul(cot_full[i], w_down[...])
+
+    up_sum[...] = jnp.zeros((1, 768), F32)
+
+    def feed(i):
+        u = matmul(b_full[i], w_up[...]) + vecs[7:8, :]
+        phi = 0.5 + 0.5 * lax.erf(u * 0.7071067811865476)
+        gl = (u * phi).astype(BF)
+        active[i] = gl
+        pr[0, i] = matmul_nt(gl, w_down[...]).astype(BF)
+        slope = phi + u * jnp.exp(-0.5 * u * u) * 0.3989422804014327
+        du = (dg[i] * slope).astype(BF)
+        du_full[i] = du
+        up_sum[...] += jnp.sum(du.astype(F32), axis=0, keepdims=True)
+        pr[1, i] = matmul_nt(du, w_up[...]).astype(BF)
+
+    feed(mine)
+    rows_core.wait()
+    feed(beside)
+    first = copy(pr.at[:, beside], got_two.at[:, t], core)
+    rows_far.wait()
+    rows_pass = copy(b_full.at[across], b_full.at[across], core)
+    feed(across)
+    rows_pass.wait()
+    feed(both)
+    second = copy(pr.at[:, both], got_two.at[:, 1 - t], core)
+    second.wait()
+    two = []
+    for i in range(2):
+        v = pr[i, across].astype(F32) + got_two[i, 1 - t].astype(F32)
+        mid_two[i] = v.astype(BF)
+        two.append(copy(mid_two.at[i], far_two.at[i], far))
+    b_rows, du_rows = b_full[...].reshape(512, 768), du_full[...].reshape(512, 768)
+    for i in range(2):
+        cols = slice(i * 384, i * 384 + 384)
+        g = matmul_tn(b_rows[:, cols], du_rows).astype(BF)
+        g0[i] = matmul_tn(select[...], g).astype(BF).reshape(4, 4, 2, 16, 768)
+    c_rows, a_rows = cot_full[...].reshape(512, 768), active[...].reshape(512, 768)
+    for i in range(2):
+        cols = slice(i * 384, i * 384 + 384)
+        g = matmul_tn(c_rows[:, cols], a_rows).astype(BF)
+        g1[i] = matmul_tn(select[...], g).astype(BF).reshape(4, 4, 2, 16, 768)
     over = spread_first(copy, g0, g1, b0, b1, x, y, xs, ys)
-    finish()
+    first.wait()
+    pair = []
+    for i in range(2):
+        v = pr[i, mine].astype(F32) + got_two[i, t].astype(F32)
+        two[i].wait()
+        pair.append(v + far_two[i].astype(F32))
+    hidden = e1[...]
+    output[...] = (hidden + pair[0] + vecs[5:6, :]).astype(BF)
+    centred = hidden - jnp.mean(hidden, axis=-1, keepdims=True)
+    scale = lax.rsqrt(jnp.mean(centred * centred, axis=-1, keepdims=True) + EPS)
+    unit = centred * scale
+    w = pair[1] * vecs[1:2, :]
+    mean_w = jnp.mean(w, axis=-1, keepdims=True)
+    mean_wu = jnp.mean(w * unit, axis=-1, keepdims=True)
+    cot_f = cot[...].astype(F32)
+    grad = cot_f + scale * (w - mean_w - unit * mean_wu)
+    e1[...] = grad
+    low_grad = grad.astype(BF)
+    dr[...] = low_grad
+    finish_rows = exchange_rows(copy, dr, dr_full, k, t, core, far)
+    sums[0:1, :] = jnp.sum(pair[1] * unit, axis=0, keepdims=True)
+    sums[1:2, :] = jnp.sum(low_grad.astype(F32), axis=0, keepdims=True)
+    sums[2:3, :] = jnp.sum(pair[1], axis=0, keepdims=True)
+    sums[3:4, :] = jnp.sum(cot_f, axis=0, keepdims=True)
     add_first(g0, g1, b0, b1, s0, s1, x, y, *over)
-
-
-def sum_mlp(p, g0, g1):
+    over = spread_second(copy, s0, s1, a0, a1, x, y, xs, ys)
+    finish_rows()
+    add_second(s0, s1, a0, a1, u0, u1, x, y, *over)
+
+
+def mid(p, f0, f1, cot, tok, vecs, select):
+    rows = pltpu.VMEM((128, 768), BF)
+    two = pltpu.VMEM((2, 128, 768), BF)
+    four = pltpu.VMEM((4, 128, 768), BF)
+    square = pltpu.VMEM((768, 768), BF)
+    piece = pltpu.VMEM((2, 4, 4, 2, 16, 768), BF)
     return comm_call(
-        sum_mlp_kernel,
-        [jax.ShapeDtypeStruct((2, 128, 768), F32)]
-        + [jax.ShapeDtypeStruct((2, 4, 2, 16, 768), BF)] * 2,
-        sum_scratch(2)
+        mid_kernel,
+        [
+            jax.ShapeDtypeStruct((128, 768), BF),
+            jax.ShapeDtypeStruct((128, 768), F32),
+            jax.ShapeDtypeStruct((4, 128, 768), BF),
+            jax.ShapeDtypeStruct((4, 768), F32),
+            jax.ShapeDtypeStruct((1, 768), F32),
+            jax.ShapeDtypeStruct((2, 2, 16, 768), BF),
+            jax.ShapeDtypeStruct((2, 2, 16, 768), BF),
+        ],
+        [two, rows, rows, piece, piece, square, square, four, four]
+        + [pltpu.VMEM((4, 128, 768), F32), four, four]
+        + [pltpu.VMEM((2, 4, 128, 768), BF), pltpu.VMEM((2, 2, 128, 768), BF), two, two, rows]
+        + [piece, piece]
         + [pltpu.VMEM((3, 2, 4, 2, 16, 768), BF)] * 2
-        + [DMA((10,)), DMA((10,))],
-        3,
-        "sum_mlp",
-        (p, g0, g1),
-    )
-
-
-def rows_back_kernel(a, s0, s1, out, u0, u1, a0, a1, send, recv):
-    (z, y, x, k, t), xs, ys, core, far, low, ring = spots()
-    copy = Copies(send, recv)
-    greet(xs + ys + [core, far])
-    finish = exchange_rows(copy, a, out, k, t, core, far)
-    over = spread_second(copy, s0, s1, a0, a1, x, y, xs, ys)
-    finish()
-    add_second(s0, s1, a0, a1, u0, u1, x, y, *over)
-
-
-def rows_back(a, s0, s1):
-    return comm_call(
-        rows_back_kernel,
-        [jax.ShapeDtypeStruct((4, 128, 768), BF)]
-        + [jax.ShapeDtypeStruct((2, 2, 16, 768), BF)] * 2,
-        [pltpu.VMEM((3, 2, 2, 16, 768), BF)] * 2 + [DMA((9,)), DMA((9,))],
-        4,
-        "rows_back",
-        (a, s0, s1),
+        + [pltpu.VMEM((2, 4, 2, 16, 768), BF)] * 2
+        + [pltpu.VMEM((3, 2, 2, 16, 768), BF)] * 2
+        + [DMA((39,)), DMA((39,))],
+        1,
+        "mid",
+        (p, f0, f1, cot, tok, vecs, select),
     )
 
 
@@ -608,60 +623,6 @@
     )(lim, clip, w, row12, row13, spread, fetch, select, tk)
 
 
-def middle_kernel(
-    b, cot, up_a, up_b, down_a, down_b, vecs, select,
-    pair, g0, g1, up_sum, w_up, w_down, active, inner_back,
-):
-    for i, (up, down) in enumerate(((up_a, down_a), (up_b, down_b))):
-        rows = slice(i * 384, i * 384 + 384)
-        w_up[rows, :] = matmul(select[...], up[...]).astype(BF)
-        w_down[rows, :] = matmul(select[...], down[...]).astype(BF)
-    up_sum[...] = jnp.zeros((1, 768), F32)
-
-    @pl.loop(0, 4)
-    def _(r):
-        rows = pl.ds(pl.multiple_of(r * 128, 128), 128)
-        u = matmul(b[rows, :], w_up[...]) + vecs[7:8, :]
-        phi = 0.5 + 0.5 * lax.erf(u * 0.7071067811865476)
-        gl = (u * phi).astype(BF)
-        active[rows, :] = gl
-        pair[0, rows, :] = matmul_nt(gl, w_down[...]).astype(BF)
-        slope = phi + u * jnp.exp(-0.5 * u * u) * 0.3989422804014327
-        du = (matmul(cot[rows, :], w_down[...]) * slope).astype(BF)
-        inner_back[rows, :] = du
-        up_sum[...] += jnp.sum(du.astype(F32), axis=0, keepdims=True)
-        pair[1, rows, :] = matmul_nt(du, w_up[...]).astype(BF)
-
-    for i in range(2):
-        cols = slice(i * 384, i * 384 + 384)
-        g = matmul_tn(b[:, cols], inner_back[...]).astype(BF)
-        g0[i] = matmul_tn(select[...], g).astype(BF)
-        g = matmul_tn(cot[:, cols], active[...]).astype(BF)
-        g1[i] = matmul_tn(select[...], g).astype(BF)
-
-
-def middle(b, cot, up_a, up_b, down_a, down_b, vecs, select):
-    return pl.pallas_call(
-        middle_kernel,
-        out_shape=[
-            jax.ShapeDtypeStruct((2, 512, 768), BF),
-            jax.ShapeDtypeStruct((2, 512, 768), BF),
-            jax.ShapeDtypeStruct((2, 512, 768), BF),
-            jax.ShapeDtypeStruct((1, 768), F32),
-        ],
-        in_specs=[VM] * 8,
-        out_specs=[VM] * 4,
-        scratch_shapes=[
-            pltpu.VMEM((768, 768), BF),
-            pltpu.VMEM((768, 768), BF),
-            pltpu.VMEM((512, 768), BF),
-            pltpu.VMEM((512, 768), BF),
-        ],
-        compiler_params=pltpu.CompilerParams(vmem_limit_bytes=LIMIT),
-        name="middle",
-    )(b, cot, up_a, up_b, down_a, down_b, vecs, select)
-
-
 def back_kernel(
     lim, clip, q, dr, of, kv, lse, unit, w_attn, vecs, sums, up_sum, spread, put, select, row12,
     d_out, grad, total, dox, delta, dq, ug,
@@ -852,40 +813,8 @@
         select,
         near_tokens.reshape(14, 256, 768),
     )
-    gains, biases = vecs[0:2], vecs[2:6]
-    hidden = tokens.astype(F32)
-    attn, up_a, down_a = sum_attn(attn.reshape(1, 4, 128, 768), f0, f1)
-    hidden_one = hidden + attn[0] + biases[1]
-    normed_two, unit_two, scale_two = normalize(hidden_one, gains[1], biases[2])
-    full_two, cot, up_b, down_b = rows_two(normed_two.astype(BF), cotangent, f0, f1)
-    pair, grad_up, grad_down, up_sum = middle(
-        full_two.reshape(512, 768),
-        cot.reshape(512, 768),
-        up_a.reshape(512, 768),
-        up_b.reshape(512, 768),
-        down_a.reshape(512, 768),
-        down_b.reshape(512, 768),
-        vecs,
-        select,
-    )
-    shape = (2, 4, 4, 2, 16, 768)
-    pair_sum, s0, s1 = sum_mlp(
-        pair.reshape(2, 4, 128, 768), grad_up.reshape(shape), grad_down.reshape(shape)
-    )
-    output = (hidden_one + pair_sum[0] + biases[3]).astype(BF)
-    grad_normed_two = pair_sum[1]
-    grad_hidden_one = cotangent.astype(F32) + normalize_back(
-        grad_normed_two, unit_two, scale_two, gains[1]
-    )
-    grad_attn = grad_hidden_one.astype(BF)
-    full_attn, u0, u1 = rows_back(grad_attn, s0, s1)
-    sums = jnp.stack(
-        [
-            jnp.sum(grad_normed_two * unit_two, axis=0),
-            jnp.sum(grad_attn.astype(F32), axis=0),
-            jnp.sum(grad_normed_two, axis=0),
-            jnp.sum(cotangent.astype(F32), axis=0),
-        ]
+    output, grad_hidden_one, full_attn, sums, up_sum, u0, u1 = mid(
+        attn.reshape(4, 128, 768), f0, f1, cotangent, tokens, vecs, select
     )
     near_back, grad_w = back(
         lim,
@@ -906,10 +835,10 @@
         row12,
     )
     back_one, own, far = return_all(
-        near_back.reshape(7, 4, 128, 768), grad_w.reshape(shape), u0, u1
-    )
-    _, unit_one, scale_one = normalize(hidden, gains[0], biases[0])
-    grad_tokens = grad_hidden_one + normalize_back(back_one, unit_one, scale_one, gains[0])
+        near_back.reshape(7, 4, 128, 768), grad_w.reshape(2, 4, 4, 2, 16, 768), u0, u1
+    )
+    _, unit_one, scale_one = normalize(tokens.astype(F32), vecs[0], vecs[2])
+    grad_tokens = grad_hidden_one + normalize_back(back_one, unit_one, scale_one, vecs[0])
     vec = own[0, 12, 0:128] + own[1, 12, 0:128] + far[12]
     vec = vec[0:72].reshape(6, 2, 6)
     vec = jnp.where(t == 0, vec[:, 0], vec[:, 1])

time: 312 us -> 286 us (0.917); the launches traced: 314 us -> 285 us
  Pallas kernels: 275 us -> 254 us
  other arithmetic: 13.5 us -> 4.77 us
    pallas_call x1 -> x0, Pallas kernels: 13.5 us -> none  [middle(): pl.pallas_call(middle_kernel, out_shape=[jax.ShapeDtypeStruct((2, 512, 76...]
    pallas_call x6 -> x3, Pallas kernels: 201 us -> 193 us  [comm_call(): pl.pallas_call(kernel, out_shape=out_shape, in_specs=[VM] * len(args), ou...]
    reduce_sum x3 -> x0, other arithmetic: 3.27 us -> none  [the longest x1 1.23 us: body(): jnp.sum(grad_normed_two * unit_two, axis=0)]
where the time goes in v4:
time: 286 us; the launch traced here: 285 us
  Pallas kernels  254 us (89%)
  local copies, waits for them, and re-layouts  22.2 us (8%)
  other arithmetic  4.77 us (2%)
  between operations  3.62 us (1%)
    pallas_call x3, Pallas kernels, comm_call(): pl.pallas_call(kernel, out_shape=out_shape, in_specs=[VM] * len(args), ou...  193 us
    pallas_call x1, Pallas kernels, back(): pl.pallas_call(back_kernel, out_shape=[jax.ShapeDtypeStruct((14, 256, 768...  31.1 us
    pallas_call x1, Pallas kernels, front(): pl.pallas_call(front_kernel, out_shape=[jax.ShapeDtypeStruct((8, 768), F3...  29.7 us

profile of v4, /device:TPU:1, one launch (start us, length us, event | category | flops | bytes accessed | tf_op | source)
XLA Modules:
  0.0 284.6 jit_solution(16702309072110076523)
XLA Ops:
  0.7 0.8 copy.40
  1.5 0.7 reshape.125
  2.3 0.8 reshape.126
  3.1 0.7 reshape.127
  3.9 0.8 fusion.21
  4.7 0.1 stack_squeeze.12
  4.9 0.1 pad_maximum_fusion
  5.0 0.1 reshape.122
  5.2 0.8 stack_reshape.4
  6.0 0.1 pad_maximum_fusion.1
  6.1 0.1 reshape.123
  6.2 0.8 reshape_squeeze.13
  7.1 0.8 reshape.124
  7.9 0.7 maximum_maximum_fusion.pay
  8.6 0.6 pad.21.tile
  9.2 63.8 %gather_first.1 = (bf16[2,4,4,2,16,768]{5,4,3,2,1,0:T(8,128)(2,1)}, bf16[2,4,2,16,768]{4,3,2,1,0:T(8,128)(2,1)}, bf16[2,4,2,16,768]{4,3,2,1,0:T(8,128)(2,1)}, s3...) custom-call(bf16[2,16,2304]{2,1,0:T(8,128)(2,1)} %maximum_maximum_fusion.pay, bf16[16,128]{1,0:T(8,128)(2,1)} %pad.21.tile, ...), custom_call_target="tpu_custom_call" | custom-call | tf_op jit(solution)/shard_map/gather_first/pallas_call | solution.py:52
  73.0 1.3 fusion.22
  77.0 0.6 stack.34.lim
  77.6 1.4 multiply_add_fusion.fetch
  78.9 1.0 fusion.18
  80.0 0.6 copy.59
  80.6 0.6 copy.60
  81.2 29.7 %front.1 = (f32[8,768]{1,0:T(8,128)}, bf16[768,768]{1,0:T(8,128)(2,1)}, bf16[14,256,768]{2,1,0:T(8,128)(2,1)}, bf16[14,256,384]{2,1,0:T(8,128)(2,1)}, bf16[512,3...) custom-call(s32[5]{0:T(128)} %stack.34.lim, s32[2,512]{1,0:T(2,128)} %bitcast.74, ...), custom_call_target="tpu_custom_call" | custom-call | tf_op jit(solution)/shard_map/front/pallas_call | solution.py:607
  110.9 62.7 %mid.1 = (bf16[128,768]{1,0:T(8,128)(2,1)}, f32[128,768]{1,0:T(8,128)}, bf16[4,128,768]{2,1,0:T(8,128)(2,1)}, f32[4,768]{1,0:T(4,128)}, f32[1,768]{1,0:T(1,128)}...) custom-call(bf16[4,128,768]{2,1,0:T(8,128)(2,1)} %bitcast.66, ...), custom_call_target="tpu_custom_call" | custom-call | tf_op jit(solution)/shard_map/mid/pallas_call | solution.py:52
  173.7 31.1 %back.1 = (bf16[14,256,768]{2,1,0:T(8,128)(2,1)}, bf16[2,512,768]{2,1,0:T(8,128)(2,1)}) custom-call(s32[5]{0:T(128)} %stack.34.lim, s32[2,512]{1,0:T(2,128)} %bitcast.75, bf16[512,384]{1,0:T(8,128)(2,1)} %get-tuple-element.44.q, bf16[512,768]{1,0:T(8,128)(2,1)} %bitcast.65, f32[512,384]{1,0:T(8,128)} %get-tuple-element.46.of, ...), custom_call_target="tpu_custom_call" | custom-call | tf_op jit(solution)/shard_map/back/pallas_call | solution.py:717
  204.8 66.7 %return_all.1 = (f32[128,768]{1,0:T(8,128)}, f32[2,16,2304]{2,1,0:T(8,128)}, f32[16,128]{1,0:T(8,128)}) custom-call(bf16[7,4,128,768]{3,2,1,0:T(8,128)(2,1)} %bitcast.60, bf16[2,4,4,2,16,768]{5,4,3,2,1,0:T(8,128)(2,1)} %bitcast.64, bf16[2,2,16,768]{3,2,1,0:T(8,128)(2,1)} %get-tuple-element.55.u0, bf16[2,2,16,768]{3,2,1,0:T(8,128)(2,1)} %get-tuple-element.56.u1), custom_call_target="tpu_custom_call" | custom-call | tf_op jit(solution)/shard_map/return_all/pallas_call | solution.py:52
  271.5 0.8 bitcast_add_fusion
  272.4 0.6 slice.141
  272.9 0.6 slice.140
  273.5 1.0 slice_bitcast_fusion
  274.5 0.1 reshape.138
  274.7 0.2 slice_reduce_fusion.2
  275.1 0.1 reshape.137
  275.2 0.2 slice_reduce_fusion
  275.6 0.7 copy.47
  276.4 0.7 copy.52
  277.2 0.6 copy.49
  277.9 0.7 reshape.145
  278.6 0.8 slice_reduce_fusion.4
  279.4 0.1 convert_reduce_fusion
  279.5 0.2 fusion.8
  279.7 0.2 multiply_reduce_fusion
  280.0 0.9 fusion.7
  280.9 0.8 slice_reduce_fusion.5
  281.7 0.7 copy.51
  282.4 0.8 slice_reduce_fusion.6
  283.3 0.6 reshape.139
  283.9 0.7 copy.62
  (41 shorter events, 1.4 us)
Async XLA Ops:
  271.4 7.9 %copy-start = (bf16[128,768]{1,0:T(8,128)(2,1)S(1)}, bf16[128,768]{1,0:T(8,128)(2,1)}, u32[]{:S(2)}) copy-start(bf16[128,768]{1,0:T(8,128)(2,1)} %tok.3) | copy-start | bytes 589828
  271.4 8.3 %copy-start.1 = (f32[128,768]{1,0:T(8,128)S(1)}, f32[128,768]{1,0:T(8,128)}, u32[]{:S(2)}) copy-start(f32[128,768]{1,0:T(8,128)} %get-tuple-element.57) | copy-start | bytes 1179652
  271.5 8.5 %copy-start.2 = (f32[128,768]{1,0:T(8,128)S(1)}, f32[128,768]{1,0:T(8,128)}, u32[]{:S(2)}) copy-start(f32[128,768]{1,0:T(8,128)} %get-tuple-element.43) | copy-start | bytes 1179652
  274.5 9.5 %copy-start.3 = (bf16[128,768]{1,0:T(8,128)(2,1)S(1)}, bf16[128,768]{1,0:T(8,128)(2,1)}, u32[]{:S(2)}) copy-start(bf16[128,768]{1,0:T(8,128)(2,1)} %get-tuple-element.111) | copy-start | bytes 589828

commit v5 on v4

--- a/solution.py
+++ b/solution.py
@@ -87,28 +87,54 @@
         return made
 
 
+def build_rows(attn_w, proj, up, down, gain, row, qv, fc, pads, place, masks, t, pay, tile):
+    def tall(v):
+        return matmul(pads[...], v)
+
+    query, keys, values = [tall(attn_w[i]) for i in range(3)]
+    mixed, up_rows, down_rows = tall(proj[...]), tall(up[...]), tall(down[...])
+    norms = jnp.sum(matmul(gain[...], place[0:6, :]) * masks[0:2, :], axis=0, keepdims=True)
+    norms += jnp.sum(matmul(row[...], place[0:6, :]) * masks[2:6, :], axis=0, keepdims=True)
+    lane = lax.broadcasted_iota(jnp.int32, (16, 128), 1)
+    line = lax.broadcasted_iota(jnp.int32, (16, 128), 0)
+    others = jnp.sum(matmul(qv[...], place[0:6, :]) * masks[6:8, :], axis=0, keepdims=True)
+    others += jnp.sum(matmul(fc[...], place[8:14, :]) * masks[8:12, :], axis=0, keepdims=True)
+    mine = (line == 12) & (lane >= 64 * t) & (lane < 64 * t + 64)
+    small = jnp.where(mine, norms, 0.0)
+    tile[...] = small.astype(BF)
+    small = small + jnp.where(line == 13, others, 0.0)
+    for q in range(2):
+        for h in range(3):
+            n = slice((q * 3 + h) * 64, (q * 3 + h) * 64 + 64)
+            first = jnp.concatenate([keys[:, n], values[:, n]], axis=1)
+            if h == 0:
+                first = first + small
+            pay[q, :, h * 128 : h * 128 + 128] = first.astype(BF)
+            second = jnp.concatenate([query[:, n], mixed[:, n]], axis=1)
+            pay[q, :, 384 + h * 128 : 512 + h * 128] = second.astype(BF)
+        pay[q, :, 768:1536] = up_rows[:, q * 768 : q * 768 + 768].astype(BF)
+        pay[q, :, 1536:2304] = down_rows[:, q * 768 : q * 768 + 768].astype(BF)
+
+
+H0, H1 = pl.ds(0, 512), pl.ds(512, 256)
+
+
 def gather_kernel(
-    pay, tile, clip, tok, w, f0, f1, clip_out, tk, pay_s, tile_in, ws, send, recv
+    clip, tok, attn_w, proj, up, down, gain, row, qv, fc, pads, place, masks,
+    w, f0, f1, clip_out, tk, pay_s, tile, tile_in, ws, send, recv,
 ):
     (z, y, x, k, t), xs, ys, core, far, low, ring = spots()
     copy = Copies(send, recv)
     mine, other = k * 2 + t, k * 2 + 1 - t
     greet(xs + ys + [core, far, low] + ring)
-    c_tile = copy(tile, tile_in, far)
     own_far = copy(tok, tk.at[3, mine], far)
     order = (4, 5, 2, 3, 0, 1)
     pushes = {i: copy(tok, tk.at[3 - RING[i], mine], ring[i]) for i in order}
     done = [copy(tok, tk.at[3, mine], core), copy(clip, clip_out.at[k], core)]
+    build_rows(attn_w, proj, up, down, gain, row, qv, fc, pads, place, masks, t, pay_s, tile)
+    c_tile = copy(tile, tile_in, far)
     clip_out[k] = clip[...]
     tk[3, mine] = tok[...]
-    c_tile.wait()
-    pay_s[...] = pay[...]
-    for q in range(2):
-        pay_s[q, :, 0:128] = pay[q, :, 0:128] + tile_in[...]
-    swap = copy(pay_s.at[1 - k], ws.at[z, k], core)
-    ws[z, k] = pay_s[k]
-    swap.wait()
-    c_low = copy(ws.at[z], ws.at[z], low)
     to_far = {}
 
     def pass_on(i):
@@ -117,26 +143,32 @@
         to_far[i] = copy(a, a, far)
         done.append(copy(a, a, core))
 
+    c_tile.wait()
+    for q in range(2):
+        pay_s[q, :, 0:128] = pay_s[q, :, 0:128] + tile_in[...]
+    swap = copy(pay_s.at[1 - k], ws.at[z, k], core)
+    ws[z, k] = pay_s[k]
+    swap.wait()
+    c_low = copy(ws.at[z], ws.at[z], low)
     pass_on(4)
     pass_on(5)
     c_low.wait()
     w[:, y, x] = ws[:, :, :, 0:768]
     f0[:, x] = ws[:, :, :, 768:1536]
     f1[:, y] = ws[:, :, :, 1536:2304]
-    h0, h1 = pl.ds(0, 384), pl.ds(384, 384)
     phase = []
     for i in range(3):
-        phase.append(copy(ws.at[:, :, :, h0], w.at[:, y, x, :, :, h0], xs[i]))
-        phase.append(copy(ws.at[:, :, :, h1], w.at[:, y, x, :, :, h1], ys[i]))
+        phase.append(copy(ws.at[:, :, :, H0], w.at[:, y, x, :, :, H0], xs[i]))
+        phase.append(copy(ws.at[:, :, :, H1], w.at[:, y, x, :, :, H1], ys[i]))
     pass_on(2)
     pass_on(3)
     for c in phase:
         c.wait()
     rest = []
     for i in range(3):
-        a = w.at[:, y, :, :, :, h0]
+        a = w.at[:, y, :, :, :, H0]
         rest.append(copy(a, a, ys[i]))
-        b = w.at[:, :, x, :, :, h1]
+        b = w.at[:, :, x, :, :, H1]
         rest.append(copy(b, b, xs[i]))
     pass_on(0)
     pass_on(1)
@@ -157,7 +189,7 @@
         c.wait()
 
 
-def gather_all(pay, tile, clip, tok):
+def gather_all(*args):
     return comm_call(
         gather_kernel,
         [
@@ -170,13 +202,14 @@
         [
             pltpu.VMEM((2, 16, 2304), BF),
             pltpu.VMEM((16, 128), BF),
+            pltpu.VMEM((16, 128), BF),
             pltpu.VMEM((2, 2, 16, 2304), BF),
-            DMA((53,)),
-            DMA((53,)),
+            DMA((50,)),
+            DMA((50,)),
         ],
         0,
         "gather_first",
-        (pay, tile, clip, tok),
+        args,
     )
 
 
@@ -397,60 +430,78 @@
 
 def return_kernel(
     d, g, u0, u1, out, own, tile_out,
-    got_core, e_send, got_far, r_send, got_ring,
-    b0, b1, s0, s1, a0, a1, v0, v1, z_in0, z_in1, z_in2, z_in3, res, tile, send, recv,
+    got_core, v1, in1, e_send, got_far, r_send, got_ring,
+    b0, b1, s0, s1, a0, a1, v_0, v_1, z_in0, z_in1, z_in2, z_in3, res, tile, send, recv,
 ):
     (z, y, x, k, t), xs, ys, core, far, low, ring = spots()
     copy = Copies(send, recv)
     greet(xs + ys + [core, far, low] + ring)
-    order = [3 + r for r in RING] + [3]
+    mine, across = k * 2 + t, k * 2 + 1 - t
+    near = (ring[4], ring[5])
+    order = (4, 2, 5, 1, 6, 0, 3)
     to_core = {j: copy(d.at[j, pl.ds((1 - k) * 2, 2)], got_core.at[j], core) for j in order}
-    g0, g1 = g.at[:, :, :, :, :, pl.ds(0, 384)], g.at[:, :, :, :, :, pl.ds(384, 384)]
+    g0, g1 = g.at[:, :, :, :, :, H0], g.at[:, :, :, :, :, H1]
+    fc_z = [copy(u0.at[1 - z], z_in0, low), copy(u1.at[1 - z], z_in1, low)]
+    hop1, to_far = [], []
     over = spread_first(copy, g0, g1, b0, b1, x, y, xs, ys)
-    fc_z = [copy(u0.at[1 - z], z_in0, low), copy(u1.at[1 - z], z_in1, low)]
-    to_far = {}
-    for j in order:
+    for i, j in enumerate((4, 2)):
         to_core[j].wait()
-        e_send[j] = (d[j, k * 2 + 1 - t].astype(F32) + got_core[j, 1 - t].astype(F32)).astype(BF)
-        to_far[j] = copy(e_send.at[j], got_far.at[j], far)
+        v1[i] = (d[j, pl.ds(k * 2, 2)].astype(F32) + got_core[j].astype(F32)).astype(BF)
+        hop1.append(copy(v1.at[i], in1.at[i], near[i]))
+    for i, j in enumerate(order[2:6]):
+        to_core[j].wait()
+        e_send[i] = (d[j, across].astype(F32) + got_core[j, 1 - t].astype(F32)).astype(BF)
+        to_far.append(copy(e_send.at[i], got_far.at[i], far))
+    home = []
+
+    def send_home(i):
+        j = order[2 + i]
+        to_far[i].wait()
+        v = d[j, mine].astype(F32) + got_core[j, t].astype(F32) + got_far[i].astype(F32)
+        r_send[i] = v.astype(BF)
+        home.append(copy(r_send.at[i], got_ring.at[i], ring[i]))
+
+    send_home(0)
+    send_home(1)
     add_first(g0, g1, b0, b1, s0, s1, x, y, *over)
     over = spread_second(copy, s0, s1, a0, a1, x, y, xs, ys)
-    home = []
-
-    def send_home(i):
-        j = order[i]
-        to_far[j].wait()
-        v = d[j, k * 2 + t].astype(F32) + got_core[j, t].astype(F32) + got_far[j].astype(F32)
-        r_send[i] = v.astype(BF)
-        home.append(copy(r_send.at[i], got_ring.at[i], ring[i]))
-
-    for i in range(3):
-        send_home(i)
-    add_second(s0, s1, a0, a1, v0, v1, x, y, *over)
-    attn_z = [copy(v0.at[1 - z], z_in2, low), copy(v1.at[1 - z], z_in3, low)]
-    for i in range(3, 6):
-        send_home(i)
-    for c in fc_z + attn_z:
+    to_core[3].wait()
+    hop1[0].wait()
+    hop1[1].wait()
+    v = d[3, across].astype(F32) + got_core[3, 1 - t].astype(F32)
+    v = v + in1[0, 1 - t].astype(F32) + in1[1, 1 - t].astype(F32)
+    e_send[4] = v.astype(BF)
+    last = copy(e_send.at[4], got_far.at[4], far)
+    send_home(2)
+    send_home(3)
+    add_second(s0, s1, a0, a1, v_0, v_1, x, y, *over)
+    attn_z = [copy(v_0.at[1 - z], z_in2, low), copy(v_1.at[1 - z], z_in3, low)]
+    for c in fc_z:
         c.wait()
-    res[:, :, 0:384] = v0[z].astype(F32) + z_in2[...].astype(F32)
-    res[:, :, 384:768] = v1[z].astype(F32) + z_in3[...].astype(F32)
     res[:, :, 768:1536] = u0[z].astype(F32) + z_in0[...].astype(F32)
     res[:, :, 1536:2304] = u1[z].astype(F32) + z_in1[...].astype(F32)
+    for c in attn_z:
+        c.wait()
+    res[:, :, H0] = v_0[z].astype(F32) + z_in2[...].astype(F32)
+    res[:, :, H1] = v_1[z].astype(F32) + z_in3[...].astype(F32)
     swap = copy(res.at[1 - k], own.at[k], core)
     own[k] = res[k]
-    to_far[3].wait()
-    total = d[3, k * 2 + t].astype(F32) + got_core[3, t].astype(F32) + got_far[3].astype(F32)
+    total = d[3, mine].astype(F32) + got_core[3, t].astype(F32)
+    total = total + in1[0, t].astype(F32) + in1[1, t].astype(F32)
     swap.wait()
     tile[...] = own[0, :, 0:128] + own[1, :, 0:128]
     c_tile = copy(tile, tile_out, far)
-    for i in range(6):
+    for i in range(4):
         home[i].wait()
         total = total + got_ring[i].astype(F32)
-    out[...] = total
+    last.wait()
+    out[...] = total + got_far[4].astype(F32)
     c_tile.wait()
 
 
 def return_all(d, g, u0, u1):
+    two = pltpu.VMEM((2, 2, 128, 768), BF)
+    wide, slim = 512, 256
     return comm_call(
         return_kernel,
         [
@@ -458,20 +509,15 @@
             jax.ShapeDtypeStruct((2, 16, 2304), F32),
             jax.ShapeDtypeStruct((16, 128), F32),
         ],
-        [
-            pltpu.VMEM((7, 2, 128, 768), BF),
-            pltpu.VMEM((7, 128, 768), BF),
-            pltpu.VMEM((7, 128, 768), BF),
-            pltpu.VMEM((6, 128, 768), BF),
-            pltpu.VMEM((6, 128, 768), BF),
-        ]
-        + [pltpu.VMEM((3, 2, 4, 2, 16, 384), BF)] * 2
-        + [pltpu.VMEM((2, 4, 2, 16, 384), BF)] * 2
-        + [pltpu.VMEM((3, 2, 2, 16, 384), BF)] * 2
-        + [pltpu.VMEM((2, 2, 16, 384), BF)] * 2
-        + [pltpu.VMEM((2, 16, 768), BF)] * 2
-        + [pltpu.VMEM((2, 16, 384), BF)] * 2
-        + [pltpu.VMEM((2, 16, 2304), F32), pltpu.VMEM((16, 128), F32), DMA((38,)), DMA((38,))],
+        [pltpu.VMEM((7, 2, 128, 768), BF), two, two]
+        + [pltpu.VMEM((5, 128, 768), BF)] * 2
+        + [pltpu.VMEM((4, 128, 768), BF)] * 2
+        + [pltpu.VMEM((3, 2, 4, 2, 16, n), BF) for n in (wide, slim)]
+        + [pltpu.VMEM((2, 4, 2, 16, n), BF) for n in (wide, slim)]
+        + [pltpu.VMEM((3, 2, 2, 16, n), BF) for n in (wide, slim)]
+        + [pltpu.VMEM((2, 2, 16, n), BF) for n in (wide, slim)]
+        + [pltpu.VMEM((2, 16, n), BF) for n in (768, 768, wide, slim)]
+        + [pltpu.VMEM((2, 16, 2304), F32), pltpu.VMEM((16, 128), F32), DMA((36,)), DMA((36,))],
         5,
         "return_all",
         (d, g, u0, u1),
@@ -500,17 +546,48 @@
     back.append(78 + (d // 256) * 4 + d % 4)
     select = np.arange(512)[None, :] == (np.arange(384) // 12 * 16 + np.arange(384) % 12)[:, None]
     row12 = np.arange(512)[:, None] == np.arange(32)[None, :] * 16 + 12
+    row13 = np.arange(512)[:, None] == np.arange(32)[None, :] * 16 + 13
+    pads = np.arange(16)[:, None] == np.arange(12)[None, :]
+    lane = np.arange(128)
+    half = lane % 64
+    six = half % 6 == np.arange(6)[:, None]
+    four = lane % 4 == np.arange(4)[:, None]
+    place = np.zeros((14, 128), np.float32)
+    place[0:6], place[8:14] = six, lane // 4 == 3 + np.arange(6)[:, None]
+    masks = [half // 6 == p for p in range(6)] + [lane // 6 == p for p in range(2)]
+    masks += [(lane >= 12) & (lane < 36) & four[e] for e in range(4)]
+    three = lane % 3 == np.arange(3)[:, None]
+    ends = np.zeros((24, 128), np.float32)
+    ends[0:6], ends[8:11], ends[19:22] = lane % 6 == np.arange(6)[:, None], three, three
+    fours = (lane + 2) % 4 == np.arange(4)[:, None]
     return (
         spread,
         np.stack(rows).astype(np.int32),
         step,
         np.stack(back).astype(np.int32),
         select.astype(np.float32),
-        row12.astype(np.float32),
-    )
-
-
-SPREAD, FETCH, FETCH_STEP, PUT, SELECT, ROW12 = layout_tables()
+        np.stack([row12, row13]).astype(np.float32),
+        pads.astype(np.float32),
+        place,
+        np.stack(masks).astype(np.float32),
+        ends,
+        fours.astype(np.float32),
+    )
+
+
+(
+    SPREAD,
+    FETCH,
+    FETCH_STEP,
+    PUT,
+    SELECT,
+    ROWS,
+    PADS,
+    PLACE,
+    MASKS,
+    ENDS,
+    FOURS,
+) = layout_tables()
 
 
 def matmul(left, right):
@@ -525,24 +602,37 @@
     return lax.dot_general(left, right, TN, preferred_element_type=F32)
 
 
-def allowed_pairs(lim, clip, qb, j):
-    cols = pl.ds(qb * 256, 256)
-    pos = lim[4] + j * 256 + lax.broadcasted_iota(jnp.int32, (256, 256), 0)
-    return (pos >= clip[0:1, cols]) & (pos < clip[1:2, cols])
+def allowed_pairs(clip, qb, j):
+    pos = first_key() + j * 256 + lax.broadcasted_iota(jnp.int32, (256, 256), 0)
+    return (pos >= clip[qb, 0:1, :]) & (pos < clip[qb, 1:2, :])
+
+
+def first_key():
+    return (lax.axis_index("dp") // 2 - 3) * 512
+
+
+def key_blocks(ends, qb):
+    first = (ends[qb, 0, 0] - first_key()) // 256
+    return first, (ends[qb, 1, 255] - first_key() + 255) // 256
 
 
 def front_kernel(
-    lim, clip, w, row12, row13, spread, fetch, select, tk,
+    ends, clip, w, small_rows, spread, fetch, step_k, select, tk,
     vecs, w_attn, unit, kv, q, of, lse, attn,
 ):
     line = lax.broadcasted_iota(jnp.int32, (128, 768), 0)
-    wide = matmul_tn(row12[...], spread[0])
+    k = lax.axis_index("dp") % 2
+    row12, row13 = [
+        jnp.concatenate([matmul_tn(small_rows[i], w[z, :, 0:128]) for z in range(2)]).astype(BF)
+        for i in range(2)
+    ]
+    wide = matmul_tn(row12, spread[0])
     for p in range(6):
         hit = line == fetch[p : p + 1, :]
         vecs[p : p + 1, :] = jnp.sum(jnp.where(hit, wide, 0.0), axis=0, keepdims=True)
     for p in (6, 7):
-        wide = matmul_tn(row13[...], spread[p - 5])
-        hit = line == fetch[p : p + 1, :]
+        wide = matmul_tn(row13, spread[p - 5])
+        hit = line == fetch[p : p + 1, :] + k * step_k[p : p + 1, :]
         vecs[p : p + 1, :] = jnp.sum(jnp.where(hit, wide, 0.0), axis=0, keepdims=True)
     for z in range(2):
         w_attn[z * 384 : z * 384 + 384, :] = matmul(select[...], w[z]).astype(BF)
@@ -554,7 +644,9 @@
         u = centred * lax.rsqrt(spread_out + EPS)
         return u, (u * vecs[0:1, :] + vecs[2:3, :]).astype(BF)
 
-    @pl.loop(lim[0], lim[3])
+    bounds = [key_blocks(ends, qb) for qb in range(2)]
+
+    @pl.loop(bounds[0][0], bounds[1][1])
     def _(j):
         u, a = norm_rows(j)
         unit[j] = u.astype(BF)
@@ -571,7 +663,7 @@
         rows = slice(qb * 256, qb * 256 + 256)
 
         def step(j, carry):
-            ok = allowed_pairs(lim, clip, qb, j)
+            ok = allowed_pairs(clip, qb, j)
             new = []
             for h in range(3):
                 m, l, acc = carry[h]
@@ -594,7 +686,7 @@
             )
             for _ in range(3)
         )
-        final = lax.fori_loop(lim[2 * qb], lim[2 * qb + 1], step, start)
+        final = lax.fori_loop(bounds[qb][0], bounds[qb][1], step, start)
         for h in range(3):
             m, l, acc = final[h]
             o = (acc / l).T
@@ -603,7 +695,7 @@
         attn[rows, :] = matmul_nt(of[rows, :].astype(BF), w_attn[:, 384:768]).astype(BF)
 
 
-def front(lim, clip, w, row12, row13, spread, fetch, select, tk):
+def front(*args):
     return pl.pallas_call(
         front_kernel,
         out_shape=[
@@ -620,13 +712,14 @@
         out_specs=[VM] * 8,
         compiler_params=pltpu.CompilerParams(vmem_limit_bytes=LIMIT),
         name="front",
-    )(lim, clip, w, row12, row13, spread, fetch, select, tk)
+    )(*args)
 
 
 def back_kernel(
-    lim, clip, q, dr, of, kv, lse, unit, w_attn, vecs, sums, up_sum, spread, put, select, row12,
+    ends, clip, q, dr, of, kv, lse, unit, w_attn, vecs, sums, up_sum, spread, put, select, row12,
     d_out, grad, total, dox, delta, dq, ug,
 ):
+    bounds = [key_blocks(ends, qb) for qb in range(2)]
     lane = lax.broadcasted_iota(jnp.int32, (256, 128), 1)
     high = (lax.broadcasted_iota(jnp.int32, (256, 384), 1) & 127) >= 64
 
@@ -648,7 +741,7 @@
         rows = slice(qb * 256, qb * 256 + 256)
 
         def step(j, carry):
-            ok = allowed_pairs(lim, clip, qb, j)
+            ok = allowed_pairs(clip, qb, j)
             new = []
             for h in range(3):
                 cols = slice(h * 128, h * 128 + 128)
@@ -662,7 +755,7 @@
             return tuple(new)
 
         start = tuple(jnp.zeros((128, 256), F32) for _ in range(3))
-        final = lax.fori_loop(lim[2 * qb], lim[2 * qb + 1], step, start)
+        final = lax.fori_loop(bounds[qb][0], bounds[qb][1], step, start)
         for h in range(3):
             part = jnp.where(lane < 64, SCORE_SCALE * final[h].T, 0.0)
             dq[rows, h * 128 : h * 128 + 128] = part.astype(BF)
@@ -675,7 +768,7 @@
         ug[:, 0:384] += matmul_tn(unit[j], z)
         return kv_sum + jnp.sum(z.astype(F32), axis=0, keepdims=True)
 
-    kv_sum = lax.fori_loop(lim[0], lim[3], chunk, jnp.zeros((1, 384), F32))
+    kv_sum = lax.fori_loop(bounds[0][0], bounds[1][1], chunk, jnp.zeros((1, 384), F32))
     for qb in range(2):
         rows = slice(qb * 256, qb * 256 + 256)
         own = matmul_nt(total[6 + qb].astype(BF), w_attn[:, 0:384])
@@ -713,14 +806,14 @@
         grad[i, :, 0:128] = (g[:, 0:128] + extra).astype(BF)
 
 
-def back(lim, *args):
+def back(*args):
     return pl.pallas_call(
         back_kernel,
         out_shape=[
             jax.ShapeDtypeStruct((14, 256, 768), BF),
             jax.ShapeDtypeStruct((2, 512, 768), BF),
         ],
-        in_specs=[SM] + [VM] * len(args),
+        in_specs=[SM] + [VM] * (len(args) - 1),
         out_specs=[VM, VM],
         scratch_shapes=[
             pltpu.VMEM((14, 256, 384), F32),
@@ -731,23 +824,83 @@
         ],
         compiler_params=pltpu.CompilerParams(vmem_limit_bytes=LIMIT),
         name="back",
-    )(lim, *args)
-
-
-def normalize(hidden, gain, offset):
-    average = jnp.mean(hidden, axis=-1, keepdims=True)
-    centred = hidden - average
-    spread = jnp.mean(centred * centred, axis=-1, keepdims=True)
-    scale = lax.rsqrt(spread + EPS)
+    )(*args)
+
+
+def finish_kernel(
+    own, far, back_one, e1, tok, vecs, ends, fours,
+    tokens, g_in, g_qv, g_out, g_up, g_fc, g_down, g_gain, g_row,
+):
+    t = lax.axis_index("tensor")
+    hidden = tok[...].astype(F32)
+    centred = hidden - jnp.mean(hidden, axis=-1, keepdims=True)
+    scale = lax.rsqrt(jnp.mean(centred * centred, axis=-1, keepdims=True) + EPS)
     unit = centred * scale
-    return unit * gain + offset, unit, scale
-
-
-def normalize_back(grad_out, unit, scale, gain):
-    grad_unit = grad_out * gain
-    first = jnp.mean(grad_unit, axis=-1, keepdims=True)
-    second = jnp.mean(grad_unit * unit, axis=-1, keepdims=True)
-    return scale * (grad_unit - first - unit * second)
+    w = back_one[...] * vecs[0:1, :]
+    mean_w = jnp.mean(w, axis=-1, keepdims=True)
+    mean_wu = jnp.mean(w * unit, axis=-1, keepdims=True)
+    tokens[...] = e1[...] + scale * (w - mean_w - unit * mean_wu)
+
+    exact = dict(precision=lax.Precision.HIGHEST, preferred_element_type=F32)
+    for n in range(3):
+        cols = slice(n * 128, n * 128 + 128)
+        parts = []
+        for head in (2 * n, 2 * n + 1):
+            q, h = head // 3, head % 3
+            parts.append(
+                (own[q, :, 384 + h * 128 : 512 + h * 128], own[q, :, h * 128 : h * 128 + 128])
+            )
+        (qo_a, kv_a), (qo_b, kv_b) = parts
+        g_in[0, :, 0, cols] = jnp.concatenate([qo_a[:, 0:64], qo_b[:, 0:64]], axis=1)[0:12]
+        g_in[1, :, 0, cols] = jnp.concatenate([kv_a[:, 0:64], kv_b[:, 0:64]], axis=1)[0:12]
+        g_in[2, :, 0, cols] = jnp.concatenate([kv_a[:, 64:128], kv_b[:, 64:128]], axis=1)[0:12]
+        mixed = jnp.concatenate([qo_a[:, 64:128], qo_b[:, 64:128]], axis=1)
+        g_out[:, 0, cols] = mixed[0:12]
+    for q in range(2):
+        cols = slice(q * 768, q * 768 + 768)
+        g_up[:, 0, cols] = own[q, 0:12, 768:1536]
+        g_down[:, 0, cols] = own[q, 0:12, 1536:2304]
+    row0, row1 = own[0, 12:13, 0:128], own[1, 12:13, 0:128]
+    vec = row0 + row1 + far[12:13, :]
+    lane = lax.broadcasted_iota(jnp.int32, (8, 128), 1)
+    line = lax.broadcasted_iota(jnp.int32, (8, 128), 0)
+
+    def pick(row, start, width, stride):
+        begin = start + line * stride
+        return jnp.where((lane >= begin) & (lane < begin + width), row, 0.0)
+
+    norms = lax.dot_general(pick(vec, 6 * t, 6, 12), ends[0:6, :], NT, **exact)
+    g_gain[...] = norms[0:2]
+    g_row[...] = norms[2:6]
+    heads = lax.dot_general(pick(row0, 72, 3, 3), ends[8:14, :], NT, **exact)
+    heads += lax.dot_general(pick(row1, 72, 3, 3), ends[16:22, :], NT, **exact)
+    g_qv[...] = heads[0:2]
+    hidden_rows = jnp.where(line < 3, pick(row0, 78, 4, 4), pick(row1, 66, 4, 4))
+    g_fc[...] = lax.dot_general(fours[...], hidden_rows, NT, **exact)[:, 0:6]
+
+
+def finish(*args):
+    return pl.pallas_call(
+        finish_kernel,
+        out_shape=[
+            jax.ShapeDtypeStruct(dims, F32)
+            for dims in (
+                (128, 768),
+                (3, 12, 1, 384),
+                (2, 6),
+                (12, 1, 384),
+                (12, 1, 1536),
+                (4, 6),
+                (12, 1, 1536),
+                (2, 6),
+                (4, 6),
+            )
+        ],
+        in_specs=[VM] * len(args),
+        out_specs=[VM] * 9,
+        compiler_params=pltpu.CompilerParams(vmem_limit_bytes=LIMIT),
+        name="finish",
+    )(*args)
 
 
 def body(
@@ -763,53 +916,30 @@
     row_bias,
     cotangent,
 ):
-    dp = lax.axis_index("dp")
-    c, k, t = dp // 2, dp % 2, lax.axis_index("tensor")
-    spread, select, row12 = jnp.asarray(SPREAD, BF), jnp.asarray(SELECT, BF), jnp.asarray(ROW12, BF)
-    put = jnp.asarray(PUT)
-    fetch = jnp.asarray(FETCH) + k * jnp.asarray(FETCH_STEP)
-
-    parts = attn_in[0].reshape(3, 12, 6, 64)
-    proj = out_proj[0].T.reshape(12, 6, 64)
-    kv_w = jnp.stack([parts[1], parts[2]], axis=2).reshape(12, 2, 384)
-    qo_w = jnp.stack([parts[0], proj], axis=2).reshape(12, 2, 384)
-    up_w = fc_in[0].reshape(12, 2, 768)
-    down_w = fc_out[0].T.reshape(12, 2, 768)
-    pay = jnp.concatenate([kv_w, qo_w, up_w, down_w], axis=-1).transpose(1, 0, 2)
-    norms = jnp.concatenate([ln_gain.reshape(1, 12), row_bias.reshape(1, 24)], axis=1)
-    blank = jnp.zeros((1, 64), BF)
-    norms = jnp.pad(norms, ((0, 0), (0, 28)))
-    norms = jnp.where(
-        t == 0,
-        jnp.concatenate([norms, blank], axis=1),
-        jnp.concatenate([blank, norms], axis=1),
-    )
-    others = jnp.concatenate([qv_bias.reshape(1, 12), fc_bias.reshape(1, 24)], axis=1)
-    others = jnp.pad(others, ((0, 0), (0, 92)))
-    extra = jnp.pad(jnp.concatenate([norms, others]), ((0, 2), (0, 2176)))[None]
-    pay = jnp.concatenate([pay, jnp.concatenate([extra, extra])], axis=1)
-    tile = jnp.pad(norms, ((12, 3), (0, 0)))
-    w, f0, f1, clip, near_tokens = gather_all(pay, tile, clip_bounds, tokens)
-    clip = clip.transpose(1, 0, 2).reshape(2, 512)
-    rows = w.reshape(64, 16, 768)[:, 12:14, 0:128]
-    base = (c - 3) * 512
-    lim = jnp.stack(
-        [
-            (clip[0, 0] - base) // 256,
-            (clip[1, 255] - base + 255) // 256,
-            (clip[0, 256] - base) // 256,
-            (clip[1, 511] - base + 255) // 256,
-            base,
-        ]
-    ).astype(jnp.int32)
+    spread, select, small_rows = [jnp.asarray(v, BF) for v in (SPREAD, SELECT, ROWS)]
+    w, f0, f1, clip, near_tokens = gather_all(
+        clip_bounds,
+        tokens,
+        attn_in[0],
+        out_proj[0].T,
+        fc_in[0],
+        fc_out[0].T,
+        ln_gain[0],
+        row_bias[0],
+        qv_bias.reshape(2, 6),
+        fc_bias[0].T,
+        jnp.asarray(PADS, BF),
+        jnp.asarray(PLACE, BF),
+        jnp.asarray(MASKS),
+    )
     vecs, w_attn, unit, near, query, mixed, lse, attn = front(
-        lim,
+        clip,
         clip,
         w.reshape(2, 512, 768),
-        rows[:, 0],
-        rows[:, 1],
+        small_rows,
         spread,
-        fetch,
+        jnp.asarray(FETCH),
+        jnp.asarray(FETCH_STEP),
         select,
         near_tokens.reshape(14, 256, 768),
     )
@@ -817,7 +947,7 @@
         attn.reshape(4, 128, 768), f0, f1, cotangent, tokens, vecs, select
     )
     near_back, grad_w = back(
-        lim,
+        clip,
         clip,
         query,
         full_attn.reshape(512, 768),
@@ -830,45 +960,28 @@
         sums,
         up_sum,
         spread,
-        put,
+        jnp.asarray(PUT),
         select,
-        row12,
+        small_rows[0],
     )
     back_one, own, far = return_all(
         near_back.reshape(7, 4, 128, 768), grad_w.reshape(2, 4, 4, 2, 16, 768), u0, u1
     )
-    _, unit_one, scale_one = normalize(tokens.astype(F32), vecs[0], vecs[2])
-    grad_tokens = grad_hidden_one + normalize_back(back_one, unit_one, scale_one, vecs[0])
-    vec = own[0, 12, 0:128] + own[1, 12, 0:128] + far[12]
-    vec = vec[0:72].reshape(6, 2, 6)
-    vec = jnp.where(t == 0, vec[:, 0], vec[:, 1])
-    grad_gain, grad_row = vec[0:2].reshape(1, 2, 6), vec[2:6].reshape(1, 4, 6)
-    grad_qv = own[:, 12, 72:78].reshape(2, 2, 3).transpose(1, 0, 2).reshape(1, 2, 6, 1)
-    grad_up_bias = own[:, 12, 78:90].reshape(1, 6, 4)
-    main = own[:, 0:12].transpose(1, 0, 2)
-    g_kv = main[:, :, 0:384].reshape(12, 6, 2, 64)
-    g_qo = main[:, :, 384:768].reshape(12, 6, 2, 64)
-    grad_in = jnp.stack(
-        [
-            g_qo[:, :, 0].reshape(12, 384),
-            g_kv[:, :, 0].reshape(12, 384),
-            g_kv[:, :, 1].reshape(12, 384),
-        ]
-    )[None]
-    grad_out = g_qo[:, :, 1].reshape(12, 384).T[None]
-    grad_fc_in = main[:, :, 768:1536].reshape(1, 12, 1536)
-    grad_fc_out = main[:, :, 1536:2304].reshape(12, 1536).T[None]
+    grads = finish(
+        own, far, back_one, grad_hidden_one, tokens, vecs, jnp.asarray(ENDS), jnp.asarray(FOURS)
+    )
+    grad_tokens, g_in, g_qv, g_out, g_up, g_fc, g_down, g_gain, g_row = grads
     return (
         output,
         grad_tokens,
-        grad_in,
-        grad_qv,
-        grad_out,
-        grad_fc_in,
-        grad_up_bias,
-        grad_fc_out,
-        grad_gain,
-        grad_row,
+        g_in.reshape(1, 3, 12, 384),
+        g_qv.reshape(1, 2, 6, 1),
+        g_out.reshape(12, 384).T[None],
+        g_up.reshape(1, 12, 1536),
+        g_fc.T[None],
+        g_down.reshape(12, 1536).T[None],
+        g_gain[None],
+        g_row[None],
     )
 
 

time: 286 us -> 264 us (0.923)
  local copies, waits for them, and re-layouts: 22.2 us -> 3.63 us
  other arithmetic: 4.77 us -> 0 us
  Pallas kernels: 254 us -> 257 us
  between operations: 3.62 us -> 0.68 us
    slice x16 -> x0, local copies, waits for them, and re-layouts: 7.12 us -> none  [the longest x1 1.28 us: body(): clip[1, 511] - base + 255]
    reshape x15 -> x0, local copies, waits for them, and re-layouts: 5.1 us -> none  [the longest x2 0.84 us: body(): down_w = fc_out[0].T.reshape(12, 2, 768)]
    add x3 -> x0, other arithmetic: 3.07 us -> none  [the longest x1 1.37 us: body(): fetch = jnp.asarray(FETCH) + k * jnp.asarray(FETCH_STEP)]
    another operation x13 -> x0, local copies, waits for them, and re-layouts: 3.01 us -> none  [the longest x2 0.89 us: body(): qo_w = jnp.stack([parts[0], proj], axis=2).reshape(12, 2, 384)]
where the time goes in v5:
time: 264 us; the launch traced here: 261 us
  Pallas kernels  257 us (97%)
  local copies, waits for them, and re-layouts  3.63 us (1%)
    pallas_call x3, Pallas kernels, comm_call(): pl.pallas_call(kernel, out_shape=out_shape, in_specs=[VM] * len(args), ou...  193 us
    pallas_call x1, Pallas kernels, back(): pl.pallas_call(back_kernel, out_shape=[jax.ShapeDtypeStruct((14, 256, 768...  31.1 us
    pallas_call x1, Pallas kernels, front(): pl.pallas_call(front_kernel, out_shape=[jax.ShapeDtypeStruct((8, 768), F3...  30 us

profile of v5, /device:TPU:1, one launch (start us, length us, event | category | flops | bytes accessed | tf_op | source)
XLA Modules:
  0.0 261.4 jit_solution(12571362382029330974)
XLA Ops:
  0.6 65.9 %gather_first.1 = (bf16[2,4,4,2,16,768]{5,4,3,2,1,0:T(8,128)(2,1)}, bf16[2,4,2,16,768]{4,3,2,1,0:T(8,128)(2,1)}, bf16[2,4,2,16,768]{4,3,2,1,0:T(8,128)(2,1)}, s3...) custom-call(s32[2,256]{1,0:T(2,128)} %clip.1, bf16[128,768]{1,0:T(8,128)(2,1)} %tok.5, bf16[3,12,384]{2,1,0:T(8,128)(2,1)} %bitcast.54, ...), custom_call_target="tpu_custom_call" | custom-call | tf_op jit(solution)/shard_map/gather_first/pallas_call | solution.py:52
  66.5 30.0 %front.1 = (f32[8,768]{1,0:T(8,128)}, bf16[768,768]{1,0:T(8,128)(2,1)}, bf16[14,256,768]{2,1,0:T(8,128)(2,1)}, bf16[14,256,384]{2,1,0:T(8,128)(2,1)}, bf16[512,3...) custom-call(s32[2,2,256]{2,1,0:T(2,128)} %get-tuple-element.44.ends.clip, ...), custom_call_target="tpu_custom_call" | custom-call | tf_op jit(solution)/shard_map/front/pallas_call | solution.py:699
  96.5 64.3 %mid.1 = (bf16[128,768]{1,0:T(8,128)(2,1)}, f32[128,768]{1,0:T(8,128)}, bf16[4,128,768]{2,1,0:T(8,128)(2,1)}, f32[4,768]{1,0:T(4,128)}, f32[1,768]{1,0:T(1,128)}...) custom-call(bf16[4,128,768]{2,1,0:T(8,128)(2,1)} %bitcast.49, ...), custom_call_target="tpu_custom_call" | custom-call | tf_op jit(solution)/shard_map/mid/pallas_call | solution.py:52
  160.7 31.1 %back.1 = (bf16[14,256,768]{2,1,0:T(8,128)(2,1)}, bf16[2,512,768]{2,1,0:T(8,128)(2,1)}) custom-call(s32[2,2,256]{2,1,0:T(2,128)} %get-tuple-element.44.ends.clip, s32[2,2,256]{2,1,0:T(2,128)} %get-tuple-element.44.ends.clip, bf16[512,384]{1,0:T(8,128)(2,1)} %get-tuple-element.52.q, bf16[512,768]{1,0:T(8,128)(2,1)} %bitcast.48, ...), custom_call_target="tpu_custom_call" | custom-call | tf_op jit(solution)/shard_map/back/pallas_call | solution.py:810
  191.9 0.0 copy-start
  191.9 63.4 %return_all.1 = (f32[128,768]{1,0:T(8,128)}, f32[2,16,2304]{2,1,0:T(8,128)}, f32[16,128]{1,0:T(8,128)}) custom-call(bf16[7,4,128,768]{3,2,1,0:T(8,128)(2,1)} %bitcast.44, bf16[2,4,4,2,16,768]{5,4,3,2,1,0:T(8,128)(2,1)} %bitcast.46, bf16[2,2,16,768]{3,2,1,0:T(8,128)(2,1)} %get-tuple-element.63.u0, bf16[2,2,16,768]{3,2,1,0:T(8,128)(2,1)} %get-tuple-element.64.u1), custom_call_target="tpu_custom_call" | custom-call | tf_op jit(solution)/shard_map/return_all/pallas_call | solution.py:52
  255.2 2.5 finish.1
  257.7 0.7 copy.40
  258.4 0.6 copy.33
  259.1 0.9 copy.39
  260.0 0.7 copy.34
  260.7 0.0 copy-done
  260.7 0.7 copy.42
Async XLA Ops:
  191.9 68.8 %copy-start = (bf16[128,768]{1,0:T(8,128)(2,1)S(1)}, bf16[128,768]{1,0:T(8,128)(2,1)}, u32[]{:S(2)}) copy-start(bf16[128,768]{1,0:T(8,128)(2,1)} %get-tuple-element.98) | copy-start | bytes 589828

commit v6 on v5

--- a/solution.py
+++ b/solution.py
@@ -15,7 +15,6 @@
 VM = pl.BlockSpec(memory_space=pltpu.VMEM)
 SM = pl.BlockSpec(memory_space=pltpu.SMEM)
 DMA = pltpu.SemaphoreType.DMA
-LIMIT = 56 * 2**20
 NT = (((1,), (1,)), ((), ()))
 TN = (((0,), (0,)), ((), ()))
 
@@ -47,22 +46,22 @@
     )
 
 
-def comm_call(kernel, out_shape, scratch, cid, name, args):
+def comm_call(kernel, out_shape, scratch, cid, name, args, room, place=VM):
     single = not isinstance(out_shape, (list, tuple))
     return pl.pallas_call(
         kernel,
         out_shape=out_shape,
-        in_specs=[VM] * len(args),
+        in_specs=[place] * len(args),
         out_specs=VM if single else [VM] * len(out_shape),
         scratch_shapes=scratch,
         compiler_params=pltpu.CompilerParams(
-            collective_id=cid, has_side_effects=True, vmem_limit_bytes=LIMIT
+            collective_id=cid, has_side_effects=True, vmem_limit_bytes=room * 2**20
         ),
         name=name,
     )(*args)
 
 
-def spots():
+def neighbours():
     z, y, x, k, t = coords()
     xs = [device(z, y, (x + d) % 4, k, t) for d in (1, 2, 3)]
     ys = [device(z, (y + d) % 4, x, k, t) for d in (1, 2, 3)]
@@ -87,12 +86,10 @@
         return made
 
 
-def build_rows(attn_w, proj, up, down, gain, row, qv, fc, pads, place, masks, t, pay, tile):
-    def tall(v):
-        return matmul(pads[...], v)
-
-    query, keys, values = [tall(attn_w[i]) for i in range(3)]
-    mixed, up_rows, down_rows = tall(proj[...]), tall(up[...]), tall(down[...])
+def build_small(gain, row, qv, fc, first, t, tile):
+    place = first[0:14, :].astype(BF)
+    masks = first[16:28, :]
+
     norms = jnp.sum(matmul(gain[...], place[0:6, :]) * masks[0:2, :], axis=0, keepdims=True)
     norms += jnp.sum(matmul(row[...], place[0:6, :]) * masks[2:6, :], axis=0, keepdims=True)
     lane = lax.broadcasted_iota(jnp.int32, (16, 128), 1)
@@ -102,16 +99,26 @@
     mine = (line == 12) & (lane >= 64 * t) & (lane < 64 * t + 64)
     small = jnp.where(mine, norms, 0.0)
     tile[...] = small.astype(BF)
-    small = small + jnp.where(line == 13, others, 0.0)
+    return small + jnp.where(line == 13, others, 0.0)
+
+
+def build_rows(attn_w, proj, up, down, small, first, pay):
+    pads = first[32:48, 0:12].astype(BF)
+
+    def tall(v):
+        return matmul(pads, v)
+
+    query, keys, values = [tall(attn_w[i]) for i in range(3)]
+    mixed, up_rows, down_rows = tall(proj[...]), tall(up[...]), tall(down[...])
     for q in range(2):
         for h in range(3):
             n = slice((q * 3 + h) * 64, (q * 3 + h) * 64 + 64)
-            first = jnp.concatenate([keys[:, n], values[:, n]], axis=1)
+            pair = jnp.concatenate([keys[:, n], values[:, n]], axis=1)
             if h == 0:
-                first = first + small
-            pay[q, :, h * 128 : h * 128 + 128] = first.astype(BF)
-            second = jnp.concatenate([query[:, n], mixed[:, n]], axis=1)
-            pay[q, :, 384 + h * 128 : 512 + h * 128] = second.astype(BF)
+                pair = pair + small
+            pay[q, :, h * 128 : h * 128 + 128] = pair.astype(BF)
+            pair = jnp.concatenate([query[:, n], mixed[:, n]], axis=1)
+            pay[q, :, 384 + h * 128 : 512 + h * 128] = pair.astype(BF)
         pay[q, :, 768:1536] = up_rows[:, q * 768 : q * 768 + 768].astype(BF)
         pay[q, :, 1536:2304] = down_rows[:, q * 768 : q * 768 + 768].astype(BF)
 
@@ -120,10 +127,24 @@
 
 
 def gather_kernel(
-    clip, tok, attn_w, proj, up, down, gain, row, qv, fc, pads, place, masks,
-    w, f0, f1, clip_out, tk, pay_s, tile, tile_in, ws, send, recv,
+    clip, tok, cot, attn_h, proj_h, up_h, down_h, gain_h, row_h, qv_h, fc_h, first_h,
+    ones_h, spots_h, last_h,
+    w, f0, f1, clip_out, tk, tok_out, cot_out, ones, spots, last,
+    attn_w, proj, up, down, gain, row, qv, fc, first,
+    pay_s, tile, tile_in, ws, send, recv, local,
 ):
-    (z, y, x, k, t), xs, ys, core, far, low, ring = spots()
+    stages = []
+
+    def stage(src, dst):
+        stages.append(pltpu.make_async_copy(src, dst, local.at[len(stages)]))
+        stages[-1].start()
+
+    for src, dst in (
+        (gain_h, gain), (row_h, row), (qv_h, qv), (fc_h, fc), (first_h, first),
+        (attn_h, attn_w), (proj_h, proj), (up_h, up), (down_h, down),
+    ):
+        stage(src, dst)
+    (z, y, x, k, t), xs, ys, core, far, low, ring = neighbours()
     copy = Copies(send, recv)
     mine, other = k * 2 + t, k * 2 + 1 - t
     greet(xs + ys + [core, far, low] + ring)
@@ -131,27 +152,38 @@
     order = (4, 5, 2, 3, 0, 1)
     pushes = {i: copy(tok, tk.at[3 - RING[i], mine], ring[i]) for i in order}
     done = [copy(tok, tk.at[3, mine], core), copy(clip, clip_out.at[k], core)]
-    build_rows(attn_w, proj, up, down, gain, row, qv, fc, pads, place, masks, t, pay_s, tile)
+    stage(tok, tk.at[3, mine])
+    stage(clip, clip_out.at[k])
+    for pair in ((tok, tok_out), (cot, cot_out), (ones_h, ones), (spots_h, spots), (last_h, last)):
+        stage(*pair)
+    for c in stages[0:9]:
+        c.wait()
+    small = build_small(gain, row, qv, fc, first, t, tile)
     c_tile = copy(tile, tile_in, far)
-    clip_out[k] = clip[...]
-    tk[3, mine] = tok[...]
+    build_rows(attn_w, proj, up, down, small, first, pay_s)
     to_far = {}
+
+    def to_core(slot, which):
+        done.append(copy(tk.at[slot, which], tk.at[slot, which], core))
 
     def pass_on(i):
         pushes[i].wait_recv()
-        a = tk.at[3 - RING[i], mine]
-        to_far[i] = copy(a, a, far)
-        done.append(copy(a, a, core))
+        slot = 3 - RING[i]
+        to_far[i] = copy(tk.at[slot, mine], tk.at[slot, mine], far)
+        to_core(slot, mine)
 
     c_tile.wait()
     for q in range(2):
         pay_s[q, :, 0:128] = pay_s[q, :, 0:128] + tile_in[...]
     swap = copy(pay_s.at[1 - k], ws.at[z, k], core)
     ws[z, k] = pay_s[k]
+    for i in (4, 5):
+        pushes[i].wait_recv()
+        to_core(3 - RING[i], mine)
     swap.wait()
     c_low = copy(ws.at[z], ws.at[z], low)
-    pass_on(4)
-    pass_on(5)
+    pass_on(2)
+    pass_on(3)
     c_low.wait()
     w[:, y, x] = ws[:, :, :, 0:768]
     f0[:, x] = ws[:, :, :, 768:1536]
@@ -160,8 +192,14 @@
     for i in range(3):
         phase.append(copy(ws.at[:, :, :, H0], w.at[:, y, x, :, :, H0], xs[i]))
         phase.append(copy(ws.at[:, :, :, H1], w.at[:, y, x, :, :, H1], ys[i]))
-    pass_on(2)
-    pass_on(3)
+    pass_on(0)
+    pass_on(1)
+    own_far.wait_recv()
+    beyond = []
+    for i in (4, 5):
+        slot = 3 - RING[i]
+        beyond.append((slot, copy(tk.at[3, other], tk.at[slot, other], ring[i])))
+    to_core(3, other)
     for c in phase:
         c.wait()
     rest = []
@@ -170,22 +208,22 @@
         rest.append(copy(a, a, ys[i]))
         b = w.at[:, :, x, :, :, H1]
         rest.append(copy(b, b, xs[i]))
-    pass_on(0)
-    pass_on(1)
     for i in range(3):
         rest.append(copy(ws.at[:, :, :, pl.ds(768, 768)], f0.at[:, x], xs[i]))
         rest.append(copy(ws.at[:, :, :, pl.ds(1536, 768)], f1.at[:, y], ys[i]))
-    own_far.wait_recv()
-    done.append(copy(tk.at[3, other], tk.at[3, other], core))
-    for i in order:
+    for i in (2, 3, 0, 1):
         to_far[i].wait_recv()
-        a = tk.at[3 - RING[i], other]
-        done.append(copy(a, a, core))
+        to_core(3 - RING[i], other)
+    for slot, c in beyond:
+        c.wait_recv()
+        to_core(slot, other)
+        c.wait_send()
     for i in order:
         pushes[i].wait_send()
+    for i in (2, 3, 0, 1):
         to_far[i].wait_send()
     own_far.wait_send()
-    for c in rest + done:
+    for c in rest + done + stages[9:]:
         c.wait()
 
 
@@ -198,18 +236,27 @@
             jax.ShapeDtypeStruct((2, 4, 2, 16, 768), BF),
             jax.ShapeDtypeStruct((2, 2, 256), jnp.int32),
             jax.ShapeDtypeStruct((7, 4, 128, 768), BF),
+            jax.ShapeDtypeStruct((128, 768), BF),
+            jax.ShapeDtypeStruct((128, 768), BF),
+            jax.ShapeDtypeStruct((640, 768), BF),
+            jax.ShapeDtypeStruct((24, 768), jnp.int32),
+            jax.ShapeDtypeStruct((32, 128), F32),
         ],
-        [
+        [pltpu.VMEM(v.shape, v.dtype) for v in args[3:12]]
+        + [
             pltpu.VMEM((2, 16, 2304), BF),
             pltpu.VMEM((16, 128), BF),
             pltpu.VMEM((16, 128), BF),
             pltpu.VMEM((2, 2, 16, 2304), BF),
             DMA((50,)),
             DMA((50,)),
+            DMA((16,)),
         ],
         0,
         "gather_first",
         args,
+        54,
+        pl.BlockSpec(memory_space=pltpu.MemorySpace.HBM),
     )
 
 
@@ -283,12 +330,12 @@
 
 
 def mid_kernel(
-    p, f0, f1, cot, tok, vecs, select,
-    output, e1, dr_full, sums, up_sum, u0, u1,
+    p, f0, f1, cot, tok, vecs, ones,
+    output, e1, dr_full, sums, up_sum, s0, s1,
     got, mid, got_far, p0, p1, w_up, w_down, b_full, cot_full, dg, active, du_full,
-    pr, got_two, mid_two, far_two, dr, g0, g1, b0, b1, s0, s1, a0, a1, send, recv,
+    pr, got_two, mid_two, far_two, dr, g0, g1, b0, b1, send, recv,
 ):
-    (z, y, x, k, t), xs, ys, core, far, low, ring = spots()
+    (z, y, x, k, t), xs, ys, core, far, low, ring = neighbours()
     copy = Copies(send, recv)
     greet(xs + ys + [core, far])
     mine, across, beside, both = k * 2 + t, k * 2 + 1 - t, 2 - 2 * k + t, 3 - 2 * k - t
@@ -319,8 +366,8 @@
         c.wait()
     for i in range(2):
         rows = slice(i * 384, i * 384 + 384)
-        w_up[rows, :] = matmul(select[...], p0[i].reshape(512, 768)).astype(BF)
-        w_down[rows, :] = matmul(select[...], p1[i].reshape(512, 768)).astype(BF)
+        w_up[rows, :] = matmul(ones[SELECT], p0[i].reshape(512, 768)).astype(BF)
+        w_down[rows, :] = matmul(ones[SELECT], p1[i].reshape(512, 768)).astype(BF)
 
     @pl.loop(0, 4)
     def _(i):
@@ -351,34 +398,34 @@
     feed(both)
     second = copy(pr.at[:, both], got_two.at[:, 1 - t], core)
     second.wait()
-    two = []
     for i in range(2):
         v = pr[i, across].astype(F32) + got_two[i, 1 - t].astype(F32)
         mid_two[i] = v.astype(BF)
-        two.append(copy(mid_two.at[i], far_two.at[i], far))
+    two = {1: copy(mid_two.at[1], far_two.at[1], far)}
     b_rows, du_rows = b_full[...].reshape(512, 768), du_full[...].reshape(512, 768)
     for i in range(2):
         cols = slice(i * 384, i * 384 + 384)
         g = matmul_tn(b_rows[:, cols], du_rows).astype(BF)
-        g0[i] = matmul_tn(select[...], g).astype(BF).reshape(4, 4, 2, 16, 768)
+        g0[i] = matmul_tn(ones[SELECT], g).astype(BF).reshape(4, 4, 2, 16, 768)
     c_rows, a_rows = cot_full[...].reshape(512, 768), active[...].reshape(512, 768)
     for i in range(2):
         cols = slice(i * 384, i * 384 + 384)
         g = matmul_tn(c_rows[:, cols], a_rows).astype(BF)
-        g1[i] = matmul_tn(select[...], g).astype(BF).reshape(4, 4, 2, 16, 768)
+        g1[i] = matmul_tn(ones[SELECT], g).astype(BF).reshape(4, 4, 2, 16, 768)
     over = spread_first(copy, g0, g1, b0, b1, x, y, xs, ys)
     first.wait()
-    pair = []
-    for i in range(2):
+
+    def summed(i):
         v = pr[i, mine].astype(F32) + got_two[i, t].astype(F32)
         two[i].wait()
-        pair.append(v + far_two[i].astype(F32))
+        return v + far_two[i].astype(F32)
+
+    back_rows = summed(1)
     hidden = e1[...]
-    output[...] = (hidden + pair[0] + vecs[5:6, :]).astype(BF)
     centred = hidden - jnp.mean(hidden, axis=-1, keepdims=True)
     scale = lax.rsqrt(jnp.mean(centred * centred, axis=-1, keepdims=True) + EPS)
     unit = centred * scale
-    w = pair[1] * vecs[1:2, :]
+    w = back_rows * vecs[1:2, :]
     mean_w = jnp.mean(w, axis=-1, keepdims=True)
     mean_wu = jnp.mean(w * unit, axis=-1, keepdims=True)
     cot_f = cot[...].astype(F32)
@@ -387,17 +434,17 @@
     low_grad = grad.astype(BF)
     dr[...] = low_grad
     finish_rows = exchange_rows(copy, dr, dr_full, k, t, core, far)
-    sums[0:1, :] = jnp.sum(pair[1] * unit, axis=0, keepdims=True)
+    two[0] = copy(mid_two.at[0], far_two.at[0], far)
+    sums[0:1, :] = jnp.sum(back_rows * unit, axis=0, keepdims=True)
     sums[1:2, :] = jnp.sum(low_grad.astype(F32), axis=0, keepdims=True)
-    sums[2:3, :] = jnp.sum(pair[1], axis=0, keepdims=True)
+    sums[2:3, :] = jnp.sum(back_rows, axis=0, keepdims=True)
     sums[3:4, :] = jnp.sum(cot_f, axis=0, keepdims=True)
+    finish_rows()
+    output[...] = (hidden + summed(0) + vecs[5:6, :]).astype(BF)
     add_first(g0, g1, b0, b1, s0, s1, x, y, *over)
-    over = spread_second(copy, s0, s1, a0, a1, x, y, xs, ys)
-    finish_rows()
-    add_second(s0, s1, a0, a1, u0, u1, x, y, *over)
-
-
-def mid(p, f0, f1, cot, tok, vecs, select):
+
+
+def mid(p, f0, f1, cot, tok, vecs, ones):
     rows = pltpu.VMEM((128, 768), BF)
     two = pltpu.VMEM((2, 128, 768), BF)
     four = pltpu.VMEM((4, 128, 768), BF)
@@ -411,29 +458,28 @@
             jax.ShapeDtypeStruct((4, 128, 768), BF),
             jax.ShapeDtypeStruct((4, 768), F32),
             jax.ShapeDtypeStruct((1, 768), F32),
-            jax.ShapeDtypeStruct((2, 2, 16, 768), BF),
-            jax.ShapeDtypeStruct((2, 2, 16, 768), BF),
+            jax.ShapeDtypeStruct((2, 4, 2, 16, 768), BF),
+            jax.ShapeDtypeStruct((2, 4, 2, 16, 768), BF),
         ],
         [two, rows, rows, piece, piece, square, square, four, four]
         + [pltpu.VMEM((4, 128, 768), F32), four, four]
         + [pltpu.VMEM((2, 4, 128, 768), BF), pltpu.VMEM((2, 2, 128, 768), BF), two, two, rows]
         + [piece, piece]
         + [pltpu.VMEM((3, 2, 4, 2, 16, 768), BF)] * 2
-        + [pltpu.VMEM((2, 4, 2, 16, 768), BF)] * 2
-        + [pltpu.VMEM((3, 2, 2, 16, 768), BF)] * 2
-        + [DMA((39,)), DMA((39,))],
+        + [DMA((33,)), DMA((33,))],
         1,
         "mid",
-        (p, f0, f1, cot, tok, vecs, select),
+        (p, f0, f1, cot, tok, vecs, ones),
+        26,
     )
 
 
 def return_kernel(
-    d, g, u0, u1, out, own, tile_out,
+    d, g, fs0, fs1, out, own, tile_out,
     got_core, v1, in1, e_send, got_far, r_send, got_ring,
-    b0, b1, s0, s1, a0, a1, v_0, v_1, z_in0, z_in1, z_in2, z_in3, res, tile, send, recv,
+    b0, b1, s0, s1, a0, a1, fa0, fa1, u0, u1, v_0, v_1, z_in0, z_in1, z_in2, z_in3, res, tile, send, recv,
 ):
-    (z, y, x, k, t), xs, ys, core, far, low, ring = spots()
+    (z, y, x, k, t), xs, ys, core, far, low, ring = neighbours()
     copy = Copies(send, recv)
     greet(xs + ys + [core, far, low] + ring)
     mine, across = k * 2 + t, k * 2 + 1 - t
@@ -441,7 +487,7 @@
     order = (4, 2, 5, 1, 6, 0, 3)
     to_core = {j: copy(d.at[j, pl.ds((1 - k) * 2, 2)], got_core.at[j], core) for j in order}
     g0, g1 = g.at[:, :, :, :, :, H0], g.at[:, :, :, :, :, H1]
-    fc_z = [copy(u0.at[1 - z], z_in0, low), copy(u1.at[1 - z], z_in1, low)]
+    fc_over = spread_second(copy, fs0, fs1, fa0, fa1, x, y, xs, ys)
     hop1, to_far = [], []
     over = spread_first(copy, g0, g1, b0, b1, x, y, xs, ys)
     for i, j in enumerate((4, 2)):
@@ -461,6 +507,8 @@
         r_send[i] = v.astype(BF)
         home.append(copy(r_send.at[i], got_ring.at[i], ring[i]))
 
+    add_second(fs0, fs1, fa0, fa1, u0, u1, x, y, *fc_over)
+    fc_z = [copy(u0.at[1 - z], z_in0, low), copy(u1.at[1 - z], z_in1, low)]
     send_home(0)
     send_home(1)
     add_first(g0, g1, b0, b1, s0, s1, x, y, *over)
@@ -499,7 +547,7 @@
     c_tile.wait()
 
 
-def return_all(d, g, u0, u1):
+def return_all(d, g, s0, s1):
     two = pltpu.VMEM((2, 2, 128, 768), BF)
     wide, slim = 512, 256
     return comm_call(
@@ -515,12 +563,14 @@
         + [pltpu.VMEM((3, 2, 4, 2, 16, n), BF) for n in (wide, slim)]
         + [pltpu.VMEM((2, 4, 2, 16, n), BF) for n in (wide, slim)]
         + [pltpu.VMEM((3, 2, 2, 16, n), BF) for n in (wide, slim)]
-        + [pltpu.VMEM((2, 2, 16, n), BF) for n in (wide, slim)]
+        + [pltpu.VMEM((3, 2, 2, 16, 768), BF)] * 2
+        + [pltpu.VMEM((2, 2, 16, n), BF) for n in (768, 768, wide, slim)]
         + [pltpu.VMEM((2, 16, n), BF) for n in (768, 768, wide, slim)]
-        + [pltpu.VMEM((2, 16, 2304), F32), pltpu.VMEM((16, 128), F32), DMA((36,)), DMA((36,))],
+        + [pltpu.VMEM((2, 16, 2304), F32), pltpu.VMEM((16, 128), F32), DMA((42,)), DMA((42,))],
         5,
         "return_all",
-        (d, g, u0, u1),
+        (d, g, s0, s1),
+        24,
     )
 
 
@@ -560,34 +610,24 @@
     ends = np.zeros((24, 128), np.float32)
     ends[0:6], ends[8:11], ends[19:22] = lane % 6 == np.arange(6)[:, None], three, three
     fours = (lane + 2) % 4 == np.arange(4)[:, None]
-    return (
-        spread,
-        np.stack(rows).astype(np.int32),
-        step,
-        np.stack(back).astype(np.int32),
-        select.astype(np.float32),
-        np.stack([row12, row13]).astype(np.float32),
-        pads.astype(np.float32),
-        place,
-        np.stack(masks).astype(np.float32),
-        ends,
-        fours.astype(np.float32),
-    )
-
-
-(
-    SPREAD,
-    FETCH,
-    FETCH_STEP,
-    PUT,
-    SELECT,
-    ROWS,
-    PADS,
-    PLACE,
-    MASKS,
-    ENDS,
-    FOURS,
-) = layout_tables()
+    ones = np.zeros((640, 768), np.float32)
+    ones[0:192] = spread.reshape(192, 768)
+    ones[192:576, 0:512] = select
+    ones[576:608, 0:512], ones[608:640, 0:512] = row12.T, row13.T
+    spots = np.concatenate([np.stack(rows), step, np.stack(back)]).astype(np.int32)
+    last = np.zeros((32, 128), np.float32)
+    last[0:24], last[24:28] = ends, fours
+    first = np.zeros((48, 128), np.float32)
+    first[0:14], first[16:28], first[32:48, 0:12] = place, np.stack(masks), pads
+    return ones, spots, last, first
+
+
+ONES, SPOTS, LAST, FIRST = layout_tables()
+SELECT = (slice(192, 576), slice(0, 512))
+
+
+def spread_of(ones, i):
+    return ones[64 * i : 64 * i + 64, :]
 
 
 def matmul(left, right):
@@ -603,7 +643,7 @@
 
 
 def allowed_pairs(clip, qb, j):
-    pos = first_key() + j * 256 + lax.broadcasted_iota(jnp.int32, (256, 256), 0)
+    pos = first_key() + j * 512 + lax.broadcasted_iota(jnp.int32, (512, 256), 0)
     return (pos >= clip[qb, 0:1, :]) & (pos < clip[qb, 1:2, :])
 
 
@@ -612,30 +652,32 @@
 
 
 def key_blocks(ends, qb):
-    first = (ends[qb, 0, 0] - first_key()) // 256
-    return first, (ends[qb, 1, 255] - first_key() + 255) // 256
+    first = (ends[qb, 0, 0] - first_key()) // 512
+    return first, (ends[qb, 1, 255] - first_key() + 511) // 512
 
 
 def front_kernel(
-    ends, clip, w, small_rows, spread, fetch, step_k, select, tk,
+    ends, clip, w, ones, spots, tk,
     vecs, w_attn, unit, kv, q, of, lse, attn,
 ):
     line = lax.broadcasted_iota(jnp.int32, (128, 768), 0)
     k = lax.axis_index("dp") % 2
     row12, row13 = [
-        jnp.concatenate([matmul_tn(small_rows[i], w[z, :, 0:128]) for z in range(2)]).astype(BF)
+        jnp.concatenate(
+            [matmul(ones[576 + 32 * i : 608 + 32 * i, 0:512], w[z, :, 0:128]) for z in range(2)]
+        ).astype(BF)
         for i in range(2)
     ]
-    wide = matmul_tn(row12, spread[0])
+    wide = matmul_tn(row12, spread_of(ones, 0))
     for p in range(6):
-        hit = line == fetch[p : p + 1, :]
+        hit = line == spots[p : p + 1, :]
         vecs[p : p + 1, :] = jnp.sum(jnp.where(hit, wide, 0.0), axis=0, keepdims=True)
     for p in (6, 7):
-        wide = matmul_tn(row13, spread[p - 5])
-        hit = line == fetch[p : p + 1, :] + k * step_k[p : p + 1, :]
+        wide = matmul_tn(row13, spread_of(ones, p - 5))
+        hit = line == spots[p : p + 1, :] + k * spots[p + 8 : p + 9, :]
         vecs[p : p + 1, :] = jnp.sum(jnp.where(hit, wide, 0.0), axis=0, keepdims=True)
     for z in range(2):
-        w_attn[z * 384 : z * 384 + 384, :] = matmul(select[...], w[z]).astype(BF)
+        w_attn[z * 384 : z * 384 + 384, :] = matmul(ones[SELECT], w[z]).astype(BF)
 
     def norm_rows(j):
         v = tk[j].astype(F32)
@@ -652,11 +694,10 @@
         unit[j] = u.astype(BF)
         kv[j] = (matmul(a, w_attn[:, 0:384]) + vecs[6:7, 0:384]).astype(BF)
 
-    low = (lax.broadcasted_iota(jnp.int32, (256, 384), 1) & 127) < 64
-    for qb in range(2):
-        _, a = norm_rows(6 + qb)
-        v = (matmul(a, w_attn[:, 384:768]) + vecs[6:7, 384:768]).astype(BF).astype(F32)
-        q[qb * 256 : qb * 256 + 256, :] = jnp.where(low, v * SCORE_SCALE, 0.0).astype(BF)
+    low = (lax.broadcasted_iota(jnp.int32, (512, 384), 1) & 127) < 64
+    _, a = norm_rows(3)
+    v = (matmul(a, w_attn[:, 384:768]) + vecs[6:7, 384:768]).astype(BF).astype(F32)
+    q[...] = jnp.where(low, v * SCORE_SCALE, 0.0).astype(BF)
 
     lane = lax.broadcasted_iota(jnp.int32, (256, 128), 1)
     for qb in range(2):
@@ -664,18 +705,23 @@
 
         def step(j, carry):
             ok = allowed_pairs(clip, qb, j)
+            keys = [kv[j, :, h * 128 : h * 128 + 128] for h in range(3)]
+            scores = [
+                jnp.where(ok, matmul_nt(keys[h], q[rows, h * 128 : h * 128 + 128]), NEGATIVE)
+                for h in range(3)
+            ]
+            tops = [
+                jnp.maximum(carry[h][0], jnp.max(scores[h], axis=0, keepdims=True))
+                for h in range(3)
+            ]
+            probs = [jnp.exp(scores[h] - tops[h]) for h in range(3)]
             new = []
             for h in range(3):
                 m, l, acc = carry[h]
-                cols = slice(h * 128, h * 128 + 128)
-                keys = kv[j, :, cols]
-                s = jnp.where(ok, matmul_nt(keys, q[rows, cols]), NEGATIVE)
-                top = jnp.maximum(m, jnp.max(s, axis=0, keepdims=True))
-                p = jnp.exp(s - top)
-                fade = jnp.exp(m - top)
-                l = l * fade + jnp.sum(p, axis=0, keepdims=True)
-                acc = acc * fade + matmul_tn(keys, p.astype(BF))
-                new.append((top, l, acc))
+                fade = jnp.exp(m - tops[h])
+                l = l * fade + jnp.sum(probs[h], axis=0, keepdims=True)
+                acc = acc * fade + matmul_tn(keys[h], probs[h].astype(BF))
+                new.append((tops[h], l, acc))
             return tuple(new)
 
         start = tuple(
@@ -701,32 +747,32 @@
         out_shape=[
             jax.ShapeDtypeStruct((8, 768), F32),
             jax.ShapeDtypeStruct((768, 768), BF),
-            jax.ShapeDtypeStruct((14, 256, 768), BF),
-            jax.ShapeDtypeStruct((14, 256, 384), BF),
+            jax.ShapeDtypeStruct((7, 512, 768), BF),
+            jax.ShapeDtypeStruct((7, 512, 384), BF),
             jax.ShapeDtypeStruct((512, 384), BF),
             jax.ShapeDtypeStruct((512, 384), F32),
             jax.ShapeDtypeStruct((3, 512), F32),
             jax.ShapeDtypeStruct((512, 768), BF),
         ],
-        in_specs=[SM] + [VM] * 8,
+        in_specs=[SM] + [VM] * 5,
         out_specs=[VM] * 8,
-        compiler_params=pltpu.CompilerParams(vmem_limit_bytes=LIMIT),
+        compiler_params=pltpu.CompilerParams(vmem_limit_bytes=16 * 2**20),
         name="front",
     )(*args)
 
 
 def back_kernel(
-    ends, clip, q, dr, of, kv, lse, unit, w_attn, vecs, sums, up_sum, spread, put, select, row12,
+    ends, clip, q, dr, of, kv, lse, unit, w_attn, vecs, sums, up_sum, ones, spots,
     d_out, grad, total, dox, delta, dq, ug,
 ):
     bounds = [key_blocks(ends, qb) for qb in range(2)]
     lane = lax.broadcasted_iota(jnp.int32, (256, 128), 1)
     high = (lax.broadcasted_iota(jnp.int32, (256, 384), 1) & 127) >= 64
 
-    @pl.loop(0, 14)
+    @pl.loop(0, 7)
     def _(j):
-        total[j] = jnp.zeros((256, 384), F32)
-        d_out[j] = jnp.zeros((256, 768), BF)
+        total[j] = jnp.zeros((512, 384), F32)
+        d_out[j] = jnp.zeros((512, 768), BF)
 
     for qb in range(2):
         rows = slice(qb * 256, qb * 256 + 256)
@@ -742,17 +788,17 @@
 
         def step(j, carry):
             ok = allowed_pairs(clip, qb, j)
-            new = []
+            cols = [slice(h * 128, h * 128 + 128) for h in range(3)]
+            keys = [kv[j, :, n] for n in cols]
+            scores = [jnp.where(ok, matmul_nt(keys[h], q[rows, cols[h]]), NEGATIVE) for h in range(3)]
+            grads = [matmul_nt(keys[h], dox[rows, cols[h]]) for h in range(3)]
+            probs = [jnp.exp(scores[h] - lse[h : h + 1, rows]) for h in range(3)]
+            ds = [(probs[h] * (grads[h] - delta[h : h + 1, rows])).astype(BF) for h in range(3)]
             for h in range(3):
-                cols = slice(h * 128, h * 128 + 128)
-                keys = kv[j, :, cols]
-                qh, dh = q[rows, cols], dox[rows, cols]
-                s = jnp.where(ok, matmul_nt(keys, qh), NEGATIVE)
-                p = jnp.exp(s - lse[h : h + 1, rows])
-                ds = (p * (matmul_nt(keys, dh) - delta[h : h + 1, rows])).astype(BF)
-                new.append(carry[h] + matmul_tn(keys, ds))
-                total[j, :, cols] += matmul(ds, qh) + matmul(p.astype(BF), dh)
-            return tuple(new)
+                total[j, :, cols[h]] += matmul(ds[h], q[rows, cols[h]]) + matmul(
+                    probs[h].astype(BF), dox[rows, cols[h]]
+                )
+            return tuple(carry[h] + matmul_tn(keys[h], ds[h]) for h in range(3))
 
         start = tuple(jnp.zeros((128, 256), F32) for _ in range(3))
         final = lax.fori_loop(bounds[qb][0], bounds[qb][1], step, start)
@@ -769,18 +815,16 @@
         return kv_sum + jnp.sum(z.astype(F32), axis=0, keepdims=True)
 
     kv_sum = lax.fori_loop(bounds[0][0], bounds[1][1], chunk, jnp.zeros((1, 384), F32))
-    for qb in range(2):
-        rows = slice(qb * 256, qb * 256 + 256)
-        own = matmul_nt(total[6 + qb].astype(BF), w_attn[:, 0:384])
-        d_out[6 + qb] = (own + matmul_nt(dq[rows, :], w_attn[:, 384:768])).astype(BF)
-        ug[:, 384:768] += matmul_tn(unit[6 + qb], dq[rows, :])
+    own = matmul_nt(total[3].astype(BF), w_attn[:, 0:384])
+    d_out[3] = (own + matmul_nt(dq[...], w_attn[:, 384:768])).astype(BF)
+    ug[:, 384:768] = matmul_tn(unit[3], dq[...])
     q_sum = jnp.sum(dq[...].astype(F32), axis=0, keepdims=True)
     z_sum = jnp.concatenate([kv_sum, q_sum], axis=1)
 
     line = lax.broadcasted_iota(jnp.int32, (128, 768), 0)
 
     def place(p, row):
-        return jnp.where(line == put[p : p + 1, :], row, 0.0)
+        return jnp.where(line == spots[p + 16 : p + 17, :], row, 0.0)
 
     columns = vecs[...].T
     gain_col, offset_col = columns[:, 0:1], columns[:, 2:3]
@@ -792,17 +836,17 @@
     own = place(0, both[0:1, :]) + place(2, both[1:2, :])
     for i, p in enumerate((1, 3, 4, 5)):
         own = own + place(p, sums[i : i + 1, :])
-    small = matmul_nt(spread[0], own.astype(BF))
-    small += matmul_nt(spread[1], place(6, z_sum).astype(BF))
-    small += matmul_nt(spread[2], place(7, up_sum[...]).astype(BF))
+    small = matmul_nt(spread_of(ones, 0), own.astype(BF))
+    small += matmul_nt(spread_of(ones, 1), place(6, z_sum).astype(BF))
+    small += matmul_nt(spread_of(ones, 2), place(7, up_sum[...]).astype(BF))
     small = small.astype(BF)
 
     ug[...] = ug[...] * gain_col + offset_col * z_sum
     ug[:, 384:768] += matmul_tn(dr[...], of[...].astype(BF))
     for i in range(2):
-        g = matmul_tn(select[...], ug[i * 384 : i * 384 + 384, :].astype(BF))
+        g = matmul_tn(ones[SELECT], ug[i * 384 : i * 384 + 384, :].astype(BF))
         grad[i] = g.astype(BF)
-        extra = matmul(row12[...], small[i * 32 : i * 32 + 32, :])
+        extra = matmul_tn(ones[576:608, 0:512], small[i * 32 : i * 32 + 32, :])
         grad[i, :, 0:128] = (g[:, 0:128] + extra).astype(BF)
 
 
@@ -810,25 +854,25 @@
     return pl.pallas_call(
         back_kernel,
         out_shape=[
-            jax.ShapeDtypeStruct((14, 256, 768), BF),
+            jax.ShapeDtypeStruct((7, 512, 768), BF),
             jax.ShapeDtypeStruct((2, 512, 768), BF),
         ],
         in_specs=[SM] + [VM] * (len(args) - 1),
         out_specs=[VM, VM],
         scratch_shapes=[
-            pltpu.VMEM((14, 256, 384), F32),
+            pltpu.VMEM((7, 512, 384), F32),
             pltpu.VMEM((512, 384), BF),
             pltpu.VMEM((3, 512), F32),
             pltpu.VMEM((512, 384), BF),
             pltpu.VMEM((768, 768), F32),
         ],
-        compiler_params=pltpu.CompilerParams(vmem_limit_bytes=LIMIT),
+        compiler_params=pltpu.CompilerParams(vmem_limit_bytes=22 * 2**20),
         name="back",
     )(*args)
 
 
 def finish_kernel(
-    own, far, back_one, e1, tok, vecs, ends, fours,
+    own, far, back_one, e1, tok, vecs, ends,
     tokens, g_in, g_qv, g_out, g_up, g_fc, g_down, g_gain, g_row,
 ):
     t = lax.axis_index("tensor")
@@ -876,7 +920,7 @@
     heads += lax.dot_general(pick(row1, 72, 3, 3), ends[16:22, :], NT, **exact)
     g_qv[...] = heads[0:2]
     hidden_rows = jnp.where(line < 3, pick(row0, 78, 4, 4), pick(row1, 66, 4, 4))
-    g_fc[...] = lax.dot_general(fours[...], hidden_rows, NT, **exact)[:, 0:6]
+    g_fc[...] = lax.dot_general(ends[24:28, :], hidden_rows, NT, **exact)[:, 0:6]
 
 
 def finish(*args):
@@ -898,7 +942,7 @@
         ],
         in_specs=[VM] * len(args),
         out_specs=[VM] * 9,
-        compiler_params=pltpu.CompilerParams(vmem_limit_bytes=LIMIT),
+        compiler_params=pltpu.CompilerParams(vmem_limit_bytes=16 * 2**20),
         name="finish",
     )(*args)
 
@@ -916,10 +960,10 @@
     row_bias,
     cotangent,
 ):
-    spread, select, small_rows = [jnp.asarray(v, BF) for v in (SPREAD, SELECT, ROWS)]
-    w, f0, f1, clip, near_tokens = gather_all(
+    w, f0, f1, clip, near_tokens, tokens, cotangent, ones, spots, last = gather_all(
         clip_bounds,
         tokens,
+        cotangent,
         attn_in[0],
         out_proj[0].T,
         fc_in[0],
@@ -928,23 +972,16 @@
         row_bias[0],
         qv_bias.reshape(2, 6),
         fc_bias[0].T,
-        jnp.asarray(PADS, BF),
-        jnp.asarray(PLACE, BF),
-        jnp.asarray(MASKS),
+        jnp.asarray(FIRST),
+        jnp.asarray(ONES, BF),
+        jnp.asarray(SPOTS),
+        jnp.asarray(LAST),
     )
     vecs, w_attn, unit, near, query, mixed, lse, attn = front(
-        clip,
-        clip,
-        w.reshape(2, 512, 768),
-        small_rows,
-        spread,
-        jnp.asarray(FETCH),
-        jnp.asarray(FETCH_STEP),
-        select,
-        near_tokens.reshape(14, 256, 768),
-    )
-    output, grad_hidden_one, full_attn, sums, up_sum, u0, u1 = mid(
-        attn.reshape(4, 128, 768), f0, f1, cotangent, tokens, vecs, select
+        clip, clip, w.reshape(2, 512, 768), ones, spots, near_tokens.reshape(7, 512, 768)
+    )
+    output, grad_hidden_one, full_attn, sums, up_sum, s0, s1 = mid(
+        attn.reshape(4, 128, 768), f0, f1, cotangent, tokens, vecs, ones
     )
     near_back, grad_w = back(
         clip,
@@ -959,16 +996,14 @@
         vecs,
         sums,
         up_sum,
-        spread,
-        jnp.asarray(PUT),
-        select,
-        small_rows[0],
+        ones,
+        spots,
     )
     back_one, own, far = return_all(
-        near_back.reshape(7, 4, 128, 768), grad_w.reshape(2, 4, 4, 2, 16, 768), u0, u1
+        near_back.reshape(7, 4, 128, 768), grad_w.reshape(2, 4, 4, 2, 16, 768), s0, s1
     )
     grads = finish(
-        own, far, back_one, grad_hidden_one, tokens, vecs, jnp.asarray(ENDS), jnp.asarray(FOURS)
+        own, far, back_one, grad_hidden_one, tokens, vecs, last
     )
     grad_tokens, g_in, g_qv, g_out, g_up, g_fc, g_down, g_gain, g_row = grads
     return (

time: 264 us -> 222 us (0.84); the launches traced: 261 us -> 222 us
  Pallas kernels: 257 us -> 212 us
  local copies, waits for them, and re-layouts: 3.63 us -> 8.78 us
    pallas_call x4, Pallas kernels: 225 us -> 196 us  [the longest x3 175 us: comm_call(): pl.pallas_call(kernel, out_shape=out_shape, in_specs=[place] * len(args),...]
    pallas_call x1, Pallas kernels: 30 us -> 15 us  [front(): pl.pallas_call(front_kernel, out_shape=[jax.ShapeDtypeStruct((8, 768), F3...]
    unnamed x7 -> x31, local copies, waits for them, and re-layouts: 3.63 us -> 8.78 us
where the time goes in v6:
time: 222 us
  Pallas kernels  212 us (95%)
  local copies, waits for them, and re-layouts  8.78 us (4%)
    pallas_call x3, Pallas kernels, comm_call(): pl.pallas_call(kernel, out_shape=out_shape, in_specs=[place] * len(args),...  175 us
    pallas_call x1, Pallas kernels, back(): pl.pallas_call(back_kernel, out_shape=[jax.ShapeDtypeStruct((7, 512, 768)...  21.2 us
    pallas_call x1, Pallas kernels, front(): pl.pallas_call(front_kernel, out_shape=[jax.ShapeDtypeStruct((8, 768), F3...  15 us
    unnamed x31, local copies, waits for them, and re-layouts  8.78 us

profile of v6, /device:TPU:1, one launch (start us, length us, event | category | flops | bytes accessed | tf_op | source)
XLA Modules:
  0.0 222.0 jit_solution(3643783526597775324)
XLA Ops:
  0.6 62.1 %gather_first.1 = (bf16[2,4,4,2,16,768]{5,4,3,2,1,0:T(8,128)(2,1)}, bf16[2,4,2,16,768]{4,3,2,1,0:T(8,128)(2,1)}, bf16[2,4,2,16,768]{4,3,2,1,0:T(8,128)(2,1)}, s3...) custom-call(s32[2,256]{1,0:T(2,128)} %clip.1, ...), custom_call_target="tpu_custom_call" | custom-call | tf_op jit(solution)/shard_map/gather_first/pallas_call | solution.py:51
  62.8 0.0 copy-start
  62.8 1.2 copy-done
  64.0 0.0 copy-start.2
  64.0 2.6 %copy-done.2 = bf16[7,4,128,768]{3,2,1,0:T(8,128)(2,1)S(1)} copy-done((bf16[7,4,128,768]{3,2,1,0:T(8,128)(2,1)S(1)}, bf16[7,4,128,768]{3,2,1,0:T(8,128)(2,1)}, u32[]{:S(2)}) %copy-start.2) | copy-done | bytes 5505048
  66.6 0.0 copy-start.3
  66.6 1.4 copy-done.3
  68.0 0.0 copy-start.7
  68.0 0.9 copy-done.7
  68.8 0.0 copy-start.10
  68.8 0.7 copy-done.10
  69.5 0.0 copy-start.1
  69.5 0.0 copy-start.4
  69.5 0.0 copy-start.5
  69.5 0.0 copy-start.6
  69.5 0.0 copy-start.9
  69.6 15.0 %front.1 = (f32[8,768]{1,0:T(8,128)S(1)}, bf16[768,768]{1,0:T(8,128)(2,1)S(1)}, bf16[7,512,768]{2,1,0:T(8,128)(2,1)S(1)}, bf16[7,512,384]{2,1,0:T(8,128)(2,1)S(1...) custom-call(s32[2,2,256]{2,1,0:T(2,128)S(1)} %copy-done.10, ...), custom_call_target="tpu_custom_call" | custom-call | tf_op jit(solution)/shard_map/front/pallas_call | solution.py:745
  84.6 0.0 copy-start.8
  84.6 0.0 copy-start.11
  84.6 0.0 copy-done.1
  84.6 0.0 copy-done.4
  84.6 0.0 copy-done.5
  84.7 0.0 copy-done.6
  84.7 0.0 copy-done.9
  84.7 56.0 %mid.1 = (bf16[128,768]{1,0:T(8,128)(2,1)S(1)}, f32[128,768]{1,0:T(8,128)S(1)}, bf16[4,128,768]{2,1,0:T(8,128)(2,1)S(1)}, f32[4,768]{1,0:T(4,128)S(1)}, f32[1,76...) custom-call(bf16[4,128,768]{2,1,0:T(8,128)(2,1)S(1)} %bitcast.49, ...), custom_call_target="tpu_custom_call" | custom-call | tf_op jit(solution)/shard_map/mid/pallas_call | solution.py:51
  140.7 0.0 copy-done.8
  140.7 0.0 copy-done.11
  140.7 21.2 %back.1 = (bf16[7,512,768]{2,1,0:T(8,128)(2,1)S(1)}, bf16[2,512,768]{2,1,0:T(8,128)(2,1)S(1)}) custom-call(s32[2,2,256]{2,1,0:T(2,128)S(1)} %copy-done.11, s32[2,2,256]{2,1,0:T(2,128)S(1)} %copy-done.11, bf16[512,384]{1,0:T(8,128)(2,1)S(1)} %get-tuple-element.61.q, bf16[512,768]{1,0:T(8,128)(2,1)S(1)} %bitcast.48, f32[512,384]{1,0:T(8,128)S(1)} %get-tuple-element.63.of, ...), custom_call_target="tpu_custom_call" | custom-call | tf_op jit(solution)/shard_map/back/pallas_call | solution.py:854
  161.9 0.0 copy-start.12
  161.9 56.9 %return_all.1 = (f32[128,768]{1,0:T(8,128)S(1)}, f32[2,16,2304]{2,1,0:T(8,128)S(1)}, f32[16,128]{1,0:T(8,128)S(1)}) custom-call(bf16[7,4,128,768]{3,2,1,0:T(8,128)(2,1)S(1)} %bitcast.45, bf16[2,4,4,2,16,768]{5,4,3,2,1,0:T(8,128)(2,1)S(1)} %bitcast.47, bf16[2,4,2,16,768]{4,3,2,1,0:T(8,128)(2,1)S(1)} %get-tuple-element.72.fs0, ...), custom_call_target="tpu_custom_call" | custom-call | tf_op jit(solution)/shard_map/return_all/pallas_call | solution.py:51
  218.8 0.0 copy-done.12
  218.8 1.1 finish.1
  220.0 0.6 copy.26
  220.6 0.7 copy.27
  221.3 0.7 copy.35
  (2 shorter events, 0.0 us)
Async XLA Ops:
  62.8 1.2 copy-start
  64.0 2.6 %copy-start.2 = (bf16[7,4,128,768]{3,2,1,0:T(8,128)(2,1)S(1)}, bf16[7,4,128,768]{3,2,1,0:T(8,128)(2,1)}, u32[]{:S(2)}) copy-start(bf16[7,4,128,768]{3,2,1,0:T(8,128)(2,1)} %get-tuple-element.53) | copy-start | bytes 16515076
  66.6 1.4 copy-start.3
  68.0 0.9 copy-start.7
  68.8 0.7 copy-start.10
  69.5 15.1 %copy-start.1 = (bf16[640,768]{1,0:T(8,128)(2,1)S(1)}, bf16[640,768]{1,0:T(8,128)(2,1)}, u32[]{:S(2)}) copy-start(bf16[640,768]{1,0:T(8,128)(2,1)} %get-tuple-element.51.ones) | copy-start | bytes 2949124
  69.5 15.1 %copy-start.4 = (bf16[128,768]{1,0:T(8,128)(2,1)S(1)}, bf16[128,768]{1,0:T(8,128)(2,1)}, u32[]{:S(2)}) copy-start(bf16[128,768]{1,0:T(8,128)(2,1)} %get-tuple-element.58.tok) | copy-start | bytes 589828
  69.5 15.1 %copy-start.5 = (bf16[2,4,2,16,768]{4,3,2,1,0:T(8,128)(2,1)S(1)}, bf16[2,4,2,16,768]{4,3,2,1,0:T(8,128)(2,1)}, u32[]{:S(2)}) copy-start(bf16[2,4,2,16,768]{4,3,2,1,0:T(8,128)(2,1)} %get-tuple-element.55.f0) | copy-start | bytes 1179652
  69.5 15.1 %copy-start.6 = (bf16[2,4,2,16,768]{4,3,2,1,0:T(8,128)(2,1)S(1)}, bf16[2,4,2,16,768]{4,3,2,1,0:T(8,128)(2,1)}, u32[]{:S(2)}) copy-start(bf16[2,4,2,16,768]{4,3,2,1,0:T(8,128)(2,1)} %get-tuple-element.56.f1) | copy-start | bytes 1179652
  69.5 15.1 %copy-start.9 = (bf16[128,768]{1,0:T(8,128)(2,1)S(1)}, bf16[128,768]{1,0:T(8,128)(2,1)}, u32[]{:S(2)}) copy-start(bf16[128,768]{1,0:T(8,128)(2,1)} %get-tuple-element.57.cot) | copy-start | bytes 589828
  84.6 56.1 %copy-start.8 = (s32[24,768]{1,0:T(8,128)S(1)}, s32[24,768]{1,0:T(8,128)}, u32[]{:S(2)}) copy-start(s32[24,768]{1,0:T(8,128)} %get-tuple-element.52.spots) | copy-start | bytes 221188
  84.6 56.1 %copy-start.11 = (s32[2,2,256]{2,1,0:T(2,128)S(1)}, s32[2,2,256]{2,1,0:T(2,128)}, u32[]{:S(2)}) copy-start(s32[2,2,256]{2,1,0:T(2,128)} %get-tuple-element.49.ends.clip) | copy-start | bytes 12292
  161.9 56.9 %copy-start.12 = (f32[32,128]{1,0:T(8,128)S(1)}, f32[32,128]{1,0:T(8,128)}, u32[]{:S(2)}) copy-start(f32[32,128]{1,0:T(8,128)} %get-tuple-element.78.ends) | copy-start | bytes 49156

commit v7 on v6

--- a/solution.py
+++ b/solution.py
@@ -147,7 +147,8 @@
     (z, y, x, k, t), xs, ys, core, far, low, ring = neighbours()
     copy = Copies(send, recv)
     mine, other = k * 2 + t, k * 2 + 1 - t
-    greet(xs + ys + [core, far, low] + ring)
+    both = device(z, y, x, 1 - k, 1 - t)
+    greet(xs + ys + [core, far, both, low] + ring)
     own_far = copy(tok, tk.at[3, mine], far)
     order = (4, 5, 2, 3, 0, 1)
     pushes = {i: copy(tok, tk.at[3 - RING[i], mine], ring[i]) for i in order}
@@ -159,7 +160,7 @@
     for c in stages[0:9]:
         c.wait()
     small = build_small(gain, row, qv, fc, first, t, tile)
-    c_tile = copy(tile, tile_in, far)
+    c_tile = [copy(tile, tile_in.at[0], far), copy(tile, tile_in.at[1], both)]
     build_rows(attn_w, proj, up, down, small, first, pay_s)
     to_far = {}
 
@@ -172,15 +173,16 @@
         to_far[i] = copy(tk.at[slot, mine], tk.at[slot, mine], far)
         to_core(slot, mine)
 
-    c_tile.wait()
-    for q in range(2):
-        pay_s[q, :, 0:128] = pay_s[q, :, 0:128] + tile_in[...]
     swap = copy(pay_s.at[1 - k], ws.at[z, k], core)
     ws[z, k] = pay_s[k]
     for i in (4, 5):
         pushes[i].wait_recv()
         to_core(3 - RING[i], mine)
     swap.wait()
+    for c in c_tile:
+        c.wait()
+    ws[z, k, :, 0:128] = ws[z, k, :, 0:128] + tile_in[0]
+    ws[z, 1 - k, :, 0:128] = ws[z, 1 - k, :, 0:128] + tile_in[1]
     c_low = copy(ws.at[z], ws.at[z], low)
     pass_on(2)
     pass_on(3)
@@ -246,7 +248,7 @@
         + [
             pltpu.VMEM((2, 16, 2304), BF),
             pltpu.VMEM((16, 128), BF),
-            pltpu.VMEM((16, 128), BF),
+            pltpu.VMEM((2, 16, 128), BF),
             pltpu.VMEM((2, 2, 16, 2304), BF),
             DMA((50,)),
             DMA((50,)),
@@ -276,12 +278,16 @@
     return finish
 
 
+def spread_over_y(copy, g0, b0, y, ys):
+    return [copy(g0.at[:, (y + i + 1) % 4], b0.at[i], ys[i]) for i in range(3)]
+
+
+def spread_over_x(copy, g1, b1, x, xs):
+    return [copy(g1.at[:, :, (x + i + 1) % 4], b1.at[i], xs[i]) for i in range(3)]
+
+
 def spread_first(copy, g0, g1, b0, b1, x, y, xs, ys):
-    over_y, over_x = [], []
-    for i in range(3):
-        over_y.append(copy(g0.at[:, (y + i + 1) % 4], b0.at[i], ys[i]))
-        over_x.append(copy(g1.at[:, :, (x + i + 1) % 4], b1.at[i], xs[i]))
-    return over_y, over_x
+    return spread_over_y(copy, g0, b0, y, ys), spread_over_x(copy, g1, b1, x, xs)
 
 
 def add_first(g0, g1, b0, b1, s0, s1, x, y, over_y, over_x):
@@ -329,17 +335,27 @@
         u1[zz] = v1.astype(BF)
 
 
+HALVES = (slice(0, 64), slice(64, 128))
+
+
+def unit_rows(hidden):
+    centred = hidden - jnp.mean(hidden, axis=-1, keepdims=True)
+    scale = lax.rsqrt(jnp.mean(centred * centred, axis=-1, keepdims=True) + EPS)
+    return centred * scale, scale
+
+
 def mid_kernel(
     p, f0, f1, cot, tok, vecs, ones,
     output, e1, dr_full, sums, up_sum, s0, s1,
     got, mid, got_far, p0, p1, w_up, w_down, b_full, cot_full, dg, active, du_full,
-    pr, got_two, mid_two, far_two, dr, g0, g1, b0, b1, send, recv,
+    pr, got_two, mid_two, far_two, grad_one, g0, g1, b0, b1, send, recv,
 ):
     (z, y, x, k, t), xs, ys, core, far, low, ring = neighbours()
     copy = Copies(send, recv)
     greet(xs + ys + [core, far])
     mine, across, beside, both = k * 2 + t, k * 2 + 1 - t, 2 - 2 * k + t, 3 - 2 * k - t
     to_core = copy(p.at[pl.ds((1 - k) * 2, 2)], got, core)
+    finish_cot = exchange_rows(copy, cot, cot_full, k, t, core, far)
     made = []
     for i in range(2):
         for j in range(3):
@@ -348,19 +364,22 @@
         p0[i, y] = f0[i]
         p1[i, :, x] = f1[i]
     to_core.wait()
-    mid[...] = (p[across].astype(F32) + got[1 - t].astype(F32)).astype(BF)
-    to_far = copy(mid, got_far, far)
-    finish_cot = exchange_rows(copy, cot, cot_full, k, t, core, far)
-    part = p[mine].astype(F32) + got[t].astype(F32) + tok[...].astype(F32) + vecs[3:4, :]
-    to_far.wait()
-    hidden = part + got_far[...].astype(F32)
-    centred = hidden - jnp.mean(hidden, axis=-1, keepdims=True)
-    scale = lax.rsqrt(jnp.mean(centred * centred, axis=-1, keepdims=True) + EPS)
-    unit = centred * scale
-    b_full[mine] = (unit * vecs[1:2, :] + vecs[4:5, :]).astype(BF)
-    rows_far = copy(b_full.at[mine], b_full.at[mine], far)
-    rows_core = copy(b_full.at[mine], b_full.at[mine], core)
-    e1[...] = hidden
+    to_far, rows_far, rows_core = [], [], []
+    for rows in HALVES:
+        part = p[across, rows].astype(F32) + got[1 - t, rows].astype(F32)
+        mid[rows] = part.astype(BF)
+        to_far.append(copy(mid.at[rows], got_far.at[rows], far))
+    for i, rows in enumerate(HALVES):
+        part = p[mine, rows].astype(F32) + got[t, rows].astype(F32)
+        part = part + tok[rows].astype(F32) + vecs[3:4, :]
+        to_far[i].wait()
+        hidden = part + got_far[rows].astype(F32)
+        unit, _ = unit_rows(hidden)
+        b_full[mine, rows] = (unit * vecs[1:2, :] + vecs[4:5, :]).astype(BF)
+        here = b_full.at[mine, rows]
+        rows_far.append(copy(here, here, far))
+        rows_core.append(copy(here, here, core))
+        e1[rows] = hidden
     finish_cot()
     for c in made:
         c.wait()
@@ -388,59 +407,71 @@
         pr[1, i] = matmul_nt(du, w_up[...]).astype(BF)
 
     feed(mine)
-    rows_core.wait()
+    for c in rows_core:
+        c.wait()
     feed(beside)
     first = copy(pr.at[:, beside], got_two.at[:, t], core)
-    rows_far.wait()
-    rows_pass = copy(b_full.at[across], b_full.at[across], core)
+    rows_pass = []
+    for i, rows in enumerate(HALVES):
+        rows_far[i].wait()
+        rows_pass.append(copy(b_full.at[across, rows], b_full.at[across, rows], core))
     feed(across)
-    rows_pass.wait()
+    for c in rows_pass:
+        c.wait()
     feed(both)
     second = copy(pr.at[:, both], got_two.at[:, 1 - t], core)
     second.wait()
     for i in range(2):
         v = pr[i, across].astype(F32) + got_two[i, 1 - t].astype(F32)
         mid_two[i] = v.astype(BF)
-    two = {1: copy(mid_two.at[1], far_two.at[1], far)}
+    back_far = [copy(mid_two.at[1, rows], far_two.at[1, rows], far) for rows in HALVES]
+    c_rows, a_rows = cot_full[...].reshape(512, 768), active[...].reshape(512, 768)
+    for i in range(2):
+        cols = slice(i * 384, i * 384 + 384)
+        g = matmul_tn(c_rows[:, cols], a_rows).astype(BF)
+        g1[i] = matmul_tn(ones[SELECT], g).astype(BF).reshape(4, 4, 2, 16, 768)
+    over_x = spread_over_x(copy, g1, b1, x, xs)
     b_rows, du_rows = b_full[...].reshape(512, 768), du_full[...].reshape(512, 768)
     for i in range(2):
         cols = slice(i * 384, i * 384 + 384)
         g = matmul_tn(b_rows[:, cols], du_rows).astype(BF)
         g0[i] = matmul_tn(ones[SELECT], g).astype(BF).reshape(4, 4, 2, 16, 768)
-    c_rows, a_rows = cot_full[...].reshape(512, 768), active[...].reshape(512, 768)
-    for i in range(2):
-        cols = slice(i * 384, i * 384 + 384)
-        g = matmul_tn(c_rows[:, cols], a_rows).astype(BF)
-        g1[i] = matmul_tn(ones[SELECT], g).astype(BF).reshape(4, 4, 2, 16, 768)
-    over = spread_first(copy, g0, g1, b0, b1, x, y, xs, ys)
+    over = spread_over_y(copy, g0, b0, y, ys), over_x
     first.wait()
 
-    def summed(i):
-        v = pr[i, mine].astype(F32) + got_two[i, t].astype(F32)
-        two[i].wait()
-        return v + far_two[i].astype(F32)
-
-    back_rows = summed(1)
-    hidden = e1[...]
-    centred = hidden - jnp.mean(hidden, axis=-1, keepdims=True)
-    scale = lax.rsqrt(jnp.mean(centred * centred, axis=-1, keepdims=True) + EPS)
-    unit = centred * scale
-    w = back_rows * vecs[1:2, :]
-    mean_w = jnp.mean(w, axis=-1, keepdims=True)
-    mean_wu = jnp.mean(w * unit, axis=-1, keepdims=True)
-    cot_f = cot[...].astype(F32)
-    grad = cot_f + scale * (w - mean_w - unit * mean_wu)
-    e1[...] = grad
-    low_grad = grad.astype(BF)
-    dr[...] = low_grad
-    finish_rows = exchange_rows(copy, dr, dr_full, k, t, core, far)
-    two[0] = copy(mid_two.at[0], far_two.at[0], far)
-    sums[0:1, :] = jnp.sum(back_rows * unit, axis=0, keepdims=True)
-    sums[1:2, :] = jnp.sum(low_grad.astype(F32), axis=0, keepdims=True)
-    sums[2:3, :] = jnp.sum(back_rows, axis=0, keepdims=True)
-    sums[3:4, :] = jnp.sum(cot_f, axis=0, keepdims=True)
-    finish_rows()
-    output[...] = (hidden + summed(0) + vecs[5:6, :]).astype(BF)
+    sums[...] = jnp.zeros((4, 768), F32)
+    dr_far, dr_core = [], []
+    for i, rows in enumerate(HALVES):
+        back_rows = pr[1, mine, rows].astype(F32) + got_two[1, t, rows].astype(F32)
+        back_far[i].wait()
+        back_rows = back_rows + far_two[1, rows].astype(F32)
+        unit, scale = unit_rows(e1[rows])
+        w = back_rows * vecs[1:2, :]
+        mean_w = jnp.mean(w, axis=-1, keepdims=True)
+        mean_wu = jnp.mean(w * unit, axis=-1, keepdims=True)
+        cot_f = cot[rows].astype(F32)
+        grad = cot_f + scale * (w - mean_w - unit * mean_wu)
+        low_grad = grad.astype(BF)
+        dr_full[mine, rows] = low_grad
+        here = dr_full.at[mine, rows]
+        dr_far.append(copy(here, here, far))
+        dr_core.append(copy(here, here, core))
+        grad_one[rows] = grad
+        sums[0:1, :] += jnp.sum(back_rows * unit, axis=0, keepdims=True)
+        sums[1:2, :] += jnp.sum(low_grad.astype(F32), axis=0, keepdims=True)
+        sums[2:3, :] += jnp.sum(back_rows, axis=0, keepdims=True)
+        sums[3:4, :] += jnp.sum(cot_f, axis=0, keepdims=True)
+    out_far = copy(mid_two.at[0], far_two.at[0], far)
+    dr_pass = []
+    for i, rows in enumerate(HALVES):
+        dr_far[i].wait()
+        dr_pass.append(copy(dr_full.at[across, rows], dr_full.at[across, rows], core))
+    part = e1[...] + pr[0, mine].astype(F32) + got_two[0, t].astype(F32) + vecs[5:6, :]
+    e1[...] = grad_one[...]
+    out_far.wait()
+    output[...] = (part + far_two[0].astype(F32)).astype(BF)
+    for c in dr_core + dr_pass:
+        c.wait()
     add_first(g0, g1, b0, b1, s0, s1, x, y, *over)
 
 
@@ -463,10 +494,11 @@
         ],
         [two, rows, rows, piece, piece, square, square, four, four]
         + [pltpu.VMEM((4, 128, 768), F32), four, four]
-        + [pltpu.VMEM((2, 4, 128, 768), BF), pltpu.VMEM((2, 2, 128, 768), BF), two, two, rows]
+        + [pltpu.VMEM((2, 4, 128, 768), BF), pltpu.VMEM((2, 2, 128, 768), BF), two, two]
+        + [pltpu.VMEM((128, 768), F32)]
         + [piece, piece]
         + [pltpu.VMEM((3, 2, 4, 2, 16, 768), BF)] * 2
-        + [DMA((33,)), DMA((33,))],
+        + [DMA((41,)), DMA((41,))],
         1,
         "mid",
         (p, f0, f1, cot, tok, vecs, ones),
@@ -477,11 +509,12 @@
 def return_kernel(
     d, g, fs0, fs1, out, own, tile_out,
     got_core, v1, in1, e_send, got_far, r_send, got_ring,
-    b0, b1, s0, s1, a0, a1, fa0, fa1, u0, u1, v_0, v_1, z_in0, z_in1, z_in2, z_in3, res, tile, send, recv,
+    b0, b1, s0, s1, a0, a1, fa0, fa1, u0, u1, v_0, v_1, z_in0, z_in1, z_in2, z_in3, res, send, recv,
 ):
     (z, y, x, k, t), xs, ys, core, far, low, ring = neighbours()
     copy = Copies(send, recv)
-    greet(xs + ys + [core, far, low] + ring)
+    both = device(z, y, x, 1 - k, 1 - t)
+    greet(xs + ys + [core, far, both, low] + ring)
     mine, across = k * 2 + t, k * 2 + 1 - t
     near = (ring[4], ring[5])
     order = (4, 2, 5, 1, 6, 0, 3)
@@ -533,18 +566,21 @@
     res[:, :, H0] = v_0[z].astype(F32) + z_in2[...].astype(F32)
     res[:, :, H1] = v_1[z].astype(F32) + z_in3[...].astype(F32)
     swap = copy(res.at[1 - k], own.at[k], core)
+    tiles = [
+        copy(res.at[k, :, pl.ds(0, 128)], tile_out.at[0], far),
+        copy(res.at[1 - k, :, pl.ds(0, 128)], tile_out.at[1], both),
+    ]
     own[k] = res[k]
     total = d[3, mine].astype(F32) + got_core[3, t].astype(F32)
     total = total + in1[0, t].astype(F32) + in1[1, t].astype(F32)
-    swap.wait()
-    tile[...] = own[0, :, 0:128] + own[1, :, 0:128]
-    c_tile = copy(tile, tile_out, far)
     for i in range(4):
         home[i].wait()
         total = total + got_ring[i].astype(F32)
     last.wait()
     out[...] = total + got_far[4].astype(F32)
-    c_tile.wait()
+    swap.wait()
+    for c in tiles:
+        c.wait()
 
 
 def return_all(d, g, s0, s1):
@@ -555,7 +591,7 @@
         [
             jax.ShapeDtypeStruct((128, 768), F32),
             jax.ShapeDtypeStruct((2, 16, 2304), F32),
-            jax.ShapeDtypeStruct((16, 128), F32),
+            jax.ShapeDtypeStruct((2, 16, 128), F32),
         ],
         [pltpu.VMEM((7, 2, 128, 768), BF), two, two]
         + [pltpu.VMEM((5, 128, 768), BF)] * 2
@@ -566,7 +602,7 @@
         + [pltpu.VMEM((3, 2, 2, 16, 768), BF)] * 2
         + [pltpu.VMEM((2, 2, 16, n), BF) for n in (768, 768, wide, slim)]
         + [pltpu.VMEM((2, 16, n), BF) for n in (768, 768, wide, slim)]
-        + [pltpu.VMEM((2, 16, 2304), F32), pltpu.VMEM((16, 128), F32), DMA((42,)), DMA((42,))],
+        + [pltpu.VMEM((2, 16, 2304), F32), DMA((43,)), DMA((43,))],
         5,
         "return_all",
         (d, g, s0, s1),
@@ -658,8 +694,17 @@
 
 def front_kernel(
     ends, clip, w, ones, spots, tk,
-    vecs, w_attn, unit, kv, q, of, lse, attn,
+    vecs, w_attn, unit, kv, q, of, lse, attn, held, sems,
 ):
+    bounds = [key_blocks(ends, qb) for qb in range(2)]
+
+    def fetch(j):
+        return pltpu.make_async_copy(tk.at[j], held.at[j], sems.at[j])
+
+    @pl.loop(bounds[0][0], bounds[1][1])
+    def _(j):
+        fetch(j).start()
+
     line = lax.broadcasted_iota(jnp.int32, (128, 768), 0)
     k = lax.axis_index("dp") % 2
     row12, row13 = [
@@ -680,16 +725,15 @@
         w_attn[z * 384 : z * 384 + 384, :] = matmul(ones[SELECT], w[z]).astype(BF)
 
     def norm_rows(j):
-        v = tk[j].astype(F32)
+        v = held[j].astype(F32)
         centred = v - jnp.mean(v, axis=-1, keepdims=True)
         spread_out = jnp.mean(centred * centred, axis=-1, keepdims=True)
         u = centred * lax.rsqrt(spread_out + EPS)
         return u, (u * vecs[0:1, :] + vecs[2:3, :]).astype(BF)
 
-    bounds = [key_blocks(ends, qb) for qb in range(2)]
-
     @pl.loop(bounds[0][0], bounds[1][1])
     def _(j):
+        fetch(j).wait()
         u, a = norm_rows(j)
         unit[j] = u.astype(BF)
         kv[j] = (matmul(a, w_attn[:, 0:384]) + vecs[6:7, 0:384]).astype(BF)
@@ -754,9 +798,10 @@
             jax.ShapeDtypeStruct((3, 512), F32),
             jax.ShapeDtypeStruct((512, 768), BF),
         ],
-        in_specs=[SM] + [VM] * 5,
+        in_specs=[SM] + [VM] * 4 + [pl.BlockSpec(memory_space=pl.ANY)],
         out_specs=[VM] * 8,
-        compiler_params=pltpu.CompilerParams(vmem_limit_bytes=16 * 2**20),
+        scratch_shapes=[pltpu.VMEM((7, 512, 768), BF), DMA((7,))],
+        compiler_params=pltpu.CompilerParams(vmem_limit_bytes=38 * 2**20),
         name="front",
     )(*args)
 
@@ -905,7 +950,7 @@
         g_up[:, 0, cols] = own[q, 0:12, 768:1536]
         g_down[:, 0, cols] = own[q, 0:12, 1536:2304]
     row0, row1 = own[0, 12:13, 0:128], own[1, 12:13, 0:128]
-    vec = row0 + row1 + far[12:13, :]
+    vec = row0 + row1 + far[0, 12:13, :] + far[1, 12:13, :]
     lane = lax.broadcasted_iota(jnp.int32, (8, 128), 1)
     line = lax.broadcasted_iota(jnp.int32, (8, 128), 0)
 

time: 222 us -> 222 us (level)
  local copies, waits for them, and re-layouts: 8.78 us -> 6.22 us
    unnamed x31 -> x29, local copies, waits for them, and re-layouts: 8.78 us -> 6.22 us
where the time goes in v7:
time: 222 us; the launch traced here: 221 us
  Pallas kernels  214 us (96%)
  local copies, waits for them, and re-layouts  6.22 us (3%)
    pallas_call x3, Pallas kernels, comm_call(): pl.pallas_call(kernel, out_shape=out_shape, in_specs=[place] * len(args),...  176 us
    pallas_call x1, Pallas kernels, back(): pl.pallas_call(back_kernel, out_shape=[jax.ShapeDtypeStruct((7, 512, 768)...  21.3 us
    pallas_call x1, Pallas kernels, front(): pl.pallas_call(front_kernel, out_shape=[jax.ShapeDtypeStruct((8, 768), F3...  15 us
    unnamed x29, local copies, waits for them, and re-layouts  6.22 us

profile of v7, /device:TPU:1, one launch (start us, length us, event | category | flops | bytes accessed | tf_op | source)
XLA Modules:
  0.0 220.9 jit_solution(4020122753244344720)
XLA Ops:
  0.6 61.1 %gather_first.1 = (bf16[2,4,4,2,16,768]{5,4,3,2,1,0:T(8,128)(2,1)}, bf16[2,4,2,16,768]{4,3,2,1,0:T(8,128)(2,1)}, bf16[2,4,2,16,768]{4,3,2,1,0:T(8,128)(2,1)}, s3...) custom-call(s32[2,256]{1,0:T(2,128)} %clip.1, ...), custom_call_target="tpu_custom_call" | custom-call | tf_op jit(solution)/shard_map/gather_first/pallas_call | solution.py:51
  61.8 0.0 copy-start
  61.8 1.2 copy-done
  63.0 0.0 copy-start.2
  63.0 1.4 copy-done.2
  64.4 0.0 copy-start.6
  64.4 0.9 copy-done.6
  65.2 0.0 copy-start.9
  65.2 0.7 copy-done.9
  65.9 0.0 copy-start.3
  65.9 0.0 copy-start.4
  65.9 0.0 copy-start.5
  65.9 0.0 copy-start.8
  65.9 15.0 %front.1 = (f32[8,768]{1,0:T(8,128)S(1)}, bf16[768,768]{1,0:T(8,128)(2,1)S(1)}, bf16[7,512,768]{2,1,0:T(8,128)(2,1)S(1)}, bf16[7,512,384]{2,1,0:T(8,128)(2,1)S(1...) custom-call(s32[2,2,256]{2,1,0:T(2,128)S(1)} %copy-done.9, ...), custom_call_target="tpu_custom_call" | custom-call | tf_op jit(solution)/shard_map/front/pallas_call | solution.py:789
  81.0 0.0 copy-start.1
  81.0 0.0 copy-start.7
  81.0 0.0 copy-start.10
  81.0 0.0 copy-done.3
  81.0 0.0 copy-done.4
  81.0 0.0 copy-done.5
  81.0 0.0 copy-done.8
  81.0 56.5 %mid.1 = (bf16[128,768]{1,0:T(8,128)(2,1)S(1)}, f32[128,768]{1,0:T(8,128)S(1)}, bf16[4,128,768]{2,1,0:T(8,128)(2,1)S(1)}, f32[4,768]{1,0:T(4,128)S(1)}, f32[1,76...) custom-call(bf16[4,128,768]{2,1,0:T(8,128)(2,1)S(1)} %bitcast.48, ...), custom_call_target="tpu_custom_call" | custom-call | tf_op jit(solution)/shard_map/mid/pallas_call | solution.py:51
  137.5 0.0 copy-done.1
  137.5 0.0 copy-done.7
  137.5 0.0 copy-done.10
  137.6 21.3 %back.1 = (bf16[7,512,768]{2,1,0:T(8,128)(2,1)S(1)}, bf16[2,512,768]{2,1,0:T(8,128)(2,1)S(1)}) custom-call(s32[2,2,256]{2,1,0:T(2,128)S(1)} %copy-done.10, s32[2,2,256]{2,1,0:T(2,128)S(1)} %copy-done.10, bf16[512,384]{1,0:T(8,128)(2,1)S(1)} %get-tuple-element.61.q, bf16[512,768]{1,0:T(8,128)(2,1)S(1)} %bitcast.47, f32[512,384]{1,0:T(8,128)S(1)} %get-tuple-element.63.of, ...), custom_call_target="tpu_custom_call" | custom-call | tf_op jit(solution)/shard_map/back/pallas_call | solution.py:899
  158.9 0.0 copy-start.11
  158.9 58.9 %return_all.1 = (f32[128,768]{1,0:T(8,128)S(1)}, f32[2,16,2304]{2,1,0:T(8,128)S(1)}, f32[2,16,128]{2,1,0:T(8,128)S(1)}) custom-call(bf16[7,4,128,768]{3,2,1,0:T(8,128)(2,1)S(1)} %bitcast.44, bf16[2,4,4,2,16,768]{5,4,3,2,1,0:T(8,128)(2,1)S(1)} %bitcast.46, bf16[2,4,2,16,768]{4,3,2,1,0:T(8,128)(2,1)S(1)} %get-tuple-element.72.fs0, ...), custom_call_target="tpu_custom_call" | custom-call | tf_op jit(solution)/shard_map/return_all/pallas_call | solution.py:51
  217.7 0.0 copy-done.11
  217.7 1.1 finish.1
  218.9 0.6 copy.26
  219.5 0.7 copy.27
  220.2 0.7 copy.35
  (2 shorter events, 0.0 us)
Async XLA Ops:
  61.8 1.2 copy-start
  63.0 1.4 copy-start.2
  64.4 0.9 copy-start.6
  65.2 0.7 copy-start.9
  65.9 15.1 %copy-start.3 = (bf16[128,768]{1,0:T(8,128)(2,1)S(1)}, bf16[128,768]{1,0:T(8,128)(2,1)}, u32[]{:S(2)}) copy-start(bf16[128,768]{1,0:T(8,128)(2,1)} %get-tuple-element.58.tok) | copy-start | bytes 589828
  65.9 15.1 %copy-start.4 = (bf16[2,4,2,16,768]{4,3,2,1,0:T(8,128)(2,1)S(1)}, bf16[2,4,2,16,768]{4,3,2,1,0:T(8,128)(2,1)}, u32[]{:S(2)}) copy-start(bf16[2,4,2,16,768]{4,3,2,1,0:T(8,128)(2,1)} %get-tuple-element.55.f0) | copy-start | bytes 1179652
  65.9 15.1 %copy-start.5 = (bf16[2,4,2,16,768]{4,3,2,1,0:T(8,128)(2,1)S(1)}, bf16[2,4,2,16,768]{4,3,2,1,0:T(8,128)(2,1)}, u32[]{:S(2)}) copy-start(bf16[2,4,2,16,768]{4,3,2,1,0:T(8,128)(2,1)} %get-tuple-element.56.f1) | copy-start | bytes 1179652
  65.9 15.1 %copy-start.8 = (bf16[128,768]{1,0:T(8,128)(2,1)S(1)}, bf16[128,768]{1,0:T(8,128)(2,1)}, u32[]{:S(2)}) copy-start(bf16[128,768]{1,0:T(8,128)(2,1)} %get-tuple-element.57.cot) | copy-start | bytes 589828
  81.0 56.6 %copy-start.1 = (bf16[640,768]{1,0:T(8,128)(2,1)S(1)}, bf16[640,768]{1,0:T(8,128)(2,1)}, u32[]{:S(2)}) copy-start(bf16[640,768]{1,0:T(8,128)(2,1)} %get-tuple-element.51.ones) | copy-start | bytes 2949124
  81.0 56.6 %copy-start.7 = (s32[24,768]{1,0:T(8,128)S(1)}, s32[24,768]{1,0:T(8,128)}, u32[]{:S(2)}) copy-start(s32[24,768]{1,0:T(8,128)} %get-tuple-element.52.spots) | copy-start | bytes 221188
  81.0 56.6 %copy-start.10 = (s32[2,2,256]{2,1,0:T(2,128)S(1)}, s32[2,2,256]{2,1,0:T(2,128)}, u32[]{:S(2)}) copy-start(s32[2,2,256]{2,1,0:T(2,128)} %get-tuple-element.49.ends.clip) | copy-start | bytes 12292
  158.9 58.9 %copy-start.11 = (f32[32,128]{1,0:T(8,128)S(1)}, f32[32,128]{1,0:T(8,128)}, u32[]{:S(2)}) copy-start(f32[32,128]{1,0:T(8,128)} %get-tuple-element.78.ends) | copy-start | bytes 49156

commit v8 on v7

--- a/solution.py
+++ b/solution.py
@@ -46,13 +46,13 @@
     )
 
 
-def comm_call(kernel, out_shape, scratch, cid, name, args, room, place=VM):
+def comm_call(kernel, out_shape, scratch, cid, name, args, room, place=VM, outs=None):
     single = not isinstance(out_shape, (list, tuple))
     return pl.pallas_call(
         kernel,
         out_shape=out_shape,
         in_specs=[place] * len(args),
-        out_specs=VM if single else [VM] * len(out_shape),
+        out_specs=VM if single else outs or [VM] * len(out_shape),
         scratch_shapes=scratch,
         compiler_params=pltpu.CompilerParams(
             collective_id=cid, has_side_effects=True, vmem_limit_bytes=room * 2**20
@@ -259,6 +259,7 @@
         args,
         54,
         pl.BlockSpec(memory_space=pltpu.MemorySpace.HBM),
+        [VM] * 4 + [pl.BlockSpec(memory_space=pltpu.MemorySpace.HBM)] + [VM] * 5,
     )
 
 

time: 222 us -> 217 us (0.977)
  Pallas kernels: 214 us -> 211 us
    pallas_call x3, Pallas kernels: 176 us -> 173 us  [comm_call(): pl.pallas_call(kernel, out_shape=out_shape, in_specs=[place] * len(args),...]
where the time goes in v8:
time: 217 us; the launch traced here: 218 us
  Pallas kernels  211 us (97%)
  local copies, waits for them, and re-layouts  6.22 us (3%)
    pallas_call x3, Pallas kernels, comm_call(): pl.pallas_call(kernel, out_shape=out_shape, in_specs=[place] * len(args),...  173 us
    pallas_call x1, Pallas kernels, back(): pl.pallas_call(back_kernel, out_shape=[jax.ShapeDtypeStruct((7, 512, 768)...  21.3 us
    pallas_call x1, Pallas kernels, front(): pl.pallas_call(front_kernel, out_shape=[jax.ShapeDtypeStruct((8, 768), F3...  15 us
    unnamed x29, local copies, waits for them, and re-layouts  6.22 us

profile of v8, /device:TPU:1, one launch (start us, length us, event | category | flops | bytes accessed | tf_op | source)
XLA Modules:
  0.0 217.8 jit_solution(15334293536068751570)
XLA Ops:
  0.6 59.9 %gather_first.1 = (bf16[2,4,4,2,16,768]{5,4,3,2,1,0:T(8,128)(2,1)}, bf16[2,4,2,16,768]{4,3,2,1,0:T(8,128)(2,1)}, bf16[2,4,2,16,768]{4,3,2,1,0:T(8,128)(2,1)}, s3...) custom-call(s32[2,256]{1,0:T(2,128)} %clip.1, ...), custom_call_target="tpu_custom_call" | custom-call | tf_op jit(solution)/shard_map/gather_first/pallas_call | solution.py:51
  60.5 0.0 copy-start
  60.5 1.2 copy-done
  61.7 0.0 copy-start.2
  61.7 1.4 copy-done.2
  63.1 0.0 copy-start.6
  63.1 0.9 copy-done.6
  64.0 0.0 copy-start.9
  64.0 0.7 copy-done.9
  64.7 0.0 copy-start.3
  64.7 0.0 copy-start.4
  64.7 0.0 copy-start.5
  64.7 0.0 copy-start.8
  64.7 15.0 %front.1 = (f32[8,768]{1,0:T(8,128)S(1)}, bf16[768,768]{1,0:T(8,128)(2,1)S(1)}, bf16[7,512,768]{2,1,0:T(8,128)(2,1)S(1)}, bf16[7,512,384]{2,1,0:T(8,128)(2,1)S(1...) custom-call(s32[2,2,256]{2,1,0:T(2,128)S(1)} %copy-done.9, ...), custom_call_target="tpu_custom_call" | custom-call | tf_op jit(solution)/shard_map/front/pallas_call | solution.py:790
  79.7 0.0 copy-start.1
  79.8 0.0 copy-start.7
  79.8 0.0 copy-start.10
  79.8 0.0 copy-done.3
  79.8 0.0 copy-done.4
  79.8 0.0 copy-done.5
  79.8 0.0 copy-done.8
  79.8 56.5 %mid.1 = (bf16[128,768]{1,0:T(8,128)(2,1)S(1)}, f32[128,768]{1,0:T(8,128)S(1)}, bf16[4,128,768]{2,1,0:T(8,128)(2,1)S(1)}, f32[4,768]{1,0:T(4,128)S(1)}, f32[1,76...) custom-call(bf16[4,128,768]{2,1,0:T(8,128)(2,1)S(1)} %bitcast.48, ...), custom_call_target="tpu_custom_call" | custom-call | tf_op jit(solution)/shard_map/mid/pallas_call | solution.py:51
  136.3 0.0 copy-done.1
  136.3 0.0 copy-done.7
  136.3 0.0 copy-done.10
  136.3 21.3 %back.1 = (bf16[7,512,768]{2,1,0:T(8,128)(2,1)S(1)}, bf16[2,512,768]{2,1,0:T(8,128)(2,1)S(1)}) custom-call(s32[2,2,256]{2,1,0:T(2,128)S(1)} %copy-done.10, s32[2,2,256]{2,1,0:T(2,128)S(1)} %copy-done.10, bf16[512,384]{1,0:T(8,128)(2,1)S(1)} %get-tuple-element.61.q, bf16[512,768]{1,0:T(8,128)(2,1)S(1)} %bitcast.47, f32[512,384]{1,0:T(8,128)S(1)} %get-tuple-element.63.of, ...), custom_call_target="tpu_custom_call" | custom-call | tf_op jit(solution)/shard_map/back/pallas_call | solution.py:900
  157.6 0.0 copy-start.11
  157.6 56.9 %return_all.1 = (f32[128,768]{1,0:T(8,128)S(1)}, f32[2,16,2304]{2,1,0:T(8,128)S(1)}, f32[2,16,128]{2,1,0:T(8,128)S(1)}) custom-call(bf16[7,4,128,768]{3,2,1,0:T(8,128)(2,1)S(1)} %bitcast.44, bf16[2,4,4,2,16,768]{5,4,3,2,1,0:T(8,128)(2,1)S(1)} %bitcast.46, bf16[2,4,2,16,768]{4,3,2,1,0:T(8,128)(2,1)S(1)} %get-tuple-element.72.fs0, ...), custom_call_target="tpu_custom_call" | custom-call | tf_op jit(solution)/shard_map/return_all/pallas_call | solution.py:51
  214.6 0.0 copy-done.11
  214.6 1.1 finish.1
  215.7 0.6 copy.26
  216.4 0.7 copy.27
  217.1 0.7 copy.35
  (2 shorter events, 0.0 us)
Async XLA Ops:
  60.5 1.2 copy-start
  61.7 1.4 copy-start.2
  63.1 0.9 copy-start.6
  64.0 0.7 copy-start.9
  64.7 15.1 %copy-start.3 = (bf16[128,768]{1,0:T(8,128)(2,1)S(1)}, bf16[128,768]{1,0:T(8,128)(2,1)}, u32[]{:S(2)}) copy-start(bf16[128,768]{1,0:T(8,128)(2,1)} %get-tuple-element.58.tok) | copy-start | bytes 589828
  64.7 15.1 %copy-start.4 = (bf16[2,4,2,16,768]{4,3,2,1,0:T(8,128)(2,1)S(1)}, bf16[2,4,2,16,768]{4,3,2,1,0:T(8,128)(2,1)}, u32[]{:S(2)}) copy-start(bf16[2,4,2,16,768]{4,3,2,1,0:T(8,128)(2,1)} %get-tuple-element.55.f0) | copy-start | bytes 1179652
  64.7 15.1 %copy-start.5 = (bf16[2,4,2,16,768]{4,3,2,1,0:T(8,128)(2,1)S(1)}, bf16[2,4,2,16,768]{4,3,2,1,0:T(8,128)(2,1)}, u32[]{:S(2)}) copy-start(bf16[2,4,2,16,768]{4,3,2,1,0:T(8,128)(2,1)} %get-tuple-element.56.f1) | copy-start | bytes 1179652
  64.7 15.1 %copy-start.8 = (bf16[128,768]{1,0:T(8,128)(2,1)S(1)}, bf16[128,768]{1,0:T(8,128)(2,1)}, u32[]{:S(2)}) copy-start(bf16[128,768]{1,0:T(8,128)(2,1)} %get-tuple-element.57.cot) | copy-start | bytes 589828
  79.7 56.6 %copy-start.1 = (bf16[640,768]{1,0:T(8,128)(2,1)S(1)}, bf16[640,768]{1,0:T(8,128)(2,1)}, u32[]{:S(2)}) copy-start(bf16[640,768]{1,0:T(8,128)(2,1)} %get-tuple-element.51.ones) | copy-start | bytes 2949124
  79.8 56.6 %copy-start.7 = (s32[24,768]{1,0:T(8,128)S(1)}, s32[24,768]{1,0:T(8,128)}, u32[]{:S(2)}) copy-start(s32[24,768]{1,0:T(8,128)} %get-tuple-element.52.spots) | copy-start | bytes 221188
  79.8 56.6 %copy-start.10 = (s32[2,2,256]{2,1,0:T(2,128)S(1)}, s32[2,2,256]{2,1,0:T(2,128)}, u32[]{:S(2)}) copy-start(s32[2,2,256]{2,1,0:T(2,128)} %get-tuple-element.49.ends.clip) | copy-start | bytes 12292
  157.6 56.9 %copy-start.11 = (f32[32,128]{1,0:T(8,128)S(1)}, f32[32,128]{1,0:T(8,128)}, u32[]{:S(2)}) copy-start(f32[32,128]{1,0:T(8,128)} %get-tuple-element.78.ends) | copy-start | bytes 49156
